TPU v7x, 32 devices: a whole 2x2x4 slice. The times are simulated.
32 devices in a mesh: groups: 2 (over y), sink: 16 (over z, x, core).
Axes of the slice: x: 2, y: 2, z: 4, core: 2. Of those that a mesh axis runs over, the one named last changes fastest.
Arguments:
- eigvecs: bfloat16 [16, 2, 3, 192, 8192], P('groups', None, None, None, 'sink'), parts along dimension 0
- momentum: int32 [6], P('groups'), parts along dimension 0, may hold values from -5 to 5, as said below
- peram: bfloat16 [32, 2, 768, 768], P(('groups', 'sink')), parts along dimension 0, may hold values from -0.009338379 to 0.009338379
- times: int32 [32, 2], P(('groups', 'sink')), parts along dimension 0, may hold values from 0 to 7, as said below
Outputs:
- blocks: bfloat16 [32, 2, 768, 768], P(('groups', 'sink')), parts along dimension 0
There are 2 independent parts, one for each index of `groups`. A program takes and returns all parts, laid end to end along the dimension named above; each array names one. Nothing has to cross between parts.
Inputs may be any that keep to these rules, and one draw needn't show every extreme that they name: `momentum`: the three components are distinct; one is -5 and one is 5. In each of the two columns every timeslice appears exactly 16 // 8 times.
All inputs are finite; a program needn't handle non-finite values.
Results may differ from a plain program's by a relative error of at most 0.0075.
Values may be sent and summed in bfloat16 or wider, within the bound.
No kernel may reach another device: no remote copies, remote signals or barrier semaphores. Data moves between devices by JAX's collectives and lax.ppermute only.
A program may use at most 64 MiB of HBM per device.

v0:
```python
import math

import jax
import jax.numpy as jnp
from jax import lax
from jax.sharding import PartitionSpec as P


def angles(momentum, sites, devices, device):
    local = jnp.arange(sites, dtype=jnp.int32)
    second = local // 16
    third = local % 16
    extent = sites // 16
    frac = jnp.mod(momentum[0] * device, devices).astype(jnp.float32) / devices
    frac = frac + jnp.mod(momentum[1] * second, extent).astype(jnp.float32) / extent
    frac = frac + jnp.mod(momentum[2] * third, 16).astype(jnp.float32) / 16.0
    return 2.0 * math.pi * frac


def pair_block(block, sink_el, src_el, signs):
    width = sink_el.shape[0]
    a_re = sink_el[:, :width]
    a_im = sink_el[:, width:]
    left_mat = jnp.concatenate(
        [jnp.concatenate([a_re, -a_im], axis=1), jnp.concatenate([a_im, a_re], axis=1)], axis=0
    )
    t_re = jnp.roll(block[0].reshape(4, width, 4 * width), 2, axis=0) * signs[:, None, None]
    t_im = jnp.roll(block[1].reshape(4, width, 4 * width), 2, axis=0) * signs[:, None, None]
    right_mat = jnp.concatenate([t_re, t_im], axis=1)
    stacked = jnp.einsum("kl,alc->akc", left_mat, right_mat, preferred_element_type=jnp.float32)
    x_re = stacked[:, :width].reshape(4 * width, 4 * width).astype(jnp.bfloat16)
    x_im = stacked[:, width:].reshape(4 * width, 4 * width).astype(jnp.bfloat16)
    y_both = jnp.concatenate(
        [
            jnp.roll(x_re.reshape(4 * width, 4, width), 2, axis=1),
            jnp.roll(x_im.reshape(4 * width, 4, width), 2, axis=1),
        ],
        axis=-1,
    )
    e_re = src_el[:, :width]
    e_im = src_el[:, width:]
    q_mat = jnp.concatenate(
        [jnp.concatenate([e_re, e_im], axis=1), jnp.concatenate([-e_im, e_re], axis=1)], axis=0
    )
    result = jnp.einsum("rbl,nl->rbn", y_both, q_mat, preferred_element_type=jnp.float32)
    m_re = result[..., :width].reshape(4 * width, 4 * width)
    m_im = result[..., width:].reshape(4 * width, 4 * width)
    return jnp.stack([m_re, m_im]).astype(jnp.bfloat16)


def shards(eigvecs, momentum, peram, times):
    devices = lax.axis_size("sink")
    device = lax.axis_index("sink")
    slices, _, _, width, sites = eigvecs.shape
    theta = angles(momentum, sites, devices, device)
    cosine = jnp.cos(theta)
    sine = jnp.sin(theta)
    vec_re = eigvecs[:, 0]
    vec_im = eigvecs[:, 1]
    rot_re = (cosine * vec_re.astype(jnp.float32) + sine * vec_im.astype(jnp.float32)).astype(
        jnp.bfloat16
    )
    rot_im = (cosine * vec_im.astype(jnp.float32) - sine * vec_re.astype(jnp.float32)).astype(
        jnp.bfloat16
    )
    form = "tckx,tclx->tkl"
    real = jnp.einsum(form, vec_re, rot_re, preferred_element_type=jnp.float32) + jnp.einsum(
        form, vec_im, rot_im, preferred_element_type=jnp.float32
    )
    imag = jnp.einsum(form, vec_re, rot_im, preferred_element_type=jnp.float32) - jnp.einsum(
        form, vec_im, rot_re, preferred_element_type=jnp.float32
    )
    partial_sums = jnp.concatenate([real, imag], axis=-1)
    totals = lax.psum(partial_sums, "sink")
    elemental = totals.astype(jnp.bfloat16)
    signs = jnp.array([1.0, 1.0, -1.0, -1.0], jnp.bfloat16)
    sink_el = lax.dynamic_index_in_dim(elemental, times[0, 0], 0, keepdims=False)
    src_el = lax.dynamic_index_in_dim(elemental, times[0, 1], 0, keepdims=False)
    outputs = [pair_block(peram[0], sink_el, src_el, signs)]
    return jnp.stack(outputs)


def solution(mesh):
    in_specs = (
        P("groups", None, None, None, "sink"),
        P("groups"),
        P(("groups", "sink"), None, None, None),
        P(("groups", "sink"), None),
    )
    out_specs = P(("groups", "sink"), None, None, None)
    return jax.shard_map(shards, mesh=mesh, in_specs=in_specs, out_specs=out_specs, check_vma=False)
```

profile of v0, /device:TPU:0, one launch (start us, length us, event | category | flops | bytes accessed | tf_op | source)
XLA Modules:
  0.0 135.8 jit_solution(463698671766163533)
XLA Ops:
  0.0 1.3 fusion.100
  5.1 1.4 %fusion.101 = (s32[1]{0:T(128)}, s32[1]{0:T(128)}, s32[1]{0:T(128)}) fusion(s32[3]{0:T(128)} %param.6), kind=kLoop, calls=%fused_computation.112 | loop fusion | bytes 24 | tf_op jit(solution)/shard_map/slice | solution.py:14
  7.2 1.3 fusion.91
  8.5 7.4 %fusion.6 = f32[8,192,192,1]{1,2,3,0:T(8,128)S(1)} fusion(f32[512]{0:T(512)S(1)} %get-tuple-element.31, f32[512]{0:T(512)S(1)} %get-tuple-element.32, bf16[8,2,3,192,512]{4,3,2,1,0:T(8,128)(2,1)} %param.5), kind=kOutput, calls=%fused_computation.9 | convolution fusion | flops 920125440 | bytes 15339520 | tf_op jit(solution)/shard_map/tckx,tclx->tkl/dot_general | solution.py:67
  15.9 7.5 %fusion.54 = f32[8,192,192]{2,1,0:T(8,128)S(1)} fusion(f32[8,192,192,1]{1,2,3,0:T(8,128)S(1)} %fusion.6, bf16[8,2,3,192,512]{4,3,2,1,0:T(8,128)(2,1)} %param.5, f32[512]{0:T(512)S(1)} %get-tuple-element.31, f32[512]{0:T(512)S(1)} %get-tuple-element.32), kind=kOutput, calls=%fused_computation.55 | convolution fusion | flops 920420352 | bytes 16519168 | tf_op jit(solution)/shard_map/tckx,tclx->tkl/dot_general | solution.py:67
  23.4 7.4 %fusion.4 = f32[8,192,192,1]{1,2,3,0:T(8,128)S(1)} fusion(f32[512]{0:T(512)S(1)} %get-tuple-element.31, f32[512]{0:T(512)S(1)} %get-tuple-element.32, bf16[8,2,3,192,512]{4,3,2,1,0:T(8,128)(2,1)} %param.5), kind=kOutput, calls=%fused_computation.8 | convolution fusion | flops 920125440 | bytes 15339520 | tf_op jit(solution)/shard_map/tckx,tclx->tkl/dot_general | solution.py:70
  30.8 7.5 %fusion.53 = f32[8,192,192]{2,1,0:T(8,128)S(1)} fusion(f32[8,192,192,1]{1,2,3,0:T(8,128)S(1)} %fusion.4, bf16[8,2,3,192,512]{4,3,2,1,0:T(8,128)(2,1)} %param.5, f32[512]{0:T(512)S(1)} %get-tuple-element.31, f32[512]{0:T(512)S(1)} %get-tuple-element.32), kind=kOutput, calls=%fused_computation.53 | convolution fusion | flops 920420352 | bytes 16519168 | tf_op jit(solution)/shard_map/tckx,tclx->tkl/dot_general | solution.py:70
  38.3 0.5 pad_maximum_fusion
  38.8 77.0 %all-reduce.1 = bf16[8,192,384]{2,1,0:T(8,128)(2,1)S(1)} all-reduce(f32[8,192,384]{2,1,0:T(8,128)S(1)} %pad_maximum_fusion), channel_id=1, replica_groups=mesh['groups'=2,'sink'=16] {'sink'}, use_global_device_ids=true, to_apply=%region_0.1 | all-reduce | flops 589824 | bytes 3538944 | tf_op jit(solution)/shard_map/psum | solution.py:74
  116.1 0.4 copy-done
  116.5 1.8 %fusion.97 = (bf16[1,1,384,768]{3,2,1,0:T(8,128)(2,1)S(1)}, bf16[1,1,384,768]{3,2,1,0:T(8,128)(2,1)S(1)}, bf16[1,1,384,768]{3,2,1,0:T(8,128)(2,1)S(1)}, bf16[1,1,384,768]{3,2,1,0:T(8,128)(2,1)S(1)}) fusion(bf16[1,2,768,768]{3,2,1,0:T(8,128)(2,1)} %param.7), kind=kLoop, calls=%fused_computation.108 | loop fusion | bytes 4718592 | tf_op jit(solution)/shard_map/jit(_roll_static)/slice | solution.py:27
  118.3 0.3 maximum_multiply_fusion
  118.5 1.4 %convert_bitcast_fusion = bf16[4,384,768]{2,1,0:T(8,128)(2,1)S(1)} fusion(bf16[4,192,768]{2,1,0:T(8,128)(2,1)S(1)} %get-tuple-element.30, bf16[4,192,768]{2,1,0:T(8,128)(2,1)S(1)} %get-tuple-element.29, bf16[192,192]{1,0:T(8,128)(2,1)S(1)} %get-tuple-element.23, bf16[192,192]{1,0:T(8,128)(2,1)S(1)} %get-tuple-element.22, ...), kind=kOutput, calls=%fused_computation.50 | convolution fusion | flops 913047552 | bytes 4939776 | tf_op jit(solution)/shard_map/kl,alc->akc/dot_general | solution.py:30
  120.0 1.2 fusion.96
  121.2 3.5 %convert_element_type.66 = bf16[768,4,192]{2,1,0:T(4,128)(2,1)S(1)} reshape(bf16[4,192,768]{2,1,0:T(8,128)(2,1)} %get-tuple-element.7) | data formatting | bytes 2359296 | tf_op jit(solution)/shard_map/convert_element_type | solution.py:31
  124.6 1.1 fusion.98
  125.7 1.0 copy.28
  126.8 1.0 copy.29
  127.7 1.4 %convert_element_type.67 = bf16[768,4,192]{2,1,0:T(4,128)(2,1)S(1)} reshape(bf16[4,192,768]{2,1,0:T(8,128)(2,1)S(1)} %get-tuple-element.8) | data formatting | bytes 2359296 | tf_op jit(solution)/shard_map/convert_element_type | solution.py:32
  129.2 1.1 fusion.99
  130.5 2.1 %fusion.48 = bf16[768,4,384]{0,2,1:T(8,128)(2,1)S(1)} fusion(bf16[768,2,192]{2,0,1:T(8,128)(2,1)S(1)} %copy.31, bf16[768,2,192]{2,0,1:T(8,128)(2,1)S(1)} %copy.30, bf16[768,2,192]{2,0,1:T(8,128)(2,1)S(1)} %copy-done.3, bf16[768,2,192]{2,0,1:T(8,128)(2,1)S(1)} %copy-done.2, bf16[192,192]{1,0:T(8,128)(2,1)S(1)} %get-tuple-element.20, ...), kind=kOutput, calls=%fused_computation.51 | convolution fusion | flops 917471232 | bytes 5013504 | tf_op jit(solution)/shard_map/rbl,nl->rbn/dot_general | solution.py:45
  132.8 0.6 copy.20
  133.5 0.6 copy.21
  134.1 1.6 %pad_maximum_fusion.1 = bf16[1,2,768,768]{3,2,1,0:T(8,128)(2,1)} fusion(bf16[1,1,768,768]{3,2,1,0:T(8,128)(2,1)S(1)} %copy.21, bf16[1,1,768,768]{3,2,1,0:T(8,128)(2,1)S(1)} %copy.20), kind=kLoop, calls=%fused_computation.49 | loop fusion | flops 1179648 | bytes 4718592 | tf_op jit(solution)/shard_map/stack | solution.py:48
  (15 shorter events, 0.6 us)
Async XLA Ops:
  38.7 79.5 %copy-start.4 = (bf16[4]{0:T(256)(128)(2,1)S(1)}, bf16[4]{0:T(256)(128)(2,1)}, u32[]{:S(2)}) copy-start(bf16[4]{0:T(256)(128)(2,1)} %constant.78.clone) | copy-start | bytes 28
  115.8 0.6 copy-start
  127.7 2.7 %copy-start.1 = (bf16[192,384]{1,0:T(8,128)(2,1)S(1)}, bf16[192,384]{1,0:T(8,128)(2,1)}, u32[]{:S(2)}) copy-start(bf16[192,384]{1,0:T(8,128)(2,1)} %copy-done) | copy-start | bytes 442372
  129.1 1.4 %copy-start.2 = (bf16[768,2,192]{2,0,1:T(8,128)(2,1)S(1)}, bf16[768,2,192]{2,0,1:T(8,128)(2,1)}, u32[]{:S(2)}) copy-start(bf16[768,2,192]{2,0,1:T(8,128)(2,1)} %copy.28) | copy-start | bytes 1769476
  129.2 1.4 %copy-start.3 = (bf16[768,2,192]{2,0,1:T(8,128)(2,1)S(1)}, bf16[768,2,192]{2,0,1:T(8,128)(2,1)}, u32[]{:S(2)}) copy-start(bf16[768,2,192]{2,0,1:T(8,128)(2,1)} %copy.29) | copy-start | bytes 1769476
where the time goes:
time: 136 us
  blocking collectives  77 us (57%)
  matrix products  33.3 us (24%)
  local copies, waits for them, and re-layouts  16.9 us (12%)
  between operations  4.72 us (3%)
  other arithmetic  3.86 us (3%)
    psum x1, blocking collectives, shards(): totals = lax.psum(partial_sums, 'sink')  77 us
    dot_general x1, matrix products, shards(): jnp.einsum(form, vec_re, rot_re, preferred_element_type=jnp.float32)  7.48 us
    dot_general x1, matrix products, shards(): jnp.einsum(form, vec_im, rot_re, preferred_element_type=jnp.float32)  7.48 us
    dot_general x1, matrix products, shards(): jnp.einsum(form, vec_re, rot_im, preferred_element_type=jnp.float32)  7.37 us
    dot_general x1, matrix products, shards(): jnp.einsum(form, vec_im, rot_im, preferred_element_type=jnp.float32)  7.37 us
    convert_element_type x1, local copies, waits for them, and re-layouts, pair_block(): x_re = stacked[:, :width].reshape(4 * width, 4 * width).astype(jnp.bfloat16)  3.47 us

commit v1 on v0

v1 whole, which is shorter than its diff:
```python
import functools
import math

import jax
import jax.numpy as jnp
from jax import lax
from jax.experimental import pallas as pl
from jax.experimental.pallas import tpu as pltpu
from jax.sharding import PartitionSpec as P

BF16 = jnp.bfloat16
F32 = jnp.float32
NT_DIMS = (((1,), (1,)), ((), ()))


def dot_nt(left, right):
    return lax.dot_general(left, right, NT_DIMS, preferred_element_type=F32)


def elemental_kernel(devices, scalars, vec, keep, send, trig, total):
    width, sites = vec.shape[3], vec.shape[4]

    @pl.when(pl.program_id(0) == 0)
    def _():
        local = lax.broadcasted_iota(jnp.int32, (8, sites), 1)
        extent = sites // 16
        turn = jnp.mod(scalars[0] * scalars[3], devices).astype(F32) / devices
        second = scalars[1] * lax.shift_right_logical(local, 4)
        turn = turn + jnp.mod(second, extent).astype(F32) / extent
        third = scalars[2] * jnp.bitwise_and(local, 15)
        turn = turn + jnp.mod(third, 16).astype(F32) / 16.0
        theta = (2.0 * math.pi) * turn
        trig[0] = jnp.cos(theta)
        trig[1] = jnp.sin(theta)

    cosine = trig[0, 0:1, :]
    sine = trig[1, 0:1, :]
    with_re = jnp.zeros((2 * width, width), F32)
    with_im = jnp.zeros((2 * width, width), F32)
    for color in range(vec.shape[2]):
        low_re = vec[0, 0, color]
        low_im = vec[0, 1, color]
        vec_re = low_re.astype(F32)
        vec_im = low_im.astype(F32)
        rot_re = (cosine * vec_re + sine * vec_im).astype(BF16)
        rot_im = (cosine * vec_im - sine * vec_re).astype(BF16)
        both = jnp.concatenate([low_re, low_im], axis=0)
        with_re = with_re + dot_nt(both, rot_re)
        with_im = with_im + dot_nt(both, rot_im)
    real = with_re[:width] + with_im[width:]
    imag = with_im[:width] - with_re[width:]
    total[...] = jnp.concatenate([real, imag], axis=1)
    rows = width // 4
    mine = jnp.bitwise_and(scalars[3], 3)
    for flip in range(4):
        start = pl.multiple_of(jnp.bitwise_xor(mine, flip) * rows, rows)
        block = total[pl.ds(start, rows), :]
        if flip % 2 == 0:
            keep[flip // 2, 0] = block
        else:
            send[flip // 2, 0] = block.astype(BF16)


def elementals(eigvecs, scalars, devices, first, count):
    _, _, colors, width, sites = eigvecs.shape
    rows = width // 4
    out_block = pl.BlockSpec((2, 1, rows, 2 * width), lambda t, s: (0, t, 0, 0))
    flops = count * 8 * colors * width * width * sites
    return pl.pallas_call(
        functools.partial(elemental_kernel, devices),
        grid_spec=pltpu.PrefetchScalarGridSpec(
            num_scalar_prefetch=1,
            grid=(count,),
            in_specs=[
                pl.BlockSpec((1, 2, colors, width, sites), lambda t, s: (first + t, 0, 0, 0, 0))
            ],
            out_specs=[out_block, out_block],
            scratch_shapes=[
                pltpu.VMEM((2, 8, sites), F32),
                pltpu.VMEM((width, 2 * width), F32),
            ],
        ),
        out_shape=[
            jax.ShapeDtypeStruct((2, count, rows, 2 * width), F32),
            jax.ShapeDtypeStruct((2, count, rows, 2 * width), BF16),
        ],
        compiler_params=pltpu.CompilerParams(vmem_limit_bytes=24 * 1024 * 1024),
        cost_estimate=pl.CostEstimate(
            flops=flops, bytes_accessed=count * 2 * colors * width * sites * 2, transcendentals=0
        ),
        name="partial_elementals",
    )(scalars, eigvecs)


def block_kernel(scalars, own, by_core, by_pair, by_both, peram, out, sink_el, src_el, left_mat, right_mat):
    width = sink_el.shape[0]
    rows = width // 4

    @pl.when(pl.program_id(0) == 0)
    def _():
        for flip, part in enumerate((own, by_core, by_pair, by_both)):
            start = pl.multiple_of(jnp.bitwise_xor(scalars[0], flip) * rows, rows)
            sink_el[pl.ds(start, rows), :] = part[0]
            src_el[pl.ds(start, rows), :] = part[1]
        a_re = sink_el[:, :width]
        a_im = sink_el[:, width:]
        left_mat[:width] = jnp.concatenate([a_re, -a_im], axis=1)
        left_mat[width:] = jnp.concatenate([a_im, a_re], axis=1)
        e_re = src_el[:, :width]
        e_im = src_el[:, width:]
        right_mat[:width] = jnp.concatenate([e_re, e_im], axis=1)
        right_mat[width:] = jnp.concatenate([-e_im, e_re], axis=1)

    sign = jnp.where(pl.program_id(0) < 2, 1.0, -1.0)
    stacked = jnp.concatenate([peram[0], peram[1]], axis=0)
    left = jnp.dot(left_mat[...], stacked, preferred_element_type=F32) * sign
    left = left.astype(BF16)
    y_re = jnp.concatenate([left[:width, b * width : (b + 1) * width] for b in (2, 3, 0, 1)], axis=0)
    y_im = jnp.concatenate([left[width:, b * width : (b + 1) * width] for b in (2, 3, 0, 1)], axis=0)
    y_both = jnp.concatenate([y_re, y_im], axis=1)
    m_re = dot_nt(y_both, right_mat[:width]).astype(BF16)
    m_im = dot_nt(y_both, right_mat[width:]).astype(BF16)
    out[0] = jnp.concatenate([m_re[b * width : (b + 1) * width] for b in range(4)], axis=1)
    out[1] = jnp.concatenate([m_im[b * width : (b + 1) * width] for b in range(4)], axis=1)


def pair_block(peram, place, parts):
    full = peram.shape[-1]
    width = full // 4
    part_spec = pl.BlockSpec((2, width // 4, 2 * width), lambda a, s: (0, 0, 0))
    return pl.pallas_call(
        block_kernel,
        grid_spec=pltpu.PrefetchScalarGridSpec(
            num_scalar_prefetch=1,
            grid=(4,),
            in_specs=[part_spec] * 4
            + [pl.BlockSpec((2, width, full), lambda a, s: (0, (a + 2) % 4, 0))],
            out_specs=pl.BlockSpec((2, width, full), lambda a, s: (0, a, 0)),
            scratch_shapes=[
                pltpu.VMEM((width, 2 * width), BF16),
                pltpu.VMEM((width, 2 * width), BF16),
                pltpu.VMEM((2 * width, 2 * width), BF16),
                pltpu.VMEM((2 * width, 2 * width), BF16),
            ],
        ),
        out_shape=jax.ShapeDtypeStruct(peram.shape, BF16),
        compiler_params=pltpu.CompilerParams(vmem_limit_bytes=24 * 1024 * 1024),
        cost_estimate=pl.CostEstimate(
            flops=2 * 8 * full * full * width, bytes_accessed=8 * full * full, transcendentals=0
        ),
        name="meson_block",
    )(place, *parts, peram)


def swap(value, flip, devices):
    return lax.ppermute(value, "sink", [(i, i ^ flip) for i in range(devices)])


def sum_and_share(keep, send, device, devices):
    _, count, rows, both = keep.shape
    owners = devices // 4
    group = device // 4
    over_core = keep + swap(send, 1, devices).astype(F32)
    over_pair = over_core[0] + swap(over_core[1].astype(BF16), 2, devices).astype(F32)
    cut = over_pair.reshape(owners, count * rows // owners, both)
    low = cut.astype(BF16)
    total = lax.dynamic_index_in_dim(cut, group, 0, keepdims=False)
    for flip in range(1, owners):
        piece = lax.dynamic_index_in_dim(low, group ^ flip, 0, keepdims=False)
        total = total + swap(piece, 4 * flip, devices).astype(F32)
    total = total.astype(BF16)
    shared = [total] + [swap(total, 4 * flip, devices) for flip in range(1, owners)]
    shared = jnp.stack(shared)
    shared = jnp.take(shared, jnp.arange(owners) ^ group, axis=0)
    return shared.reshape(count, rows, both)


def shards(eigvecs, momentum, peram, times):
    devices = lax.axis_size("sink")
    device = lax.axis_index("sink")
    slices = eigvecs.shape[0]
    scalars = jnp.concatenate([momentum, device[None].astype(jnp.int32)])
    wanted = [times, swap(times, 1, devices)]
    other = swap(jnp.stack(wanted), 2, devices)
    wanted = wanted + [other[0], other[1]]
    half = slices // 2
    chunks = []
    for first in (0, half):
        keep, send = elementals(eigvecs, scalars, devices, first, half)
        chunks.append(sum_and_share(keep, send, device, devices))
    quarter = jnp.concatenate(chunks, axis=0)
    place = jnp.bitwise_and(device, 3)[None].astype(jnp.int32)
    outputs = []
    for pair in range(peram.shape[0]):
        parts = []
        for flip in range(4):
            chosen = jnp.stack(
                [
                    lax.dynamic_index_in_dim(quarter, wanted[flip][pair, side], 0, keepdims=False)
                    for side in range(2)
                ]
            )
            parts.append(chosen if flip == 0 else swap(chosen, flip, devices))
        outputs.append(pair_block(peram[pair], place, parts))
    return jnp.stack(outputs)


def solution(mesh):
    in_specs = (
        P("groups", None, None, None, "sink"),
        P("groups"),
        P(("groups", "sink"), None, None, None),
        P(("groups", "sink"), None),
    )
    out_specs = P(("groups", "sink"), None, None, None)
    return jax.shard_map(shards, mesh=mesh, in_specs=in_specs, out_specs=out_specs, check_vma=False)
```

time: 136 us -> 78.7 us (0.58)
  blocking collectives: 77 us -> 0 us
  matrix products: 33.3 us -> 0 us
  starting transfers between devices: 0 us -> 26.1 us
  Pallas kernels: 0 us -> 16 us
  waiting for transfers between devices: 0 us -> 12.2 us
  between operations: 4.72 us -> 15.8 us
  local copies, waits for them, and re-layouts: 16.9 us -> 6.89 us
  other arithmetic: 3.86 us -> 1.38 us
    psum x1 -> x0, blocking collectives: 77 us -> none  [shards(): totals = lax.psum(partial_sums, 'sink')]
    dot_general x6 -> x0, matrix products: 33.3 us -> none  [the longest x1 7.48 us: shards(): jnp.einsum(form, vec_re, rot_re, preferred_element_type=jnp.float32)]
    ppermute x0 -> x21, starting transfers between devices: none -> 26.1 us  [swap(): return lax.ppermute(value, 'sink', [(i, i ^ flip) for i in range(devices)])]
    pallas_call x0 -> x3, Pallas kernels: none -> 16 us  [the longest x2 9.76 us: elementals(): pl.pallas_call(functools.partial(elemental_kernel, devices), grid_spec=pl...]
    ppermute x0 -> x21, waiting for transfers between devices: none -> 12.2 us  [swap(): return lax.ppermute(value, 'sink', [(i, i ^ flip) for i in range(devices)])]
    slice x7 -> x3, local copies, waits for them, and re-layouts: 8.01 us -> 1.95 us  [shards(): wanted[flip][pair, side]]
    convert_element_type x2, local copies, waits for them, and re-layouts: 4.86 us -> 0.04 us  [sum_and_share(): over_core[1].astype(BF16)]
    another operation x1 -> x7, other arithmetic: 1.61 us -> 0.11 us  [the longest x2 0.05 us: sum_and_share(): shared = jnp.stack(shared)]
  transfers between devices with their start and end apart: 0 -> 21, of which waited for: 0 -> 7; matrix products, arithmetic and copies ran while one was open for 0% -> 5% of each run, Pallas kernels for 0% -> 12%
where the time goes in v1:
time: 78.7 us; the launch traced here: 78.4 us
  starting transfers between devices  26.1 us (33%)
  Pallas kernels  16 us (20%)
  between operations  15.8 us (20%)
  waiting for transfers between devices  12.2 us (16%)
  local copies, waits for them, and re-layouts  6.89 us (9%)
  other arithmetic  1.38 us (2%)
    ppermute x21, starting transfers between devices, swap(): return lax.ppermute(value, 'sink', [(i, i ^ flip) for i in range(devices)])  26.1 us
    ppermute x21, waiting for transfers between devices, swap(): return lax.ppermute(value, 'sink', [(i, i ^ flip) for i in range(devices)])  12.2 us
    pallas_call x2, Pallas kernels, elementals(): pl.pallas_call(functools.partial(elemental_kernel, devices), grid_spec=pl...  9.76 us
    pallas_call x1, Pallas kernels, pair_block(): pl.pallas_call(block_kernel, grid_spec=pltpu.PrefetchScalarGridSpec(num_s...  6.27 us
    unnamed x6, local copies, waits for them, and re-layouts  3.69 us
    slice x3, local copies, waits for them, and re-layouts, shards(): wanted[flip][pair, side]  1.95 us
  transfers between devices with their start and end apart: 21, of which 7 were waited for; matrix products, arithmetic and copies ran while one was open for 5% of the time, Pallas kernels for 12%

profile of v1, /device:TPU:0, one launch (start us, length us, event | category | flops | bytes accessed | tf_op | source)
XLA Modules:
  0.0 78.4 jit_solution(2852266397640936143)
XLA Ops:
  0.5 0.7 pad_add_fusion.1.scalars
  1.2 3.7 %copy-done = bf16[8,2,3,192,512]{4,3,2,1,0:T(8,128)(2,1)S(1)} copy-done((bf16[8,2,3,192,512]{4,3,2,1,0:T(8,128)(2,1)S(1)}, bf16[8,2,3,192,512]{4,3,2,1,0:T(8,128)(2,1)}, u32[]{:S(2)}) %copy-start) | copy-done | bytes 9437208
  4.9 4.9 %partial_elementals.3 = (f32[2,4,48,384]{3,2,1,0:T(8,128)S(1)}, bf16[2,4,48,384]{3,2,1,0:T(8,128)(2,1)S(1)}) custom-call(s32[4]{0:T(128)S(1)} %pad_add_fusion.1.scalars, bf16[8,2,3,192,512]{4,3,2,1,0:T(8,128)(2,1)S(1)} %copy-done), custom_call_target="tpu_custom_call" | custom-call | flops 1811939328 | bytes 4718592 | tf_op jit(solution)/shard_map/partial_elementals/pallas_call | solution.py:69
  9.9 4.9 %partial_elementals.2 = (f32[2,4,48,384]{3,2,1,0:T(8,128)S(1)}, bf16[2,4,48,384]{3,2,1,0:T(8,128)(2,1)S(1)}) custom-call(s32[4]{0:T(128)S(1)} %pad_add_fusion.1.scalars, bf16[8,2,3,192,512]{4,3,2,1,0:T(8,128)(2,1)S(1)} %copy-done), custom_call_target="tpu_custom_call" | custom-call | flops 1811939328 | bytes 4718592 | tf_op jit(solution)/shard_map/partial_elementals/pallas_call | solution.py:69
  15.3 0.6 fusion.25
  23.3 2.7 %collective-permute-start.18 = (s32[2,1,2]{2,1,0:T(1,128)S(1)}, s32[2,1,2]{2,1,0:T(1,128)S(1)}, u32[]{:S(2)}, u32[]{:S(2)}) collective-permute-start(s32[2,1,2]{2,1,0:T(1,128)S(1)} %pad_add_fusion), channel_id=1, source_target_pairs={{0,2},{1,3},{2,0},{3,1},{4,6},{5,7},{6,4},{7,5},{8,10},{9,11},{10,... | collective-permute-start | bytes 56 | tf_op jit(solution)/shard_map/ppermute | solution.py:156
  27.5 0.7 fusion.22
  35.8 2.1 %collective-permute-start.9 = (bf16[4,48,384]{2,1,0:T(8,128)(2,1)S(1)}, bf16[4,48,384]{2,1,0:T(8,128)(2,1)S(1)}, u32[]{:S(2)}, u32[]{:S(2)}) collective-permute-start(bf16[4,48,384]{2,1,0:T(8,128)(2,1)S(1)} %fusion.3), channel_id=1, source_target_pairs={{0,2},{1,3},{2,0},{3,1},{4,6},{5,7},{6,4},{7,5},{8,10},{9,11},{10,... | collective-permute-start | bytes 442376 | tf_op jit(solution)/shard_map/ppermute | solution.py:156
  38.1 4.5 %collective-permute-done.9 = bf16[4,48,384]{2,1,0:T(8,128)(2,1)S(1)} collective-permute-done((bf16[4,48,384]{2,1,0:T(8,128)(2,1)S(1)}, bf16[4,48,384]{2,1,0:T(8,128)(2,1)S(1)}, u32[]{:S(2)}, u32[]{:S(2)}) %collective-permute-start.9) | collective-permute-done | bytes 147488 | tf_op jit(solution)/shard_map/ppermute | solution.py:156
  42.7 2.2 %collective-permute-start.10 = (bf16[48,384]{1,0:T(8,128)(2,1)S(1)}, bf16[48,384]{1,0:T(8,128)(2,1)S(1)}, u32[]{:S(2)}, u32[]{:S(2)}) collective-permute-start(bf16[48,384]{1,0:T(8,128)(2,1)S(1)} %get-tuple-element.26), channel_id=1, source_target_pairs={{0,4},{1,5},{2,6},{3,7},{4,0},{5,1},{6,2},{7,3},{8,12},{9,13},{10,... | collective-permute-start | bytes 110600 | tf_op jit(solution)/shard_map/ppermute | solution.py:156
  44.9 2.5 %collective-permute-start.12 = (bf16[48,384]{1,0:T(8,128)(2,1)S(1)}, bf16[48,384]{1,0:T(8,128)(2,1)S(1)}, u32[]{:S(2)}, u32[]{:S(2)}) collective-permute-start(bf16[48,384]{1,0:T(8,128)(2,1)S(1)} %get-tuple-element.27), channel_id=1, source_target_pairs={{0,12},{1,13},{2,14},{3,15},{4,8},{5,9},{6,10},{7,11},{8,4},{9,5},... | collective-permute-start | bytes 110600 | tf_op jit(solution)/shard_map/ppermute | solution.py:156
  47.5 1.9 %collective-permute-start.2 = (bf16[48,384]{1,0:T(8,128)(2,1)S(1)}, bf16[48,384]{1,0:T(8,128)(2,1)S(1)}, u32[]{:S(2)}, u32[]{:S(2)}) collective-permute-start(bf16[48,384]{1,0:T(8,128)(2,1)S(1)} %get-tuple-element.29), channel_id=1, source_target_pairs={{0,4},{1,5},{2,6},{3,7},{4,0},{5,1},{6,2},{7,3},{8,12},{9,13},{10,... | collective-permute-start | bytes 110600 | tf_op jit(solution)/shard_map/ppermute | solution.py:156
  49.4 2.5 %collective-permute-start.4 = (bf16[48,384]{1,0:T(8,128)(2,1)S(1)}, bf16[48,384]{1,0:T(8,128)(2,1)S(1)}, u32[]{:S(2)}, u32[]{:S(2)}) collective-permute-start(bf16[48,384]{1,0:T(8,128)(2,1)S(1)} %get-tuple-element.30), channel_id=1, source_target_pairs={{0,12},{1,13},{2,14},{3,15},{4,8},{5,9},{6,10},{7,11},{8,4},{9,5},... | collective-permute-start | bytes 110600 | tf_op jit(solution)/shard_map/ppermute | solution.py:156
  51.9 1.2 %collective-permute-done.11 = bf16[48,384]{1,0:T(8,128)(2,1)S(1)} collective-permute-done((bf16[48,384]{1,0:T(8,128)(2,1)S(1)}, bf16[48,384]{1,0:T(8,128)(2,1)S(1)}, u32[]{:S(2)}, u32[]{:S(2)}) %collective-permute-start.11) | collective-permute-done | bytes 36896 | tf_op jit(solution)/shard_map/ppermute | solution.py:156
  53.1 2.3 %collective-permute-start.15 = (bf16[48,384]{1,0:T(8,128)(2,1)S(1)}, bf16[48,384]{1,0:T(8,128)(2,1)S(1)}, u32[]{:S(2)}, u32[]{:S(2)}) collective-permute-start(bf16[48,384]{1,0:T(8,128)(2,1)S(1)} %fusion.6), channel_id=1, source_target_pairs={{0,12},{1,13},{2,14},{3,15},{4,8},{5,9},{6,10},{7,11},{8,4},{9,5},... | collective-permute-start | bytes 110600 | tf_op jit(solution)/shard_map/ppermute | solution.py:156
  55.4 2.2 %collective-permute-start.13 = (bf16[48,384]{1,0:T(8,128)(2,1)S(1)}, bf16[48,384]{1,0:T(8,128)(2,1)S(1)}, u32[]{:S(2)}, u32[]{:S(2)}) collective-permute-start(bf16[48,384]{1,0:T(8,128)(2,1)S(1)} %fusion.6), channel_id=1, source_target_pairs={{0,4},{1,5},{2,6},{3,7},{4,0},{5,1},{6,2},{7,3},{8,12},{9,13},{10,... | collective-permute-start | bytes 110600 | tf_op jit(solution)/shard_map/ppermute | solution.py:156
  57.6 2.3 %collective-permute-start.7 = (bf16[48,384]{1,0:T(8,128)(2,1)S(1)}, bf16[48,384]{1,0:T(8,128)(2,1)S(1)}, u32[]{:S(2)}, u32[]{:S(2)}) collective-permute-start(bf16[48,384]{1,0:T(8,128)(2,1)S(1)} %fusion.9), channel_id=1, source_target_pairs={{0,12},{1,13},{2,14},{3,15},{4,8},{5,9},{6,10},{7,11},{8,4},{9,5},... | collective-permute-start | bytes 110600 | tf_op jit(solution)/shard_map/ppermute | solution.py:156
  59.9 2.2 %collective-permute-start.5 = (bf16[48,384]{1,0:T(8,128)(2,1)S(1)}, bf16[48,384]{1,0:T(8,128)(2,1)S(1)}, u32[]{:S(2)}, u32[]{:S(2)}) collective-permute-start(bf16[48,384]{1,0:T(8,128)(2,1)S(1)} %fusion.9), channel_id=1, source_target_pairs={{0,4},{1,5},{2,6},{3,7},{4,0},{5,1},{6,2},{7,3},{8,12},{9,13},{10,... | collective-permute-start | bytes 110600 | tf_op jit(solution)/shard_map/ppermute | solution.py:156
  62.6 0.7 collective-permute-done.7
  63.4 1.3 %collective-permute-done.6 = bf16[48,384]{1,0:T(8,128)(2,1)S(1)} collective-permute-done((bf16[48,384]{1,0:T(8,128)(2,1)S(1)}, bf16[48,384]{1,0:T(8,128)(2,1)S(1)}, u32[]{:S(2)}, u32[]{:S(2)}) %collective-permute-start.6) | collective-permute-done | bytes 36896 | tf_op jit(solution)/shard_map/ppermute | solution.py:156
  65.8 1.9 %collective-permute-start.19 = (bf16[2,48,384]{2,1,0:T(8,128)(2,1)S(1)}, bf16[2,48,384]{2,1,0:T(8,128)(2,1)S(1)}, u32[]{:S(2)}, u32[]{:S(2)}) collective-permute-start(bf16[2,48,384]{2,1,0:T(8,128)(2,1)S(1)} %pad_maximum_fusion.4), channel_id=1, source_target_pairs={{0,2},{1,3},{2,0},{3,1},{4,6},{5,7},{6,4},{7,5},{8,10},{9,11},{10,... | collective-permute-start | bytes 221192 | tf_op jit(solution)/shard_map/ppermute | solution.py:156
  67.9 2.7 %collective-permute-done.19.by_pair = bf16[2,48,384]{2,1,0:T(8,128)(2,1)S(1)} collective-permute-done((bf16[2,48,384]{2,1,0:T(8,128)(2,1)S(1)}, bf16[2,48,384]{2,1,0:T(8,128)(2,1)S(1)}, u32[]{:S(2)}, u32[]{:S(2)}) %collective-permute-start.19) | collective-permute-done | bytes 73760 | tf_op jit(solution)/shard_map/ppermute | solution.py:156
  70.6 1.4 %collective-permute-done.20.by_both = bf16[2,48,384]{2,1,0:T(8,128)(2,1)S(1)} collective-permute-done((bf16[2,48,384]{2,1,0:T(8,128)(2,1)S(1)}, bf16[2,48,384]{2,1,0:T(8,128)(2,1)S(1)}, u32[]{:S(2)}, u32[]{:S(2)}) %collective-permute-start.20) | collective-permute-done | bytes 73760 | tf_op jit(solution)/shard_map/ppermute | solution.py:156
  72.1 6.3 %meson_block.1 = bf16[2,768,768]{2,1,0:T(8,128)(2,1)} custom-call(s32[1]{0:T(128)} %bitcast.scalars, bf16[2,48,384]{2,1,0:T(8,128)(2,1)S(1)} %pad_maximum_fusion.2.own, bf16[2,48,384]{2,1,0:T(8,128)(2,1)S(1)} %collective-permute-done.17.by_core, bf16[2,48,384]{2,1,0:T(8,128)(2,1)S(1)} %collective-permute-done.19.by_pair, ...), custom_call_target="tpu_custom_call" | custom-call | flops 1811939328 | bytes 4718592 | tf_op jit(solution)/shard_map/meson_block/pallas_call | solution.py:131
  (57 shorter events, 4.4 us)
Async XLA Ops:
  0.0 20.0 %collective-permute-start.16 = (s32[1,2]{1,0:T(1,128)}, s32[1,2]{1,0:T(1,128)S(1)}, u32[]{:S(2)}, u32[]{:S(2)}) collective-permute-start(s32[1,2]{1,0:T(1,128)} %param.9), channel_id=1, source_target_pairs={{0,1},{1,0},{2,3},{3,2},{4,5},{5,4},{6,7},{7,6},{8,9},{9,8},{10,11... | collective-permute-start | bytes 32 | tf_op jit(solution)/shard_map/ppermute | solution.py:156
  1.2 3.7 %copy-start = (bf16[8,2,3,192,512]{4,3,2,1,0:T(8,128)(2,1)S(1)}, bf16[8,2,3,192,512]{4,3,2,1,0:T(8,128)(2,1)}, u32[]{:S(2)}) copy-start(bf16[8,2,3,192,512]{4,3,2,1,0:T(8,128)(2,1)} %vec.3) | copy-start | bytes 28311556
  9.8 5.6 %copy-start.2 = (s32[1,2]{1,0:T(1,128)S(1)}, s32[1,2]{1,0:T(1,128)}, u32[]{:S(2)}) copy-start(s32[1,2]{1,0:T(1,128)} %param.9) | copy-start | bytes 28
  9.8 26.0 %collective-permute-start.8 = (bf16[2,4,48,384]{3,2,1,0:T(8,128)(2,1)S(1)}, bf16[2,4,48,384]{3,2,1,0:T(8,128)(2,1)S(1)}, u32[]{:S(2)}, u32[]{:S(2)}) collective-permute-start(bf16[2,4,48,384]{3,2,1,0:T(8,128)(2,1)S(1)} %get-tuple-element.13), channel_id=1, source_target_pairs={{0,1},{1,0},{2,3},{3,2},{4,5},{5,4},{6,7},{7,6},{8,9},{9,8},{10,11... | collective-permute-start | bytes 884744 | tf_op jit(solution)/shard_map/ppermute | solution.py:156
  14.8 23.2 %collective-permute-start = (bf16[2,4,48,384]{3,2,1,0:T(8,128)(2,1)S(1)}, bf16[2,4,48,384]{3,2,1,0:T(8,128)(2,1)S(1)}, u32[]{:S(2)}, u32[]{:S(2)}) collective-permute-start(bf16[2,4,48,384]{3,2,1,0:T(8,128)(2,1)S(1)} %get-tuple-element.11), channel_id=1, source_target_pairs={{0,1},{1,0},{2,3},{3,2},{4,5},{5,4},{6,7},{7,6},{8,9},{9,8},{10,11... | collective-permute-start | bytes 884744 | tf_op jit(solution)/shard_map/ppermute | solution.py:156
  23.3 4.2 %collective-permute-start.18 = (s32[2,1,2]{2,1,0:T(1,128)S(1)}, s32[2,1,2]{2,1,0:T(1,128)S(1)}, u32[]{:S(2)}, u32[]{:S(2)}) collective-permute-start(s32[2,1,2]{2,1,0:T(1,128)S(1)} %pad_add_fusion), channel_id=1, source_target_pairs={{0,2},{1,3},{2,0},{3,1},{4,6},{5,7},{6,4},{7,5},{8,10},{9,11},{10,... | collective-permute-start | bytes 56 | tf_op jit(solution)/shard_map/ppermute | solution.py:156
  35.8 6.8 %collective-permute-start.9 = (bf16[4,48,384]{2,1,0:T(8,128)(2,1)S(1)}, bf16[4,48,384]{2,1,0:T(8,128)(2,1)S(1)}, u32[]{:S(2)}, u32[]{:S(2)}) collective-permute-start(bf16[4,48,384]{2,1,0:T(8,128)(2,1)S(1)} %fusion.3), channel_id=1, source_target_pairs={{0,2},{1,3},{2,0},{3,1},{4,6},{5,7},{6,4},{7,5},{8,10},{9,11},{10,... | collective-permute-start | bytes 442376 | tf_op jit(solution)/shard_map/ppermute | solution.py:156
  38.0 9.4 %collective-permute-start.1 = (bf16[4,48,384]{2,1,0:T(8,128)(2,1)S(1)}, bf16[4,48,384]{2,1,0:T(8,128)(2,1)S(1)}, u32[]{:S(2)}, u32[]{:S(2)}) collective-permute-start(bf16[4,48,384]{2,1,0:T(8,128)(2,1)S(1)} %fusion.2), channel_id=1, source_target_pairs={{0,2},{1,3},{2,0},{3,1},{4,6},{5,7},{6,4},{7,5},{8,10},{9,11},{10,... | collective-permute-start | bytes 442376 | tf_op jit(solution)/shard_map/ppermute | solution.py:156
  42.7 9.2 %collective-permute-start.10 = (bf16[48,384]{1,0:T(8,128)(2,1)S(1)}, bf16[48,384]{1,0:T(8,128)(2,1)S(1)}, u32[]{:S(2)}, u32[]{:S(2)}) collective-permute-start(bf16[48,384]{1,0:T(8,128)(2,1)S(1)} %get-tuple-element.26), channel_id=1, source_target_pairs={{0,4},{1,5},{2,6},{3,7},{4,0},{5,1},{6,2},{7,3},{8,12},{9,13},{10,... | collective-permute-start | bytes 110600 | tf_op jit(solution)/shard_map/ppermute | solution.py:156
  44.9 7.0 %collective-permute-start.12 = (bf16[48,384]{1,0:T(8,128)(2,1)S(1)}, bf16[48,384]{1,0:T(8,128)(2,1)S(1)}, u32[]{:S(2)}, u32[]{:S(2)}) collective-permute-start(bf16[48,384]{1,0:T(8,128)(2,1)S(1)} %get-tuple-element.27), channel_id=1, source_target_pairs={{0,12},{1,13},{2,14},{3,15},{4,8},{5,9},{6,10},{7,11},{8,4},{9,5},... | collective-permute-start | bytes 110600 | tf_op jit(solution)/shard_map/ppermute | solution.py:156
  47.3 24.7 %copy-start.1 = (bf16[1,2,768,768]{3,2,1,0:T(8,128)(2,1)S(1)}, bf16[1,2,768,768]{3,2,1,0:T(8,128)(2,1)}, u32[]{:S(2)}) copy-start(bf16[1,2,768,768]{3,2,1,0:T(8,128)(2,1)} %param.8) | copy-start | bytes 7077892
  47.3 5.7 %collective-permute-start.11 = (bf16[48,384]{1,0:T(8,128)(2,1)S(1)}, bf16[48,384]{1,0:T(8,128)(2,1)S(1)}, u32[]{:S(2)}, u32[]{:S(2)}) collective-permute-start(bf16[48,384]{1,0:T(8,128)(2,1)S(1)} %get-tuple-element.28), channel_id=1, source_target_pairs={{0,8},{1,9},{2,10},{3,11},{4,12},{5,13},{6,14},{7,15},{8,0},{9,1},... | collective-permute-start | bytes 110600 | tf_op jit(solution)/shard_map/ppermute | solution.py:156
  47.5 7.8 %collective-permute-start.2 = (bf16[48,384]{1,0:T(8,128)(2,1)S(1)}, bf16[48,384]{1,0:T(8,128)(2,1)S(1)}, u32[]{:S(2)}, u32[]{:S(2)}) collective-permute-start(bf16[48,384]{1,0:T(8,128)(2,1)S(1)} %get-tuple-element.29), channel_id=1, source_target_pairs={{0,4},{1,5},{2,6},{3,7},{4,0},{5,1},{6,2},{7,3},{8,12},{9,13},{10,... | collective-permute-start | bytes 110600 | tf_op jit(solution)/shard_map/ppermute | solution.py:156
  49.4 8.1 %collective-permute-start.4 = (bf16[48,384]{1,0:T(8,128)(2,1)S(1)}, bf16[48,384]{1,0:T(8,128)(2,1)S(1)}, u32[]{:S(2)}, u32[]{:S(2)}) collective-permute-start(bf16[48,384]{1,0:T(8,128)(2,1)S(1)} %get-tuple-element.30), channel_id=1, source_target_pairs={{0,12},{1,13},{2,14},{3,15},{4,8},{5,9},{6,10},{7,11},{8,4},{9,5},... | collective-permute-start | bytes 110600 | tf_op jit(solution)/shard_map/ppermute | solution.py:156
  51.9 5.7 %collective-permute-start.3 = (bf16[48,384]{1,0:T(8,128)(2,1)S(1)}, bf16[48,384]{1,0:T(8,128)(2,1)S(1)}, u32[]{:S(2)}, u32[]{:S(2)}) collective-permute-start(bf16[48,384]{1,0:T(8,128)(2,1)S(1)} %get-tuple-element.31), channel_id=1, source_target_pairs={{0,8},{1,9},{2,10},{3,11},{4,12},{5,13},{6,14},{7,15},{8,0},{9,1},... | collective-permute-start | bytes 110600 | tf_op jit(solution)/shard_map/ppermute | solution.py:156
  53.1 6.8 %collective-permute-start.15 = (bf16[48,384]{1,0:T(8,128)(2,1)S(1)}, bf16[48,384]{1,0:T(8,128)(2,1)S(1)}, u32[]{:S(2)}, u32[]{:S(2)}) collective-permute-start(bf16[48,384]{1,0:T(8,128)(2,1)S(1)} %fusion.6), channel_id=1, source_target_pairs={{0,12},{1,13},{2,14},{3,15},{4,8},{5,9},{6,10},{7,11},{8,4},{9,5},... | collective-permute-start | bytes 110600 | tf_op jit(solution)/shard_map/ppermute | solution.py:156
  55.4 6.7 %collective-permute-start.14 = (bf16[48,384]{1,0:T(8,128)(2,1)S(1)}, bf16[48,384]{1,0:T(8,128)(2,1)S(1)}, u32[]{:S(2)}, u32[]{:S(2)}) collective-permute-start(bf16[48,384]{1,0:T(8,128)(2,1)S(1)} %fusion.6), channel_id=1, source_target_pairs={{0,8},{1,9},{2,10},{3,11},{4,12},{5,13},{6,14},{7,15},{8,0},{9,1},... | collective-permute-start | bytes 110600 | tf_op jit(solution)/shard_map/ppermute | solution.py:156
  55.4 6.6 %collective-permute-start.13 = (bf16[48,384]{1,0:T(8,128)(2,1)S(1)}, bf16[48,384]{1,0:T(8,128)(2,1)S(1)}, u32[]{:S(2)}, u32[]{:S(2)}) collective-permute-start(bf16[48,384]{1,0:T(8,128)(2,1)S(1)} %fusion.6), channel_id=1, source_target_pairs={{0,4},{1,5},{2,6},{3,7},{4,0},{5,1},{6,2},{7,3},{8,12},{9,13},{10,... | collective-permute-start | bytes 110600 | tf_op jit(solution)/shard_map/ppermute | solution.py:156
  57.6 5.8 %collective-permute-start.7 = (bf16[48,384]{1,0:T(8,128)(2,1)S(1)}, bf16[48,384]{1,0:T(8,128)(2,1)S(1)}, u32[]{:S(2)}, u32[]{:S(2)}) collective-permute-start(bf16[48,384]{1,0:T(8,128)(2,1)S(1)} %fusion.9), channel_id=1, source_target_pairs={{0,12},{1,13},{2,14},{3,15},{4,8},{5,9},{6,10},{7,11},{8,4},{9,5},... | collective-permute-start | bytes 110600 | tf_op jit(solution)/shard_map/ppermute | solution.py:156
  59.9 4.9 %collective-permute-start.6 = (bf16[48,384]{1,0:T(8,128)(2,1)S(1)}, bf16[48,384]{1,0:T(8,128)(2,1)S(1)}, u32[]{:S(2)}, u32[]{:S(2)}) collective-permute-start(bf16[48,384]{1,0:T(8,128)(2,1)S(1)} %fusion.9), channel_id=1, source_target_pairs={{0,8},{1,9},{2,10},{3,11},{4,12},{5,13},{6,14},{7,15},{8,0},{9,1},... | collective-permute-start | bytes 110600 | tf_op jit(solution)/shard_map/ppermute | solution.py:156
  59.9 4.9 %collective-permute-start.5 = (bf16[48,384]{1,0:T(8,128)(2,1)S(1)}, bf16[48,384]{1,0:T(8,128)(2,1)S(1)}, u32[]{:S(2)}, u32[]{:S(2)}) collective-permute-start(bf16[48,384]{1,0:T(8,128)(2,1)S(1)} %fusion.9), channel_id=1, source_target_pairs={{0,4},{1,5},{2,6},{3,7},{4,0},{5,1},{6,2},{7,3},{8,12},{9,13},{10,... | collective-permute-start | bytes 110600 | tf_op jit(solution)/shard_map/ppermute | solution.py:156
  65.6 2.3 %collective-permute-start.17 = (bf16[2,48,384]{2,1,0:T(8,128)(2,1)S(1)}, bf16[2,48,384]{2,1,0:T(8,128)(2,1)S(1)}, u32[]{:S(2)}, u32[]{:S(2)}) collective-permute-start(bf16[2,48,384]{2,1,0:T(8,128)(2,1)S(1)} %pad_maximum_fusion.3), channel_id=1, source_target_pairs={{0,1},{1,0},{2,3},{3,2},{4,5},{5,4},{6,7},{7,6},{8,9},{9,8},{10,11... | collective-permute-start | bytes 221192 | tf_op jit(solution)/shard_map/ppermute | solution.py:156
  65.8 4.9 %collective-permute-start.19 = (bf16[2,48,384]{2,1,0:T(8,128)(2,1)S(1)}, bf16[2,48,384]{2,1,0:T(8,128)(2,1)S(1)}, u32[]{:S(2)}, u32[]{:S(2)}) collective-permute-start(bf16[2,48,384]{2,1,0:T(8,128)(2,1)S(1)} %pad_maximum_fusion.4), channel_id=1, source_target_pairs={{0,2},{1,3},{2,0},{3,1},{4,6},{5,7},{6,4},{7,5},{8,10},{9,11},{10,... | collective-permute-start | bytes 221192 | tf_op jit(solution)/shard_map/ppermute | solution.py:156
  67.7 4.3 %collective-permute-start.20 = (bf16[2,48,384]{2,1,0:T(8,128)(2,1)S(1)}, bf16[2,48,384]{2,1,0:T(8,128)(2,1)S(1)}, u32[]{:S(2)}, u32[]{:S(2)}) collective-permute-start(bf16[2,48,384]{2,1,0:T(8,128)(2,1)S(1)} %pad_maximum_fusion.5), channel_id=1, source_target_pairs={{0,3},{1,2},{2,1},{3,0},{4,7},{5,6},{6,5},{7,4},{8,11},{9,10},{10,... | collective-permute-start | bytes 221192 | tf_op jit(solution)/shard_map/ppermute | solution.py:156

commit v2 on v0

v2 whole, which is shorter than its diff:
```python
import functools
import math

import jax
import jax.numpy as jnp
from jax import lax
from jax.experimental import pallas as pl
from jax.experimental.pallas import tpu as pltpu
from jax.sharding import PartitionSpec as P

BF16 = jnp.bfloat16
F32 = jnp.float32
NT_DIMS = (((1,), (1,)), ((), ()))


def dot_nt(left, right):
    return lax.dot_general(left, right, NT_DIMS, preferred_element_type=F32)


def elemental_kernel(devices, first, momentum, eigvecs, keep, send, vec, arrived):
    count, _, colors, width, sites = vec.shape
    rows = width // 4

    def load(at):
        return pltpu.make_async_copy(eigvecs.at[first + at], vec.at[at], arrived.at[at])

    for at in range(count):
        load(at).start()
    device = lax.axis_index("sink")
    core = jnp.bitwise_and(device, 1)
    chip = jnp.bitwise_and(lax.shift_right_logical(device, 1), 1)
    local = lax.broadcasted_iota(jnp.int32, (1, sites), 1)
    extent = sites // 16
    turn = jnp.mod(momentum[0:1, 0:1] * device, devices).astype(F32) / devices
    second = momentum[0:1, 1:2] * lax.shift_right_logical(local, 4)
    turn = turn + jnp.mod(second, extent).astype(F32) / extent
    third = momentum[0:1, 2:3] * jnp.bitwise_and(local, 15)
    turn = turn + jnp.mod(third, 16).astype(F32) / 16.0
    theta = (2.0 * math.pi) * turn
    cosine = jnp.cos(theta)
    sine = jnp.sin(theta)
    for at in range(count):
        load(at).wait()
        plain = []
        rotated = []
        for color in range(colors):
            low_re = vec[at, 0, color]
            low_im = vec[at, 1, color]
            vec_re = low_re.astype(F32)
            vec_im = low_im.astype(F32)
            rot_re = (cosine * vec_re + sine * vec_im).astype(BF16)
            rot_im = (cosine * vec_im - sine * vec_re).astype(BF16)
            plain.append(jnp.concatenate([low_re, low_im], axis=0))
            rotated.append(jnp.concatenate([rot_re, rot_im], axis=0))
        both = dot_nt(jnp.concatenate(plain, axis=1), jnp.concatenate(rotated, axis=1))
        real = both[:width, :width] + both[width:, width:]
        imag = both[:width, width:] - both[width:, :width]
        total = jnp.concatenate([real, imag], axis=1)
        for side in range(2):

            @pl.when(core == side)
            def _():
                for pair in range(2):
                    slot = jnp.bitwise_xor(chip, pair)
                    mine = (2 * pair + side) * rows
                    other = (2 * pair + 1 - side) * rows
                    keep[slot, at] = total[mine : mine + rows]
                    send[slot, at] = total[other : other + rows].astype(BF16)


def elementals(eigvecs, momentum, devices, first, count):
    _, _, colors, width, sites = eigvecs.shape
    rows = width // 4
    flops = count * 8 * colors * width * width * sites
    return pl.pallas_call(
        functools.partial(elemental_kernel, devices, first),
        in_specs=[pl.BlockSpec(memory_space=pltpu.VMEM), pl.BlockSpec(memory_space=pl.ANY)],
        out_specs=[pl.BlockSpec(memory_space=pltpu.VMEM)] * 2,
        scratch_shapes=[
            pltpu.VMEM((count, 2, colors, width, sites), BF16),
            pltpu.SemaphoreType.DMA((count,)),
        ],
        out_shape=[
            jax.ShapeDtypeStruct((2, count, rows, 2 * width), F32),
            jax.ShapeDtypeStruct((2, count, rows, 2 * width), BF16),
        ],
        compiler_params=pltpu.CompilerParams(vmem_limit_bytes=52 * 1024 * 1024),
        cost_estimate=pl.CostEstimate(
            flops=flops, bytes_accessed=count * 2 * colors * width * sites * 2, transcendentals=0
        ),
        name="partial_elementals",
    )(momentum, eigvecs)


def select_kernel(firsts, relative, *refs):
    wanted = refs[:4]
    blocks = refs[4 : 4 + len(firsts)]
    outs = refs[4 + len(firsts) : 8 + len(firsts)]
    held = refs[-1]
    group = lax.shift_right_logical(lax.axis_index("sink"), 2)
    for block, first in zip(blocks, firsts):
        count = block.shape[0]
        for at in range(count):
            place = jnp.bitwise_xor(first, group) * count + at if relative else first + at
            held[place] = block[at]
    for out, times in zip(outs, wanted):
        for pair in range(out.shape[0]):
            for side in range(2):
                out[pair, side] = held[times[pair, side]]


def select(blocks, firsts, relative, wanted, slices):
    pairs = wanted[0].shape[0]
    _, rows, both = blocks[0].shape
    shape = jax.ShapeDtypeStruct((pairs, 2, rows, both), BF16)
    return pl.pallas_call(
        functools.partial(select_kernel, firsts, relative),
        in_specs=[pl.BlockSpec(memory_space=pltpu.SMEM)] * 4
        + [pl.BlockSpec(memory_space=pltpu.VMEM)] * len(blocks),
        out_specs=[pl.BlockSpec(memory_space=pltpu.VMEM)] * 4,
        scratch_shapes=[pltpu.VMEM((slices, rows, both), BF16)],
        out_shape=[shape] * 4,
        compiler_params=pltpu.CompilerParams(vmem_limit_bytes=8 * 1024 * 1024),
        name="select_slices",
    )(*wanted, *blocks)


def block_kernel(own, by_core, by_pair, by_both, peram, out, sink_el, src_el, left_mat, right_mat):
    width = sink_el.shape[0]
    window = right_mat.shape[1] // 2
    rows = width // 4
    place = jnp.bitwise_and(lax.axis_index("sink"), 3)

    @pl.when(pl.program_id(1) == 0)
    def _():
        for flip, part in enumerate((own, by_core, by_pair, by_both)):
            start = pl.multiple_of(jnp.bitwise_xor(place, flip) * rows, rows)
            sink_el[pl.ds(start, rows), :] = part[0, 0]
            src_el[pl.ds(start, rows), :] = part[0, 1]
        a_re = sink_el[:, :width]
        a_im = sink_el[:, width:]
        left_mat[:width] = jnp.concatenate([a_re, -a_im], axis=1)
        left_mat[width:] = jnp.concatenate([a_im, a_re], axis=1)
        e_re = src_el[:, :width]
        e_im = src_el[:, width:]
        pad = jnp.zeros((width, window - width), BF16)
        hole = jnp.zeros((window - width, 2 * window), BF16)
        even_re = jnp.concatenate([e_re, pad, e_im, pad], axis=1)
        even_im = jnp.concatenate([-e_im, pad, e_re, pad], axis=1)
        odd_re = jnp.concatenate([pad, e_re, pad, e_im], axis=1)
        odd_im = jnp.concatenate([pad, -e_im, pad, e_re], axis=1)
        right_mat[0] = jnp.concatenate([even_re, hole, even_im, hole], axis=0)
        right_mat[1] = jnp.concatenate([hole, odd_re, hole, odd_im], axis=0)

    sign = jnp.where(pl.program_id(1) < 2, 1.0, -1.0)
    stacked = jnp.concatenate([peram[0, 0], peram[0, 1]], axis=0)
    left = jnp.dot(left_mat[...], stacked, preferred_element_type=F32) * sign
    left = left.astype(BF16)
    results = []
    for odd in range(2):
        starts = [b * width - odd * (window - width) for b in (2 + odd, odd)]
        y_re = jnp.concatenate([left[:width, at : at + window] for at in starts], axis=0)
        y_im = jnp.concatenate([left[width:, at : at + window] for at in starts], axis=0)
        results.append(dot_nt(jnp.concatenate([y_re, y_im], axis=1), right_mat[odd]))
    edge = 2 * width - window
    for half in range(2):
        for part in range(2):
            even = results[0][half * width : (half + 1) * width, part * window : (part + 1) * window]
            odd = results[1][half * width : (half + 1) * width, part * window : (part + 1) * window]
            first = 2 * half * width
            out[0, part, :, first : first + edge] = even[:, :edge].astype(BF16)
            middle = even[:, edge:] + odd[:, : window - edge]
            out[0, part, :, first + edge : first + window] = middle.astype(BF16)
            out[0, part, :, first + window : first + 2 * width] = odd[:, window - edge :].astype(BF16)


def pair_blocks(peram, parts):
    pairs, _, full, _ = peram.shape
    width = full // 4
    window = -(-width // 128) * 128
    part_spec = pl.BlockSpec((1, 2, width // 4, 2 * width), lambda p, a: (p, 0, 0, 0))
    return pl.pallas_call(
        block_kernel,
        grid=(pairs, 4),
        in_specs=[part_spec] * 4
        + [pl.BlockSpec((1, 2, width, full), lambda p, a: (p, 0, (a + 2) % 4, 0))],
        out_specs=pl.BlockSpec((1, 2, width, full), lambda p, a: (p, 0, a, 0)),
        scratch_shapes=[
            pltpu.VMEM((width, 2 * width), BF16),
            pltpu.VMEM((width, 2 * width), BF16),
            pltpu.VMEM((2 * width, 2 * width), BF16),
            pltpu.VMEM((2, 2 * window, 2 * window), BF16),
        ],
        out_shape=jax.ShapeDtypeStruct(peram.shape, BF16),
        compiler_params=pltpu.CompilerParams(vmem_limit_bytes=24 * 1024 * 1024),
        cost_estimate=pl.CostEstimate(
            flops=pairs * 16 * full * full * width, bytes_accessed=pairs * 8 * full * full, transcendentals=0
        ),
        name="meson_blocks",
    )(*parts, peram)


def swap(value, flip, devices):
    return lax.ppermute(value, "sink", [(i, i ^ flip) for i in range(devices)])


def sum_near(keep, send, devices):
    over_core = keep + swap(send, 1, devices).astype(F32)
    return over_core[0] + swap(over_core[1].astype(BF16), 2, devices).astype(F32)


def sum_far(near, group, devices):
    count, rows, both = near.shape
    owners = devices // 4
    cut = near.reshape(owners, count * rows // owners, both)
    low = cut.astype(BF16)
    total = lax.dynamic_index_in_dim(cut, group, 0, keepdims=False)
    for flip in range(1, owners):
        piece = lax.dynamic_index_in_dim(low, group ^ flip, 0, keepdims=False)
        total = total + swap(piece, 4 * flip, devices).astype(F32)
    total = total.astype(BF16)
    return [total] + [swap(total, 4 * flip, devices) for flip in range(1, owners)]


def shards(eigvecs, momentum, peram, times):
    devices = lax.axis_size("sink")
    device = lax.axis_index("sink")
    owners = devices // 4
    group = device // 4
    slices, _, _, width, _ = eigvecs.shape
    rows = width // 4
    momentum = momentum.reshape(1, 3)
    core_times = swap(times, 1, devices)
    other = swap(jnp.concatenate([times, core_times]), 2, devices)
    wanted = [times, core_times, other[: times.shape[0]], other[times.shape[0] :]]
    half = slices // 2
    near = []
    for first in (0, half):
        keep, send = elementals(eigvecs, momentum, devices, first, half)
        near.append(sum_near(keep, send, devices))
    shared = sum_far(jnp.concatenate(near), group, devices)
    if slices % owners == 0:
        shared = [block.reshape(-1, rows, 2 * width) for block in shared]
        parts = select(shared, list(range(owners)), True, wanted, slices)
    else:
        shared = jnp.take(jnp.stack(shared), jnp.arange(owners) ^ group, axis=0)
        parts = select([shared.reshape(slices, rows, 2 * width)], [0], False, wanted, slices)
    parts = [parts[0]] + [swap(parts[flip], flip, devices) for flip in range(1, 4)]
    return pair_blocks(peram, parts)


def solution(mesh):
    in_specs = (
        P("groups", None, None, None, "sink"),
        P("groups"),
        P(("groups", "sink"), None, None, None),
        P(("groups", "sink"), None),
    )
    out_specs = P(("groups", "sink"), None, None, None)
    return jax.shard_map(shards, mesh=mesh, in_specs=in_specs, out_specs=out_specs, check_vma=False)
```

time: 136 us -> 54.4 us (0.40)
  blocking collectives: 77 us -> 0 us
  matrix products: 33.3 us -> 0 us
  waiting for transfers between devices: 0 us -> 19.9 us
  starting transfers between devices: 0 us -> 17.5 us
  local copies, waits for them, and re-layouts: 16.9 us -> 0.75 us
  Pallas kernels: 0 us -> 15.6 us
  between operations: 4.72 us -> 0.1 us
  other arithmetic: 3.86 us -> 0.33 us
    psum x1 -> x0, blocking collectives: 77 us -> none  [shards(): totals = lax.psum(partial_sums, 'sink')]
    dot_general x6 -> x0, matrix products: 33.3 us -> none  [the longest x1 7.48 us: shards(): jnp.einsum(form, vec_re, rot_re, preferred_element_type=jnp.float32)]
    ppermute x0 -> x15, waiting for transfers between devices: none -> 19.9 us  [swap(): return lax.ppermute(value, 'sink', [(i, i ^ flip) for i in range(devices)])]
    ppermute x0 -> x15, starting transfers between devices: none -> 17.5 us  [swap(): return lax.ppermute(value, 'sink', [(i, i ^ flip) for i in range(devices)])]
    pallas_call x0 -> x4, Pallas kernels: none -> 15.6 us  [the longest x2 9.96 us: elementals(): pl.pallas_call(functools.partial(elemental_kernel, devices, first), in_sp...]
    slice x7 -> x1, local copies, waits for them, and re-layouts: 8.01 us -> 0.01 us  [shards(): wanted = [times, core_times, other[:times.shape[0]], other[times.shape[0]:]]]
    convert_element_type x2, local copies, waits for them, and re-layouts: 4.86 us -> 0.04 us  [sum_near(): over_core[1].astype(BF16)]
    unnamed x14 -> x6, local copies, waits for them, and re-layouts: 2.67 us -> 0.66 us
  transfers between devices with their start and end apart: 0 -> 15, of which waited for: 0 -> 8; matrix products, arithmetic and copies ran while one was open for 0% -> 1% of each run, Pallas kernels for 0% -> 9%
where the time goes in v2:
time: 54.4 us; the launch traced here: 54.2 us
  waiting for transfers between devices  19.9 us (37%)
  starting transfers between devices  17.5 us (32%)
  Pallas kernels  15.6 us (29%)
  local copies, waits for them, and re-layouts  0.75 us (1%)
    ppermute x15, waiting for transfers between devices, swap(): return lax.ppermute(value, 'sink', [(i, i ^ flip) for i in range(devices)])  19.9 us
    ppermute x15, starting transfers between devices, swap(): return lax.ppermute(value, 'sink', [(i, i ^ flip) for i in range(devices)])  17.5 us
    pallas_call x2, Pallas kernels, elementals(): pl.pallas_call(functools.partial(elemental_kernel, devices, first), in_sp...  9.96 us
    pallas_call x1, Pallas kernels, pair_blocks(): pl.pallas_call(block_kernel, grid=(pairs, 4), in_specs=[part_spec] * 4 +...  5.04 us
  transfers between devices with their start and end apart: 15, of which 8 were waited for; matrix products, arithmetic and copies ran while one was open for 1% of the time, Pallas kernels for 9%

profile of v2, /device:TPU:0, one launch (start us, length us, event | category | flops | bytes accessed | tf_op | source)
XLA Modules:
  0.0 54.2 jit_solution(11112413378651944130)
XLA Ops:
  0.0 0.7 %copy-done = s32[3]{0:T(128)S(1)} copy-done((s32[3]{0:T(128)S(1)}, s32[3]{0:T(128)}, u32[]{:S(2)}) %copy-start) | copy-done | bytes 36
  0.7 5.0 %partial_elementals.3 = (f32[2,4,48,384]{3,2,1,0:T(8,128)S(1)}, bf16[2,4,48,384]{3,2,1,0:T(8,128)(2,1)S(1)}) custom-call(s32[1,3]{1,0:T(1,128)S(1)} %bitcast.38, bf16[8,2,3,192,512]{4,3,2,1,0:T(8,128)(2,1)} %eigvecs.3), custom_call_target="tpu_custom_call" | custom-call | flops 1811939328 | bytes 4718592 | tf_op jit(solution)/shard_map/partial_elementals/pallas_call | solution.py:75
  5.7 0.5 collective-permute-start.4
  6.3 5.0 %partial_elementals.2 = (f32[2,4,48,384]{3,2,1,0:T(8,128)S(1)}, bf16[2,4,48,384]{3,2,1,0:T(8,128)(2,1)S(1)}) custom-call(s32[1,3]{1,0:T(1,128)S(1)} %bitcast.39, bf16[8,2,3,192,512]{4,3,2,1,0:T(8,128)(2,1)} %eigvecs.3), custom_call_target="tpu_custom_call" | custom-call | flops 1811939328 | bytes 4718592 | tf_op jit(solution)/shard_map/partial_elementals/pallas_call | solution.py:75
  11.3 0.5 collective-permute-start.2
  11.9 2.6 %collective-permute-start.5 = (bf16[4,48,384]{2,1,0:T(8,128)(2,1)S(1)}, bf16[4,48,384]{2,1,0:T(8,128)(2,1)S(1)}, u32[]{:S(2)}, u32[]{:S(2)}) collective-permute-start(bf16[4,48,384]{2,1,0:T(8,128)(2,1)S(1)} %fusion.3), channel_id=1, source_target_pairs={{0,2},{1,3},{2,0},{3,1},{4,6},{5,7},{6,4},{7,5},{8,10},{9,11},{10,... | collective-permute-start | bytes 442376 | tf_op jit(solution)/shard_map/ppermute | solution.py:204
  14.6 1.4 %collective-permute-start.3 = (bf16[4,48,384]{2,1,0:T(8,128)(2,1)S(1)}, bf16[4,48,384]{2,1,0:T(8,128)(2,1)S(1)}, u32[]{:S(2)}, u32[]{:S(2)}) collective-permute-start(bf16[4,48,384]{2,1,0:T(8,128)(2,1)S(1)} %fusion.2), channel_id=1, source_target_pairs={{0,2},{1,3},{2,0},{3,1},{4,6},{5,7},{6,4},{7,5},{8,10},{9,11},{10,... | collective-permute-start | bytes 442376 | tf_op jit(solution)/shard_map/ppermute | solution.py:204
  16.0 3.2 %collective-permute-done.5 = bf16[4,48,384]{2,1,0:T(8,128)(2,1)S(1)} collective-permute-done((bf16[4,48,384]{2,1,0:T(8,128)(2,1)S(1)}, bf16[4,48,384]{2,1,0:T(8,128)(2,1)S(1)}, u32[]{:S(2)}, u32[]{:S(2)}) %collective-permute-start.5) | collective-permute-done | bytes 147488 | tf_op jit(solution)/shard_map/ppermute | solution.py:204
  19.2 2.8 %collective-permute-done.3 = bf16[4,48,384]{2,1,0:T(8,128)(2,1)S(1)} collective-permute-done((bf16[4,48,384]{2,1,0:T(8,128)(2,1)S(1)}, bf16[4,48,384]{2,1,0:T(8,128)(2,1)S(1)}, u32[]{:S(2)}, u32[]{:S(2)}) %collective-permute-start.3) | collective-permute-done | bytes 147488 | tf_op jit(solution)/shard_map/ppermute | solution.py:204
  22.2 1.9 %collective-permute-start.6 = (bf16[96,384]{1,0:T(8,128)(2,1)S(1)}, bf16[96,384]{1,0:T(8,128)(2,1)S(1)}, u32[]{:S(2)}, u32[]{:S(2)}) collective-permute-start(bf16[96,384]{1,0:T(8,128)(2,1)S(1)} %get-tuple-element.21), channel_id=1, source_target_pairs={{0,4},{1,5},{2,6},{3,7},{4,0},{5,1},{6,2},{7,3},{8,12},{9,13},{10,... | collective-permute-start | bytes 221192 | tf_op jit(solution)/shard_map/ppermute | solution.py:204
  24.1 2.5 %collective-permute-start.8 = (bf16[96,384]{1,0:T(8,128)(2,1)S(1)}, bf16[96,384]{1,0:T(8,128)(2,1)S(1)}, u32[]{:S(2)}, u32[]{:S(2)}) collective-permute-start(bf16[96,384]{1,0:T(8,128)(2,1)S(1)} %get-tuple-element.22), channel_id=1, source_target_pairs={{0,12},{1,13},{2,14},{3,15},{4,8},{5,9},{6,10},{7,11},{8,4},{9,5},... | collective-permute-start | bytes 221192 | tf_op jit(solution)/shard_map/ppermute | solution.py:204
  26.7 1.6 %collective-permute-start.1 = (s32[2,2]{1,0:T(2,128)S(1)}, s32[2,2]{1,0:T(2,128)S(1)}, u32[]{:S(2)}, u32[]{:S(2)}) collective-permute-start(s32[2,2]{1,0:T(2,128)S(1)} %pad_add_fusion), channel_id=1, source_target_pairs={{0,2},{1,3},{2,0},{3,1},{4,6},{5,7},{6,4},{7,5},{8,10},{9,11},{10,... | collective-permute-start | bytes 56 | tf_op jit(solution)/shard_map/ppermute | solution.py:204
  28.3 2.8 %collective-permute-done.8 = bf16[96,384]{1,0:T(8,128)(2,1)S(1)} collective-permute-done((bf16[96,384]{1,0:T(8,128)(2,1)S(1)}, bf16[96,384]{1,0:T(8,128)(2,1)S(1)}, u32[]{:S(2)}, u32[]{:S(2)}) %collective-permute-start.8) | collective-permute-done | bytes 73760 | tf_op jit(solution)/shard_map/ppermute | solution.py:204
  31.1 2.4 %collective-permute-done.7 = bf16[96,384]{1,0:T(8,128)(2,1)S(1)} collective-permute-done((bf16[96,384]{1,0:T(8,128)(2,1)S(1)}, bf16[96,384]{1,0:T(8,128)(2,1)S(1)}, u32[]{:S(2)}, u32[]{:S(2)}) %collective-permute-start.7) | collective-permute-done | bytes 73760 | tf_op jit(solution)/shard_map/ppermute | solution.py:204
  33.5 2.6 %collective-permute-start.11 = (bf16[96,384]{1,0:T(8,128)(2,1)S(1)}, bf16[96,384]{1,0:T(8,128)(2,1)S(1)}, u32[]{:S(2)}, u32[]{:S(2)}) collective-permute-start(bf16[96,384]{1,0:T(8,128)(2,1)S(1)} %fusion.6), channel_id=1, source_target_pairs={{0,12},{1,13},{2,14},{3,15},{4,8},{5,9},{6,10},{7,11},{8,4},{9,5},... | collective-permute-start | bytes 221192 | tf_op jit(solution)/shard_map/ppermute | solution.py:204
  36.0 1.9 %collective-permute-start.9 = (bf16[96,384]{1,0:T(8,128)(2,1)S(1)}, bf16[96,384]{1,0:T(8,128)(2,1)S(1)}, u32[]{:S(2)}, u32[]{:S(2)}) collective-permute-start(bf16[96,384]{1,0:T(8,128)(2,1)S(1)} %fusion.6), channel_id=1, source_target_pairs={{0,4},{1,5},{2,6},{3,7},{4,0},{5,1},{6,2},{7,3},{8,12},{9,13},{10,... | collective-permute-start | bytes 221192 | tf_op jit(solution)/shard_map/ppermute | solution.py:204
  37.9 2.6 %collective-permute-done.11 = bf16[96,384]{1,0:T(8,128)(2,1)S(1)} collective-permute-done((bf16[96,384]{1,0:T(8,128)(2,1)S(1)}, bf16[96,384]{1,0:T(8,128)(2,1)S(1)}, u32[]{:S(2)}, u32[]{:S(2)}) %collective-permute-start.11) | collective-permute-done | bytes 73760 | tf_op jit(solution)/shard_map/ppermute | solution.py:204
  40.5 2.0 %collective-permute-done.10 = bf16[96,384]{1,0:T(8,128)(2,1)S(1)} collective-permute-done((bf16[96,384]{1,0:T(8,128)(2,1)S(1)}, bf16[96,384]{1,0:T(8,128)(2,1)S(1)}, u32[]{:S(2)}, u32[]{:S(2)}) %collective-permute-start.10) | collective-permute-done | bytes 73760 | tf_op jit(solution)/shard_map/ppermute | solution.py:204
  42.5 0.6 %select_slices.1 = (bf16[1,2,48,384]{3,2,1,0:T(8,128)(2,1)S(1)}, bf16[1,2,48,384]{3,2,1,0:T(8,128)(2,1)S(1)}, bf16[1,2,48,384]{3,2,1,0:T(8,128)(2,1)S(1)}, bf16[1,2,48,384]{3,2,1,0:T(8,128)(2,1)S(1)}) custom-call(s32[1,2]{1,0:T(1,128)S(1)} %copy-done.1, s32[1,2]{1,0:T(1,128)S(1)} %collective-permute-done.refs_1_, s32[1,2]{1,0:T(1,128)S(1)} %get-tuple-element.25.refs_2_, ...), custom_call_target="tpu_custom_call" | custom-call | tf_op jit(solution)/shard_map/select_slices/pallas_call | solution.py:116
  43.2 1.4 %collective-permute-start.13 = (bf16[1,2,48,384]{3,2,1,0:T(8,128)(2,1)S(1)}, bf16[1,2,48,384]{3,2,1,0:T(8,128)(2,1)S(1)}, u32[]{:S(2)}, u32[]{:S(2)}) collective-permute-start(bf16[1,2,48,384]{3,2,1,0:T(8,128)(2,1)S(1)} %get-tuple-element.19), channel_id=1, source_target_pairs={{0,2},{1,3},{2,0},{3,1},{4,6},{5,7},{6,4},{7,5},{8,10},{9,11},{10,... | collective-permute-start | bytes 221192 | tf_op jit(solution)/shard_map/ppermute | solution.py:204
  44.6 0.4 collective-permute-start.14
  45.1 3.1 %collective-permute-done.13.by_pair = bf16[1,2,48,384]{3,2,1,0:T(8,128)(2,1)S(1)} collective-permute-done((bf16[1,2,48,384]{3,2,1,0:T(8,128)(2,1)S(1)}, bf16[1,2,48,384]{3,2,1,0:T(8,128)(2,1)S(1)}, u32[]{:S(2)}, u32[]{:S(2)}) %collective-permute-start.13) | collective-permute-done | bytes 73760 | tf_op jit(solution)/shard_map/ppermute | solution.py:204
  48.2 1.0 %collective-permute-done.14.by_both = bf16[1,2,48,384]{3,2,1,0:T(8,128)(2,1)S(1)} collective-permute-done((bf16[1,2,48,384]{3,2,1,0:T(8,128)(2,1)S(1)}, bf16[1,2,48,384]{3,2,1,0:T(8,128)(2,1)S(1)}, u32[]{:S(2)}, u32[]{:S(2)}) %collective-permute-start.14) | collective-permute-done | bytes 73760 | tf_op jit(solution)/shard_map/ppermute | solution.py:204
  49.2 5.0 %meson_blocks.1 = bf16[1,2,768,768]{3,2,1,0:T(8,128)(2,1)} custom-call(bf16[1,2,48,384]{3,2,1,0:T(8,128)(2,1)S(1)} %get-tuple-element.17.own, bf16[1,2,48,384]{3,2,1,0:T(8,128)(2,1)S(1)} %collective-permute-done.12.by_core, bf16[1,2,48,384]{3,2,1,0:T(8,128)(2,1)S(1)} %collective-permute-done.13.by_pair, ...), custom_call_target="tpu_custom_call" | custom-call | flops 1811939328 | bytes 4718592 | tf_op jit(solution)/shard_map/meson_blocks/pallas_call | solution.py:182
  (28 shorter events, 0.7 us)
Async XLA Ops:
  0.0 0.7 %copy-start = (s32[3]{0:T(128)S(1)}, s32[3]{0:T(128)}, u32[]{:S(2)}) copy-start(s32[3]{0:T(128)} %param.5) | copy-start | bytes 40
  0.7 5.5 %copy-start.1 = (s32[1,2]{1,0:T(1,128)S(1)}, s32[1,2]{1,0:T(1,128)}, u32[]{:S(2)}) copy-start(s32[1,2]{1,0:T(1,128)} %refs_0_.1) | copy-start | bytes 28
  5.7 6.1 %collective-permute-start.4 = (bf16[2,4,48,384]{3,2,1,0:T(8,128)(2,1)S(1)}, bf16[2,4,48,384]{3,2,1,0:T(8,128)(2,1)S(1)}, u32[]{:S(2)}, u32[]{:S(2)}) collective-permute-start(bf16[2,4,48,384]{3,2,1,0:T(8,128)(2,1)S(1)} %get-tuple-element.16), channel_id=1, source_target_pairs={{0,1},{1,0},{2,3},{3,2},{4,5},{5,4},{6,7},{7,6},{8,9},{9,8},{10,11... | collective-permute-start | bytes 884744 | tf_op jit(solution)/shard_map/ppermute | solution.py:204
  6.2 20.5 %collective-permute-start = (s32[1,2]{1,0:T(1,128)S(1)}, s32[1,2]{1,0:T(1,128)S(1)}, u32[]{:S(2)}, u32[]{:S(2)}) collective-permute-start(s32[1,2]{1,0:T(1,128)S(1)} %copy-done.1), channel_id=1, source_target_pairs={{0,1},{1,0},{2,3},{3,2},{4,5},{5,4},{6,7},{7,6},{8,9},{9,8},{10,11... | collective-permute-start | bytes 32 | tf_op jit(solution)/shard_map/ppermute | solution.py:204
  11.3 3.2 %collective-permute-start.2 = (bf16[2,4,48,384]{3,2,1,0:T(8,128)(2,1)S(1)}, bf16[2,4,48,384]{3,2,1,0:T(8,128)(2,1)S(1)}, u32[]{:S(2)}, u32[]{:S(2)}) collective-permute-start(bf16[2,4,48,384]{3,2,1,0:T(8,128)(2,1)S(1)} %get-tuple-element.14), channel_id=1, source_target_pairs={{0,1},{1,0},{2,3},{3,2},{4,5},{5,4},{6,7},{7,6},{8,9},{9,8},{10,11... | collective-permute-start | bytes 884744 | tf_op jit(solution)/shard_map/ppermute | solution.py:204
  11.9 7.3 %collective-permute-start.5 = (bf16[4,48,384]{2,1,0:T(8,128)(2,1)S(1)}, bf16[4,48,384]{2,1,0:T(8,128)(2,1)S(1)}, u32[]{:S(2)}, u32[]{:S(2)}) collective-permute-start(bf16[4,48,384]{2,1,0:T(8,128)(2,1)S(1)} %fusion.3), channel_id=1, source_target_pairs={{0,2},{1,3},{2,0},{3,1},{4,6},{5,7},{6,4},{7,5},{8,10},{9,11},{10,... | collective-permute-start | bytes 442376 | tf_op jit(solution)/shard_map/ppermute | solution.py:204
  14.6 34.6 %copy-start.2 = (bf16[1,2,768,768]{3,2,1,0:T(8,128)(2,1)S(1)}, bf16[1,2,768,768]{3,2,1,0:T(8,128)(2,1)}, u32[]{:S(2)}) copy-start(bf16[1,2,768,768]{3,2,1,0:T(8,128)(2,1)} %peram.1) | copy-start | bytes 7077892
  14.6 7.5 %collective-permute-start.3 = (bf16[4,48,384]{2,1,0:T(8,128)(2,1)S(1)}, bf16[4,48,384]{2,1,0:T(8,128)(2,1)S(1)}, u32[]{:S(2)}, u32[]{:S(2)}) collective-permute-start(bf16[4,48,384]{2,1,0:T(8,128)(2,1)S(1)} %fusion.2), channel_id=1, source_target_pairs={{0,2},{1,3},{2,0},{3,1},{4,6},{5,7},{6,4},{7,5},{8,10},{9,11},{10,... | collective-permute-start | bytes 442376 | tf_op jit(solution)/shard_map/ppermute | solution.py:204
  22.2 6.1 %collective-permute-start.6 = (bf16[96,384]{1,0:T(8,128)(2,1)S(1)}, bf16[96,384]{1,0:T(8,128)(2,1)S(1)}, u32[]{:S(2)}, u32[]{:S(2)}) collective-permute-start(bf16[96,384]{1,0:T(8,128)(2,1)S(1)} %get-tuple-element.21), channel_id=1, source_target_pairs={{0,4},{1,5},{2,6},{3,7},{4,0},{5,1},{6,2},{7,3},{8,12},{9,13},{10,... | collective-permute-start | bytes 221192 | tf_op jit(solution)/shard_map/ppermute | solution.py:204
  24.1 6.9 %collective-permute-start.8 = (bf16[96,384]{1,0:T(8,128)(2,1)S(1)}, bf16[96,384]{1,0:T(8,128)(2,1)S(1)}, u32[]{:S(2)}, u32[]{:S(2)}) collective-permute-start(bf16[96,384]{1,0:T(8,128)(2,1)S(1)} %get-tuple-element.22), channel_id=1, source_target_pairs={{0,12},{1,13},{2,14},{3,15},{4,8},{5,9},{6,10},{7,11},{8,4},{9,5},... | collective-permute-start | bytes 221192 | tf_op jit(solution)/shard_map/ppermute | solution.py:204
  26.6 6.8 %collective-permute-start.7 = (bf16[96,384]{1,0:T(8,128)(2,1)S(1)}, bf16[96,384]{1,0:T(8,128)(2,1)S(1)}, u32[]{:S(2)}, u32[]{:S(2)}) collective-permute-start(bf16[96,384]{1,0:T(8,128)(2,1)S(1)} %get-tuple-element.23), channel_id=1, source_target_pairs={{0,8},{1,9},{2,10},{3,11},{4,12},{5,13},{6,14},{7,15},{8,0},{9,1},... | collective-permute-start | bytes 221192 | tf_op jit(solution)/shard_map/ppermute | solution.py:204
  26.7 11.2 %collective-permute-start.1 = (s32[2,2]{1,0:T(2,128)S(1)}, s32[2,2]{1,0:T(2,128)S(1)}, u32[]{:S(2)}, u32[]{:S(2)}) collective-permute-start(s32[2,2]{1,0:T(2,128)S(1)} %pad_add_fusion), channel_id=1, source_target_pairs={{0,2},{1,3},{2,0},{3,1},{4,6},{5,7},{6,4},{7,5},{8,10},{9,11},{10,... | collective-permute-start | bytes 56 | tf_op jit(solution)/shard_map/ppermute | solution.py:204
  33.5 7.1 %collective-permute-start.11 = (bf16[96,384]{1,0:T(8,128)(2,1)S(1)}, bf16[96,384]{1,0:T(8,128)(2,1)S(1)}, u32[]{:S(2)}, u32[]{:S(2)}) collective-permute-start(bf16[96,384]{1,0:T(8,128)(2,1)S(1)} %fusion.6), channel_id=1, source_target_pairs={{0,12},{1,13},{2,14},{3,15},{4,8},{5,9},{6,10},{7,11},{8,4},{9,5},... | collective-permute-start | bytes 221192 | tf_op jit(solution)/shard_map/ppermute | solution.py:204
  36.0 6.5 %collective-permute-start.10 = (bf16[96,384]{1,0:T(8,128)(2,1)S(1)}, bf16[96,384]{1,0:T(8,128)(2,1)S(1)}, u32[]{:S(2)}, u32[]{:S(2)}) collective-permute-start(bf16[96,384]{1,0:T(8,128)(2,1)S(1)} %fusion.6), channel_id=1, source_target_pairs={{0,8},{1,9},{2,10},{3,11},{4,12},{5,13},{6,14},{7,15},{8,0},{9,1},... | collective-permute-start | bytes 221192 | tf_op jit(solution)/shard_map/ppermute | solution.py:204
  36.0 6.5 %collective-permute-start.9 = (bf16[96,384]{1,0:T(8,128)(2,1)S(1)}, bf16[96,384]{1,0:T(8,128)(2,1)S(1)}, u32[]{:S(2)}, u32[]{:S(2)}) collective-permute-start(bf16[96,384]{1,0:T(8,128)(2,1)S(1)} %fusion.6), channel_id=1, source_target_pairs={{0,4},{1,5},{2,6},{3,7},{4,0},{5,1},{6,2},{7,3},{8,12},{9,13},{10,... | collective-permute-start | bytes 221192 | tf_op jit(solution)/shard_map/ppermute | solution.py:204
  43.1 1.9 %collective-permute-start.12 = (bf16[1,2,48,384]{3,2,1,0:T(8,128)(2,1)S(1)}, bf16[1,2,48,384]{3,2,1,0:T(8,128)(2,1)S(1)}, u32[]{:S(2)}, u32[]{:S(2)}) collective-permute-start(bf16[1,2,48,384]{3,2,1,0:T(8,128)(2,1)S(1)} %get-tuple-element.18), channel_id=1, source_target_pairs={{0,1},{1,0},{2,3},{3,2},{4,5},{5,4},{6,7},{7,6},{8,9},{9,8},{10,11... | collective-permute-start | bytes 221192 | tf_op jit(solution)/shard_map/ppermute | solution.py:204
  43.2 5.0 %collective-permute-start.13 = (bf16[1,2,48,384]{3,2,1,0:T(8,128)(2,1)S(1)}, bf16[1,2,48,384]{3,2,1,0:T(8,128)(2,1)S(1)}, u32[]{:S(2)}, u32[]{:S(2)}) collective-permute-start(bf16[1,2,48,384]{3,2,1,0:T(8,128)(2,1)S(1)} %get-tuple-element.19), channel_id=1, source_target_pairs={{0,2},{1,3},{2,0},{3,1},{4,6},{5,7},{6,4},{7,5},{8,10},{9,11},{10,... | collective-permute-start | bytes 221192 | tf_op jit(solution)/shard_map/ppermute | solution.py:204
  44.6 4.5 %collective-permute-start.14 = (bf16[1,2,48,384]{3,2,1,0:T(8,128)(2,1)S(1)}, bf16[1,2,48,384]{3,2,1,0:T(8,128)(2,1)S(1)}, u32[]{:S(2)}, u32[]{:S(2)}) collective-permute-start(bf16[1,2,48,384]{3,2,1,0:T(8,128)(2,1)S(1)} %get-tuple-element.20), channel_id=1, source_target_pairs={{0,3},{1,2},{2,1},{3,0},{4,7},{5,6},{6,5},{7,4},{8,11},{9,10},{10,... | collective-permute-start | bytes 221192 | tf_op jit(solution)/shard_map/ppermute | solution.py:204

commit v3 on v2

--- a/solution.py
+++ b/solution.py
@@ -11,13 +11,15 @@
 BF16 = jnp.bfloat16
 F32 = jnp.float32
 NT_DIMS = (((1,), (1,)), ((), ()))
+CHUNKS = ((1, 3), (1, 3))
 
 
 def dot_nt(left, right):
     return lax.dot_general(left, right, NT_DIMS, preferred_element_type=F32)
 
 
-def elemental_kernel(devices, first, momentum, eigvecs, keep, send, vec, arrived):
+def elemental_kernel(devices, first, arrivals, momentum, eigvecs, before, keep, send, vec, total, arrived):
+    del before
     count, _, colors, width, sites = vec.shape
     rows = width // 4
 
@@ -39,8 +41,11 @@
     theta = (2.0 * math.pi) * turn
     cosine = jnp.cos(theta)
     sine = jnp.sin(theta)
+    waits = [start for start, many in arrivals for _ in range(many)]
     for at in range(count):
-        load(at).wait()
+        for late in range(at, count):
+            if waits[late] == at:
+                load(late).wait()
         plain = []
         rotated = []
         for color in range(colors):
@@ -55,66 +60,71 @@
         both = dot_nt(jnp.concatenate(plain, axis=1), jnp.concatenate(rotated, axis=1))
         real = both[:width, :width] + both[width:, width:]
         imag = both[:width, width:] - both[width:, :width]
-        total = jnp.concatenate([real, imag], axis=1)
-        for side in range(2):
-
-            @pl.when(core == side)
-            def _():
+        total[at] = jnp.concatenate([real, imag], axis=1)
+    for side in range(2):
+
+        @pl.when(core == side)
+        def _():
+            for at in range(count):
                 for pair in range(2):
                     slot = jnp.bitwise_xor(chip, pair)
                     mine = (2 * pair + side) * rows
                     other = (2 * pair + 1 - side) * rows
-                    keep[slot, at] = total[mine : mine + rows]
-                    send[slot, at] = total[other : other + rows].astype(BF16)
-
-
-def elementals(eigvecs, momentum, devices, first, count):
+                    keep[slot, at] = total[at, mine : mine + rows]
+                    send[slot, at] = total[at, other : other + rows].astype(BF16)
+
+
+def elementals(eigvecs, momentum, first, arrivals, before, devices):
     _, _, colors, width, sites = eigvecs.shape
     rows = width // 4
-    flops = count * 8 * colors * width * width * sites
+    count = sum(arrivals)
+    arrivals = [(sum(arrivals[:at]), many) for at, many in enumerate(arrivals)]
     return pl.pallas_call(
-        functools.partial(elemental_kernel, devices, first),
-        in_specs=[pl.BlockSpec(memory_space=pltpu.VMEM), pl.BlockSpec(memory_space=pl.ANY)],
+        functools.partial(elemental_kernel, devices, first, arrivals),
+        in_specs=[pl.BlockSpec(memory_space=pltpu.VMEM)] + [pl.BlockSpec(memory_space=pl.ANY)] * 2,
         out_specs=[pl.BlockSpec(memory_space=pltpu.VMEM)] * 2,
         scratch_shapes=[
             pltpu.VMEM((count, 2, colors, width, sites), BF16),
+            pltpu.VMEM((count, width, 2 * width), F32),
             pltpu.SemaphoreType.DMA((count,)),
         ],
         out_shape=[
             jax.ShapeDtypeStruct((2, count, rows, 2 * width), F32),
             jax.ShapeDtypeStruct((2, count, rows, 2 * width), BF16),
         ],
-        compiler_params=pltpu.CompilerParams(vmem_limit_bytes=52 * 1024 * 1024),
+        compiler_params=pltpu.CompilerParams(vmem_limit_bytes=50 * 1024 * 1024),
         cost_estimate=pl.CostEstimate(
-            flops=flops, bytes_accessed=count * 2 * colors * width * sites * 2, transcendentals=0
+            flops=count * 8 * colors * width * width * sites,
+            bytes_accessed=count * 2 * colors * width * sites * 2,
+            transcendentals=0,
         ),
         name="partial_elementals",
-    )(momentum, eigvecs)
-
-
-def select_kernel(firsts, relative, *refs):
+    )(momentum, eigvecs, before)
+
+
+def select_kernel(places, owners, *refs):
     wanted = refs[:4]
-    blocks = refs[4 : 4 + len(firsts)]
-    outs = refs[4 + len(firsts) : 8 + len(firsts)]
+    blocks = refs[4 : 4 + len(places)]
+    outs = refs[4 + len(places) : 8 + len(places)]
     held = refs[-1]
-    group = lax.shift_right_logical(lax.axis_index("sink"), 2)
-    for block, first in zip(blocks, firsts):
+    group = jnp.bitwise_and(lax.shift_right_logical(lax.axis_index("sink"), 2), owners - 1)
+    for block, (first, flip) in zip(blocks, places):
         count = block.shape[0]
         for at in range(count):
-            place = jnp.bitwise_xor(first, group) * count + at if relative else first + at
-            held[place] = block[at]
+            start = first if flip is None else first + jnp.bitwise_xor(group, flip) * count
+            held[start + at] = block[at]
     for out, times in zip(outs, wanted):
         for pair in range(out.shape[0]):
             for side in range(2):
                 out[pair, side] = held[times[pair, side]]
 
 
-def select(blocks, firsts, relative, wanted, slices):
+def select(blocks, places, owners, wanted, slices):
     pairs = wanted[0].shape[0]
     _, rows, both = blocks[0].shape
     shape = jax.ShapeDtypeStruct((pairs, 2, rows, both), BF16)
     return pl.pallas_call(
-        functools.partial(select_kernel, firsts, relative),
+        functools.partial(select_kernel, places, owners),
         in_specs=[pl.BlockSpec(memory_space=pltpu.SMEM)] * 4
         + [pl.BlockSpec(memory_space=pltpu.VMEM)] * len(blocks),
         out_specs=[pl.BlockSpec(memory_space=pltpu.VMEM)] * 4,
@@ -206,45 +216,62 @@
 
 def sum_near(keep, send, devices):
     over_core = keep + swap(send, 1, devices).astype(F32)
-    return over_core[0] + swap(over_core[1].astype(BF16), 2, devices).astype(F32)
-
-
-def sum_far(near, group, devices):
-    count, rows, both = near.shape
-    owners = devices // 4
-    cut = near.reshape(owners, count * rows // owners, both)
-    low = cut.astype(BF16)
-    total = lax.dynamic_index_in_dim(cut, group, 0, keepdims=False)
-    for flip in range(1, owners):
-        piece = lax.dynamic_index_in_dim(low, group ^ flip, 0, keepdims=False)
-        total = total + swap(piece, 4 * flip, devices).astype(F32)
-    total = total.astype(BF16)
-    return [total] + [swap(total, 4 * flip, devices) for flip in range(1, owners)]
+    given = over_core[1].astype(BF16)
+    return over_core[0] + swap(given, 2, devices).astype(F32), given
+
+
+def sum_far(near, flip, group, devices):
+    half = near.shape[0] // 2
+    if 8 * flip == devices:
+        return [(near + swap(near.astype(BF16), 4 * flip, devices).astype(F32)).astype(BF16)]
+    cut = near.reshape(2, half, near.shape[1])
+    bit = jnp.bitwise_and(lax.shift_right_logical(group, flip.bit_length() - 1), 1)
+    kept = lax.dynamic_index_in_dim(cut, bit, 0, keepdims=False)
+    given = lax.dynamic_index_in_dim(cut, 1 - bit, 0, keepdims=False).astype(BF16)
+    kept = kept + swap(given, 4 * flip, devices).astype(F32)
+    blocks = sum_far(kept, 2 * flip, group, devices)
+    low = blocks[0] if len(blocks) == 1 else jnp.concatenate(blocks)
+    other = swap(low, 4 * flip, devices)
+    return blocks + [other[at * blocks[0].shape[0] : (at + 1) * blocks[0].shape[0]] for at in range(len(blocks))]
 
 
 def shards(eigvecs, momentum, peram, times):
     devices = lax.axis_size("sink")
-    device = lax.axis_index("sink")
-    owners = devices // 4
-    group = device // 4
+    group = lax.shift_right_logical(lax.axis_index("sink"), 2)
+    owners = devices // 8
     slices, _, _, width, _ = eigvecs.shape
     rows = width // 4
     momentum = momentum.reshape(1, 3)
-    core_times = swap(times, 1, devices)
-    other = swap(jnp.concatenate([times, core_times]), 2, devices)
+    blocks = []
+    places = []
+    first = 0
+    before = momentum
+    nears = []
+    for chunk in CHUNKS:
+        arrivals = [part * slices // 8 for part in chunk]
+        keep, send = elementals(eigvecs, momentum, first, arrivals, before, devices)
+        if nears:
+            send, nears[-1] = lax.optimization_barrier((send, nears[-1]))
+        near, before = sum_near(keep, send, devices)
+        nears.append(near)
+        first += sum(arrivals)
+    late_times, nears[-1] = lax.optimization_barrier((times, nears[-1]))
+    core_times = swap(late_times, 1, devices)
+    other = swap(jnp.concatenate([late_times, core_times]), 2, devices)
     wanted = [times, core_times, other[: times.shape[0]], other[times.shape[0] :]]
-    half = slices // 2
-    near = []
-    for first in (0, half):
-        keep, send = elementals(eigvecs, momentum, devices, first, half)
-        near.append(sum_near(keep, send, devices))
-    shared = sum_far(jnp.concatenate(near), group, devices)
-    if slices % owners == 0:
-        shared = [block.reshape(-1, rows, 2 * width) for block in shared]
-        parts = select(shared, list(range(owners)), True, wanted, slices)
-    else:
-        shared = jnp.take(jnp.stack(shared), jnp.arange(owners) ^ group, axis=0)
-        parts = select([shared.reshape(slices, rows, 2 * width)], [0], False, wanted, slices)
+    first = 0
+    for near in nears:
+        count = near.shape[0]
+        shared = sum_far(near.reshape(-1, 2 * width), 1, group, devices)
+        if count % owners == 0:
+            blocks += [block.reshape(-1, rows, 2 * width) for block in shared]
+            places += [(first, flip) for flip in range(owners)]
+        else:
+            shared = jnp.take(jnp.stack(shared), jnp.arange(owners) ^ (group & (owners - 1)), axis=0)
+            blocks.append(shared.reshape(count, rows, 2 * width))
+            places.append((first, None))
+        first += count
+    parts = select(blocks, places, owners, wanted, slices)
     parts = [parts[0]] + [swap(parts[flip], flip, devices) for flip in range(1, 4)]
     return pair_blocks(peram, parts)
 

time: 54.4 us -> 50.1 us (0.921)
  waiting for transfers between devices: 19.9 us -> 14.8 us
  other arithmetic: 0.33 us -> 1.21 us
  starting transfers between devices: 17.5 us -> 18.3 us
  Pallas kernels: 15.6 us -> 14.8 us
    ppermute x15, waiting for transfers between devices: 19.9 us -> 14.8 us  [swap(): return lax.ppermute(value, 'sink', [(i, i ^ flip) for i in range(devices)])]
    add x2, other arithmetic: 0.14 us -> 1.06 us  [sum_near(): over_core = keep + swap(send, 1, devices).astype(F32)]
    pallas_call x3, Pallas kernels: 10.6 us -> 9.78 us  [the longest x2 9.15 us: elementals(): pl.pallas_call(functools.partial(elemental_kernel, devices, first, arriva...]
    ppermute x15, starting transfers between devices: 17.5 us -> 18.3 us  [swap(): return lax.ppermute(value, 'sink', [(i, i ^ flip) for i in range(devices)])]
  transfers between devices with their start and end apart: 15 -> 15, of which waited for: 8 -> 9; matrix products, arithmetic and copies ran while one was open for 1% -> 2% of each run, Pallas kernels for 9% -> 9%
where the time goes in v3:
time: 50.1 us; the launch traced here: 50 us
  starting transfers between devices  18.3 us (37%)
  Pallas kernels  14.8 us (30%)
  waiting for transfers between devices  14.8 us (30%)
  other arithmetic  1.21 us (2%)
  local copies, waits for them, and re-layouts  0.75 us (1%)
    ppermute x15, starting transfers between devices, swap(): return lax.ppermute(value, 'sink', [(i, i ^ flip) for i in range(devices)])  18.3 us
    ppermute x15, waiting for transfers between devices, swap(): return lax.ppermute(value, 'sink', [(i, i ^ flip) for i in range(devices)])  14.8 us
    pallas_call x2, Pallas kernels, elementals(): pl.pallas_call(functools.partial(elemental_kernel, devices, first, arriva...  9.15 us
    pallas_call x1, Pallas kernels, pair_blocks(): pl.pallas_call(block_kernel, grid=(pairs, 4), in_specs=[part_spec] * 4 +...  5.04 us
    add x2, other arithmetic, sum_near(): over_core = keep + swap(send, 1, devices).astype(F32)  1.06 us
  transfers between devices with their start and end apart: 15, of which 9 were waited for; matrix products, arithmetic and copies ran while one was open for 2% of the time, Pallas kernels for 9%

profile of v3, /device:TPU:0, one launch (start us, length us, event | category | flops | bytes accessed | tf_op | source)
XLA Modules:
  0.0 50.0 jit_solution(13546131240523932601)
XLA Ops:
  0.0 0.7 %copy-done = s32[3]{0:T(128)S(1)} copy-done((s32[3]{0:T(128)S(1)}, s32[3]{0:T(128)}, u32[]{:S(2)}) %copy-start) | copy-done | bytes 36
  0.7 4.6 %partial_elementals.2 = (f32[2,4,48,384]{3,2,1,0:T(8,128)S(1)}, bf16[2,4,48,384]{3,2,1,0:T(8,128)(2,1)S(1)}) custom-call(s32[1,3]{1,0:T(1,128)S(1)} %bitcast.39, bf16[8,2,3,192,512]{4,3,2,1,0:T(8,128)(2,1)} %eigvecs.3, s32[1,3]{1,0:T(1,128)S(1)} %bitcast.40), custom_call_target="tpu_custom_call" | custom-call | flops 1811939328 | bytes 4718592 | tf_op jit(solution)/shard_map/partial_elementals/pallas_call | solution.py:82
  5.8 1.2 %collective-permute-done = bf16[2,4,48,384]{3,2,1,0:T(8,128)(2,1)S(1)} collective-permute-done((bf16[2,4,48,384]{3,2,1,0:T(8,128)(2,1)S(1)}, bf16[2,4,48,384]{3,2,1,0:T(8,128)(2,1)S(1)}, u32[]{:S(2)}, u32[]{:S(2)}) %collective-permute-start) | collective-permute-done | bytes 294944 | tf_op jit(solution)/shard_map/ppermute | solution.py:214
  7.1 2.9 %collective-permute-start.1 = (bf16[4,48,384]{2,1,0:T(8,128)(2,1)S(1)}, bf16[4,48,384]{2,1,0:T(8,128)(2,1)S(1)}, u32[]{:S(2)}, u32[]{:S(2)}) collective-permute-start(bf16[4,48,384]{2,1,0:T(8,128)(2,1)S(1)} %fusion.2.before), channel_id=1, source_target_pairs={{0,2},{1,3},{2,0},{3,1},{4,6},{5,7},{6,4},{7,5},{8,10},{9,11},{10,... | collective-permute-start | bytes 442376 | tf_op jit(solution)/shard_map/ppermute | solution.py:214
  10.0 4.6 %partial_elementals.3 = (f32[2,4,48,384]{3,2,1,0:T(8,128)S(1)}, bf16[2,4,48,384]{3,2,1,0:T(8,128)(2,1)S(1)}) custom-call(s32[1,3]{1,0:T(1,128)S(1)} %bitcast.41, bf16[8,2,3,192,512]{4,3,2,1,0:T(8,128)(2,1)} %eigvecs.3, bf16[4,48,384]{2,1,0:T(8,128)(2,1)S(1)} %fusion.2.before), custom_call_target="tpu_custom_call" | custom-call | flops 1811939328 | bytes 4718592 | tf_op jit(solution)/shard_map/partial_elementals/pallas_call | solution.py:82
  14.7 1.6 %collective-permute-start.6 = (bf16[96,384]{1,0:T(8,128)(2,1)S(1)}, bf16[96,384]{1,0:T(8,128)(2,1)S(1)}, u32[]{:S(2)}, u32[]{:S(2)}) collective-permute-start(bf16[96,384]{1,0:T(8,128)(2,1)S(1)} %fusion.6), channel_id=1, source_target_pairs={{0,4},{1,5},{2,6},{3,7},{4,0},{5,1},{6,2},{7,3},{8,12},{9,13},{10,... | collective-permute-start | bytes 221192 | tf_op jit(solution)/shard_map/ppermute | solution.py:214
  16.4 1.0 %convert_add_fusion = f32[2,4,48,384]{3,2,1,0:T(8,128)S(1)} fusion(f32[2,4,48,384]{3,2,1,0:T(8,128)S(1)} %get-tuple-element.19, bf16[2,4,48,384]{3,2,1,0:T(8,128)(2,1)} %collective-permute-done.2), kind=kLoop, calls=%fused_computation | loop fusion | flops 294912 | bytes 1474560 | tf_op jit(solution)/shard_map/add | solution.py:218
  17.5 1.3 %collective-permute-start.3 = (bf16[4,48,384]{2,1,0:T(8,128)(2,1)S(1)}, bf16[4,48,384]{2,1,0:T(8,128)(2,1)S(1)}, u32[]{:S(2)}, u32[]{:S(2)}) collective-permute-start(bf16[4,48,384]{2,1,0:T(8,128)(2,1)S(1)} %fusion.3), channel_id=1, source_target_pairs={{0,2},{1,3},{2,0},{3,1},{4,6},{5,7},{6,4},{7,5},{8,10},{9,11},{10,... | collective-permute-start | bytes 442376 | tf_op jit(solution)/shard_map/ppermute | solution.py:214
  18.8 0.7 %collective-permute-done.6 = bf16[96,384]{1,0:T(8,128)(2,1)S(1)} collective-permute-done((bf16[96,384]{1,0:T(8,128)(2,1)S(1)}, bf16[96,384]{1,0:T(8,128)(2,1)S(1)}, u32[]{:S(2)}, u32[]{:S(2)}) %collective-permute-start.6) | collective-permute-done | bytes 73760 | tf_op jit(solution)/shard_map/ppermute | solution.py:214
  19.5 2.7 %collective-permute-start.7 = (bf16[96,384]{1,0:T(8,128)(2,1)S(1)}, bf16[96,384]{1,0:T(8,128)(2,1)S(1)}, u32[]{:S(2)}, u32[]{:S(2)}) collective-permute-start(bf16[96,384]{1,0:T(8,128)(2,1)S(1)} %fusion.4), channel_id=1, source_target_pairs={{0,8},{1,9},{2,10},{3,11},{4,12},{5,13},{6,14},{7,15},{8,0},{9,1},... | collective-permute-start | bytes 221192 | tf_op jit(solution)/shard_map/ppermute | solution.py:214
  22.1 1.3 %collective-permute-done.3 = bf16[4,48,384]{2,1,0:T(8,128)(2,1)S(1)} collective-permute-done((bf16[4,48,384]{2,1,0:T(8,128)(2,1)S(1)}, bf16[4,48,384]{2,1,0:T(8,128)(2,1)S(1)}, u32[]{:S(2)}, u32[]{:S(2)}) %collective-permute-start.3) | collective-permute-done | bytes 147488 | tf_op jit(solution)/shard_map/ppermute | solution.py:214
  23.5 1.6 %collective-permute-start.9 = (bf16[96,384]{1,0:T(8,128)(2,1)S(1)}, bf16[96,384]{1,0:T(8,128)(2,1)S(1)}, u32[]{:S(2)}, u32[]{:S(2)}) collective-permute-start(bf16[96,384]{1,0:T(8,128)(2,1)S(1)} %fusion.7), channel_id=1, source_target_pairs={{0,4},{1,5},{2,6},{3,7},{4,0},{5,1},{6,2},{7,3},{8,12},{9,13},{10,... | collective-permute-start | bytes 221192 | tf_op jit(solution)/shard_map/ppermute | solution.py:214
  25.1 1.1 %collective-permute-done.7 = bf16[96,384]{1,0:T(8,128)(2,1)S(1)} collective-permute-done((bf16[96,384]{1,0:T(8,128)(2,1)S(1)}, bf16[96,384]{1,0:T(8,128)(2,1)S(1)}, u32[]{:S(2)}, u32[]{:S(2)}) %collective-permute-start.7) | collective-permute-done | bytes 73760 | tf_op jit(solution)/shard_map/ppermute | solution.py:214
  26.7 1.9 %collective-permute-done.9 = bf16[96,384]{1,0:T(8,128)(2,1)S(1)} collective-permute-done((bf16[96,384]{1,0:T(8,128)(2,1)S(1)}, bf16[96,384]{1,0:T(8,128)(2,1)S(1)}, u32[]{:S(2)}, u32[]{:S(2)}) %collective-permute-start.9) | collective-permute-done | bytes 73760 | tf_op jit(solution)/shard_map/ppermute | solution.py:214
  28.6 2.1 %collective-permute-start.10 = (bf16[96,384]{1,0:T(8,128)(2,1)S(1)}, bf16[96,384]{1,0:T(8,128)(2,1)S(1)}, u32[]{:S(2)}, u32[]{:S(2)}) collective-permute-start(bf16[96,384]{1,0:T(8,128)(2,1)S(1)} %fusion.5), channel_id=1, source_target_pairs={{0,8},{1,9},{2,10},{3,11},{4,12},{5,13},{6,14},{7,15},{8,0},{9,1},... | collective-permute-start | bytes 221192 | tf_op jit(solution)/shard_map/ppermute | solution.py:214
  30.7 1.3 %collective-permute-start.5 = (s32[2,2]{1,0:T(2,128)S(1)}, s32[2,2]{1,0:T(2,128)S(1)}, u32[]{:S(2)}, u32[]{:S(2)}) collective-permute-start(s32[2,2]{1,0:T(2,128)S(1)} %pad_add_fusion), channel_id=1, source_target_pairs={{0,2},{1,3},{2,0},{3,1},{4,6},{5,7},{6,4},{7,5},{8,10},{9,11},{10,... | collective-permute-start | bytes 56 | tf_op jit(solution)/shard_map/ppermute | solution.py:214
  32.0 1.9 %collective-permute-done.10 = bf16[96,384]{1,0:T(8,128)(2,1)S(1)} collective-permute-done((bf16[96,384]{1,0:T(8,128)(2,1)S(1)}, bf16[96,384]{1,0:T(8,128)(2,1)S(1)}, u32[]{:S(2)}, u32[]{:S(2)}) %collective-permute-start.10) | collective-permute-done | bytes 73760 | tf_op jit(solution)/shard_map/ppermute | solution.py:214
  33.9 1.7 %collective-permute-start.11 = (bf16[96,384]{1,0:T(8,128)(2,1)S(1)}, bf16[96,384]{1,0:T(8,128)(2,1)S(1)}, u32[]{:S(2)}, u32[]{:S(2)}) collective-permute-start(bf16[96,384]{1,0:T(8,128)(2,1)S(1)} %add_convert_fusion), channel_id=1, source_target_pairs={{0,4},{1,5},{2,6},{3,7},{4,0},{5,1},{6,2},{7,3},{8,12},{9,13},{10,... | collective-permute-start | bytes 221192 | tf_op jit(solution)/shard_map/ppermute | solution.py:214
  35.7 2.7 %collective-permute-done.11 = bf16[96,384]{1,0:T(8,128)(2,1)S(1)} collective-permute-done((bf16[96,384]{1,0:T(8,128)(2,1)S(1)}, bf16[96,384]{1,0:T(8,128)(2,1)S(1)}, u32[]{:S(2)}, u32[]{:S(2)}) %collective-permute-start.11) | collective-permute-done | bytes 73760 | tf_op jit(solution)/shard_map/ppermute | solution.py:214
  38.4 0.6 %select_slices.1 = (bf16[1,2,48,384]{3,2,1,0:T(8,128)(2,1)S(1)}, bf16[1,2,48,384]{3,2,1,0:T(8,128)(2,1)S(1)}, bf16[1,2,48,384]{3,2,1,0:T(8,128)(2,1)S(1)}, bf16[1,2,48,384]{3,2,1,0:T(8,128)(2,1)S(1)}) custom-call(s32[1,2]{1,0:T(1,128)S(1)} %copy-done.1, s32[1,2]{1,0:T(1,128)S(1)} %collective-permute-done.4.refs_1_, s32[1,2]{1,0:T(1,128)S(1)} %get-tuple-element.30.refs_2_, ...), custom_call_target="tpu_custom_call" | custom-call | tf_op jit(solution)/shard_map/select_slices/pallas_call | solution.py:126
  39.1 1.3 %collective-permute-start.13 = (bf16[1,2,48,384]{3,2,1,0:T(8,128)(2,1)S(1)}, bf16[1,2,48,384]{3,2,1,0:T(8,128)(2,1)S(1)}, u32[]{:S(2)}, u32[]{:S(2)}) collective-permute-start(bf16[1,2,48,384]{3,2,1,0:T(8,128)(2,1)S(1)} %get-tuple-element.27), channel_id=1, source_target_pairs={{0,2},{1,3},{2,0},{3,1},{4,6},{5,7},{6,4},{7,5},{8,10},{9,11},{10,... | collective-permute-start | bytes 221192 | tf_op jit(solution)/shard_map/ppermute | solution.py:214
  40.9 3.2 %collective-permute-done.13.by_pair = bf16[1,2,48,384]{3,2,1,0:T(8,128)(2,1)S(1)} collective-permute-done((bf16[1,2,48,384]{3,2,1,0:T(8,128)(2,1)S(1)}, bf16[1,2,48,384]{3,2,1,0:T(8,128)(2,1)S(1)}, u32[]{:S(2)}, u32[]{:S(2)}) %collective-permute-start.13) | collective-permute-done | bytes 73760 | tf_op jit(solution)/shard_map/ppermute | solution.py:214
  44.1 0.8 %collective-permute-done.14.by_both = bf16[1,2,48,384]{3,2,1,0:T(8,128)(2,1)S(1)} collective-permute-done((bf16[1,2,48,384]{3,2,1,0:T(8,128)(2,1)S(1)}, bf16[1,2,48,384]{3,2,1,0:T(8,128)(2,1)S(1)}, u32[]{:S(2)}, u32[]{:S(2)}) %collective-permute-start.14) | collective-permute-done | bytes 73760 | tf_op jit(solution)/shard_map/ppermute | solution.py:214
  44.9 5.0 %meson_blocks.1 = bf16[1,2,768,768]{3,2,1,0:T(8,128)(2,1)} custom-call(bf16[1,2,48,384]{3,2,1,0:T(8,128)(2,1)S(1)} %get-tuple-element.25.own, bf16[1,2,48,384]{3,2,1,0:T(8,128)(2,1)S(1)} %collective-permute-done.12.by_core, bf16[1,2,48,384]{3,2,1,0:T(8,128)(2,1)S(1)} %collective-permute-done.13.by_pair, ...), custom_call_target="tpu_custom_call" | custom-call | flops 1811939328 | bytes 4718592 | tf_op jit(solution)/shard_map/meson_blocks/pallas_call | solution.py:192
  (30 shorter events, 1.9 us)
Async XLA Ops:
  0.0 0.7 %copy-start = (s32[3]{0:T(128)S(1)}, s32[3]{0:T(128)}, u32[]{:S(2)}) copy-start(s32[3]{0:T(128)} %param.5) | copy-start | bytes 40
  5.2 1.7 %collective-permute-start = (bf16[2,4,48,384]{3,2,1,0:T(8,128)(2,1)S(1)}, bf16[2,4,48,384]{3,2,1,0:T(8,128)(2,1)S(1)}, u32[]{:S(2)}, u32[]{:S(2)}) collective-permute-start(bf16[2,4,48,384]{3,2,1,0:T(8,128)(2,1)S(1)} %get-tuple-element.18), channel_id=1, source_target_pairs={{0,1},{1,0},{2,3},{3,2},{4,5},{5,4},{6,7},{7,6},{8,9},{9,8},{10,11... | collective-permute-start | bytes 884744 | tf_op jit(solution)/shard_map/ppermute | solution.py:214
  7.1 7.5 %collective-permute-start.1 = (bf16[4,48,384]{2,1,0:T(8,128)(2,1)S(1)}, bf16[4,48,384]{2,1,0:T(8,128)(2,1)S(1)}, u32[]{:S(2)}, u32[]{:S(2)}) collective-permute-start(bf16[4,48,384]{2,1,0:T(8,128)(2,1)S(1)} %fusion.2.before), channel_id=1, source_target_pairs={{0,2},{1,3},{2,0},{3,1},{4,6},{5,7},{6,4},{7,5},{8,10},{9,11},{10,... | collective-permute-start | bytes 442376 | tf_op jit(solution)/shard_map/ppermute | solution.py:214
  14.6 12.1 %copy-start.1 = (s32[1,2]{1,0:T(1,128)S(1)}, s32[1,2]{1,0:T(1,128)}, u32[]{:S(2)}) copy-start(s32[1,2]{1,0:T(1,128)} %refs_0_.1) | copy-start | bytes 28
  14.6 30.3 %copy-start.2 = (bf16[1,2,768,768]{3,2,1,0:T(8,128)(2,1)S(1)}, bf16[1,2,768,768]{3,2,1,0:T(8,128)(2,1)}, u32[]{:S(2)}) copy-start(bf16[1,2,768,768]{3,2,1,0:T(8,128)(2,1)} %peram.1) | copy-start | bytes 7077892
  14.6 1.8 %collective-permute-start.2 = (bf16[2,4,48,384]{3,2,1,0:T(8,128)(2,1)S(1)}, bf16[2,4,48,384]{3,2,1,0:T(8,128)(2,1)}, u32[]{:S(2)}, u32[]{:S(2)}) collective-permute-start(bf16[2,4,48,384]{3,2,1,0:T(8,128)(2,1)S(1)} %get-tuple-element.21), channel_id=1, source_target_pairs={{0,1},{1,0},{2,3},{3,2},{4,5},{5,4},{6,7},{7,6},{8,9},{9,8},{10,11... | collective-permute-start | bytes 884744 | tf_op jit(solution)/shard_map/ppermute | solution.py:214
  14.7 4.7 %collective-permute-start.6 = (bf16[96,384]{1,0:T(8,128)(2,1)S(1)}, bf16[96,384]{1,0:T(8,128)(2,1)S(1)}, u32[]{:S(2)}, u32[]{:S(2)}) collective-permute-start(bf16[96,384]{1,0:T(8,128)(2,1)S(1)} %fusion.6), channel_id=1, source_target_pairs={{0,4},{1,5},{2,6},{3,7},{4,0},{5,1},{6,2},{7,3},{8,12},{9,13},{10,... | collective-permute-start | bytes 221192 | tf_op jit(solution)/shard_map/ppermute | solution.py:214
  17.5 6.0 %collective-permute-start.3 = (bf16[4,48,384]{2,1,0:T(8,128)(2,1)S(1)}, bf16[4,48,384]{2,1,0:T(8,128)(2,1)S(1)}, u32[]{:S(2)}, u32[]{:S(2)}) collective-permute-start(bf16[4,48,384]{2,1,0:T(8,128)(2,1)S(1)} %fusion.3), channel_id=1, source_target_pairs={{0,2},{1,3},{2,0},{3,1},{4,6},{5,7},{6,4},{7,5},{8,10},{9,11},{10,... | collective-permute-start | bytes 442376 | tf_op jit(solution)/shard_map/ppermute | solution.py:214
  19.5 6.7 %collective-permute-start.7 = (bf16[96,384]{1,0:T(8,128)(2,1)S(1)}, bf16[96,384]{1,0:T(8,128)(2,1)S(1)}, u32[]{:S(2)}, u32[]{:S(2)}) collective-permute-start(bf16[96,384]{1,0:T(8,128)(2,1)S(1)} %fusion.4), channel_id=1, source_target_pairs={{0,8},{1,9},{2,10},{3,11},{4,12},{5,13},{6,14},{7,15},{8,0},{9,1},... | collective-permute-start | bytes 221192 | tf_op jit(solution)/shard_map/ppermute | solution.py:214
  23.5 5.0 %collective-permute-start.9 = (bf16[96,384]{1,0:T(8,128)(2,1)S(1)}, bf16[96,384]{1,0:T(8,128)(2,1)S(1)}, u32[]{:S(2)}, u32[]{:S(2)}) collective-permute-start(bf16[96,384]{1,0:T(8,128)(2,1)S(1)} %fusion.7), channel_id=1, source_target_pairs={{0,4},{1,5},{2,6},{3,7},{4,0},{5,1},{6,2},{7,3},{8,12},{9,13},{10,... | collective-permute-start | bytes 221192 | tf_op jit(solution)/shard_map/ppermute | solution.py:214
  26.3 9.4 %collective-permute-start.8 = (bf16[96,384]{1,0:T(8,128)(2,1)S(1)}, bf16[96,384]{1,0:T(8,128)(2,1)S(1)}, u32[]{:S(2)}, u32[]{:S(2)}) collective-permute-start(bf16[96,384]{1,0:T(8,128)(2,1)S(1)} %add_convert_fusion.1), channel_id=1, source_target_pairs={{0,4},{1,5},{2,6},{3,7},{4,0},{5,1},{6,2},{7,3},{8,12},{9,13},{10,... | collective-permute-start | bytes 221192 | tf_op jit(solution)/shard_map/ppermute | solution.py:214
  26.7 4.0 %collective-permute-start.4 = (s32[1,2]{1,0:T(1,128)S(1)}, s32[1,2]{1,0:T(1,128)S(1)}, u32[]{:S(2)}, u32[]{:S(2)}) collective-permute-start(s32[1,2]{1,0:T(1,128)S(1)} %copy-done.1), channel_id=1, source_target_pairs={{0,1},{1,0},{2,3},{3,2},{4,5},{5,4},{6,7},{7,6},{8,9},{9,8},{10,11... | collective-permute-start | bytes 32 | tf_op jit(solution)/shard_map/ppermute | solution.py:214
  28.6 5.3 %collective-permute-start.10 = (bf16[96,384]{1,0:T(8,128)(2,1)S(1)}, bf16[96,384]{1,0:T(8,128)(2,1)S(1)}, u32[]{:S(2)}, u32[]{:S(2)}) collective-permute-start(bf16[96,384]{1,0:T(8,128)(2,1)S(1)} %fusion.5), channel_id=1, source_target_pairs={{0,8},{1,9},{2,10},{3,11},{4,12},{5,13},{6,14},{7,15},{8,0},{9,1},... | collective-permute-start | bytes 221192 | tf_op jit(solution)/shard_map/ppermute | solution.py:214
  30.7 5.0 %collective-permute-start.5 = (s32[2,2]{1,0:T(2,128)S(1)}, s32[2,2]{1,0:T(2,128)S(1)}, u32[]{:S(2)}, u32[]{:S(2)}) collective-permute-start(s32[2,2]{1,0:T(2,128)S(1)} %pad_add_fusion), channel_id=1, source_target_pairs={{0,2},{1,3},{2,0},{3,1},{4,6},{5,7},{6,4},{7,5},{8,10},{9,11},{10,... | collective-permute-start | bytes 56 | tf_op jit(solution)/shard_map/ppermute | solution.py:214
  33.9 4.4 %collective-permute-start.11 = (bf16[96,384]{1,0:T(8,128)(2,1)S(1)}, bf16[96,384]{1,0:T(8,128)(2,1)S(1)}, u32[]{:S(2)}, u32[]{:S(2)}) collective-permute-start(bf16[96,384]{1,0:T(8,128)(2,1)S(1)} %add_convert_fusion), channel_id=1, source_target_pairs={{0,4},{1,5},{2,6},{3,7},{4,0},{5,1},{6,2},{7,3},{8,12},{9,13},{10,... | collective-permute-start | bytes 221192 | tf_op jit(solution)/shard_map/ppermute | solution.py:214
  39.0 1.9 %collective-permute-start.12 = (bf16[1,2,48,384]{3,2,1,0:T(8,128)(2,1)S(1)}, bf16[1,2,48,384]{3,2,1,0:T(8,128)(2,1)S(1)}, u32[]{:S(2)}, u32[]{:S(2)}) collective-permute-start(bf16[1,2,48,384]{3,2,1,0:T(8,128)(2,1)S(1)} %get-tuple-element.26), channel_id=1, source_target_pairs={{0,1},{1,0},{2,3},{3,2},{4,5},{5,4},{6,7},{7,6},{8,9},{9,8},{10,11... | collective-permute-start | bytes 221192 | tf_op jit(solution)/shard_map/ppermute | solution.py:214
  39.1 5.1 %collective-permute-start.13 = (bf16[1,2,48,384]{3,2,1,0:T(8,128)(2,1)S(1)}, bf16[1,2,48,384]{3,2,1,0:T(8,128)(2,1)S(1)}, u32[]{:S(2)}, u32[]{:S(2)}) collective-permute-start(bf16[1,2,48,384]{3,2,1,0:T(8,128)(2,1)S(1)} %get-tuple-element.27), channel_id=1, source_target_pairs={{0,2},{1,3},{2,0},{3,1},{4,6},{5,7},{6,4},{7,5},{8,10},{9,11},{10,... | collective-permute-start | bytes 221192 | tf_op jit(solution)/shard_map/ppermute | solution.py:214
  40.4 4.5 %collective-permute-start.14 = (bf16[1,2,48,384]{3,2,1,0:T(8,128)(2,1)S(1)}, bf16[1,2,48,384]{3,2,1,0:T(8,128)(2,1)S(1)}, u32[]{:S(2)}, u32[]{:S(2)}) collective-permute-start(bf16[1,2,48,384]{3,2,1,0:T(8,128)(2,1)S(1)} %get-tuple-element.28), channel_id=1, source_target_pairs={{0,3},{1,2},{2,1},{3,0},{4,7},{5,6},{6,5},{7,4},{8,11},{9,10},{10,... | collective-permute-start | bytes 221192 | tf_op jit(solution)/shard_map/ppermute | solution.py:214

commit v4 on v3

v4 whole, which is shorter than its diff:
```python
import functools
import math

import jax
import jax.numpy as jnp
from jax import lax
from jax.experimental import pallas as pl
from jax.experimental.pallas import tpu as pltpu
from jax.sharding import PartitionSpec as P

BF16 = jnp.bfloat16
F32 = jnp.float32
NT_DIMS = (((1,), (1,)), ((), ()))
CHUNKS = (4, 4)
ARRIVALS = (1, 2, 5)


def dot_nt(left, right):
    return lax.dot_general(left, right, NT_DIMS, preferred_element_type=F32)


def elemental_kernel(devices, chunks, arrivals, momentum, eigvecs, *refs):
    outs = refs[:-3]
    vec, total, arrived = refs[-3:]
    count, _, colors, width, sites = vec.shape
    rows = width // 4

    def load(at):
        return pltpu.make_async_copy(eigvecs.at[at], vec.at[at], arrived.at[at])

    for at in range(count):
        load(at).start()
    device = lax.axis_index("sink")
    core = jnp.bitwise_and(device, 1)
    chip = jnp.bitwise_and(lax.shift_right_logical(device, 1), 1)
    local = lax.broadcasted_iota(jnp.int32, (1, sites), 1)
    extent = sites // 16
    turn = jnp.mod(momentum[0:1, 0:1] * device, devices).astype(F32) / devices
    second = momentum[0:1, 1:2] * lax.shift_right_logical(local, 4)
    turn = turn + jnp.mod(second, extent).astype(F32) / extent
    third = momentum[0:1, 2:3] * jnp.bitwise_and(local, 15)
    turn = turn + jnp.mod(third, 16).astype(F32) / 16.0
    theta = (2.0 * math.pi) * turn
    cosine = jnp.cos(theta)
    sine = jnp.sin(theta)
    waits = [start for start, many in arrivals for _ in range(many)]
    for at in range(count):
        for late in range(at, count):
            if waits[late] == at:
                load(late).wait()
        plain = []
        rotated = []
        for color in range(colors):
            low_re = vec[at, 0, color]
            low_im = vec[at, 1, color]
            vec_re = low_re.astype(F32)
            vec_im = low_im.astype(F32)
            rot_re = (cosine * vec_re + sine * vec_im).astype(BF16)
            rot_im = (cosine * vec_im - sine * vec_re).astype(BF16)
            plain.append(jnp.concatenate([low_re, low_im], axis=0))
            rotated.append(jnp.concatenate([rot_re, rot_im], axis=0))
        both = dot_nt(jnp.concatenate(plain, axis=1), jnp.concatenate(rotated, axis=1))
        real = both[:width, :width] + both[width:, width:]
        imag = both[:width, width:] - both[width:, :width]
        total[at] = jnp.concatenate([real, imag], axis=1)
    for side in range(2):

        @pl.when(core == side)
        def _():
            first = 0
            for chunk, many in enumerate(chunks):
                keep, send = outs[2 * chunk : 2 * chunk + 2]
                for at in range(many):
                    for pair in range(2):
                        slot = jnp.bitwise_xor(chip, pair)
                        mine = (2 * pair + side) * rows
                        other = (2 * pair + 1 - side) * rows
                        keep[slot, at] = total[first + at, mine : mine + rows]
                        send[slot, at] = total[first + at, other : other + rows].astype(BF16)
                first += many


def elementals(eigvecs, momentum, devices):
    slices, _, colors, width, sites = eigvecs.shape
    rows = width // 4
    chunks = [part * slices // 8 for part in CHUNKS]
    arrivals = [part * slices // 8 for part in ARRIVALS]
    arrivals = [(sum(arrivals[:at]), many) for at, many in enumerate(arrivals)]
    shapes = []
    for count in chunks:
        shapes += [
            jax.ShapeDtypeStruct((2, count, rows, 2 * width), F32),
            jax.ShapeDtypeStruct((2, count, rows, 2 * width), BF16),
        ]
    outs = pl.pallas_call(
        functools.partial(elemental_kernel, devices, chunks, arrivals),
        in_specs=[pl.BlockSpec(memory_space=pltpu.VMEM), pl.BlockSpec(memory_space=pl.ANY)],
        out_specs=[pl.BlockSpec(memory_space=pltpu.VMEM)] * len(shapes),
        scratch_shapes=[
            pltpu.VMEM((slices, 2, colors, width, sites), BF16),
            pltpu.VMEM((slices, width, 2 * width), F32),
            pltpu.SemaphoreType.DMA((slices,)),
        ],
        out_shape=shapes,
        compiler_params=pltpu.CompilerParams(vmem_limit_bytes=50 * 1024 * 1024),
        cost_estimate=pl.CostEstimate(
            flops=slices * 8 * colors * width * width * sites,
            bytes_accessed=slices * 2 * colors * width * sites * 2,
            transcendentals=0,
        ),
        name="partial_elementals",
    )(momentum, eigvecs)
    return [outs[at : at + 2] for at in range(0, len(outs), 2)]


def select_kernel(firsts, *refs):
    many = sum(2 if halves else 1 for _, halves in firsts)
    wanted = refs[:4]
    blocks = refs[4 : 4 + many]
    outs = refs[4 + many : 12 + many]
    held = refs[-1]
    rows = held.shape[1]
    upper = jnp.bitwise_and(lax.shift_right_logical(lax.axis_index("sink"), 2), 1)
    for side in range(2):

        @pl.when(upper == side)
        def _():
            at = 0
            for first, halves in firsts:
                for flip in range(2 if halves else 1):
                    block = blocks[at]
                    start = (side ^ flip) * (rows // 2) if halves else 0
                    held[first : first + block.shape[0], start : start + block.shape[1], :] = block[...]
                    at += 1

    for at, times in enumerate(wanted):
        for side in range(2):
            out = outs[4 * side + at]
            for pair in range(out.shape[0]):
                out[pair] = held[times[pair, side]]


def select(blocks, firsts, wanted, slices, rows):
    pairs = wanted[0].shape[0]
    both = blocks[0].shape[2]
    shape = jax.ShapeDtypeStruct((pairs, rows, both), BF16)
    return pl.pallas_call(
        functools.partial(select_kernel, firsts),
        in_specs=[pl.BlockSpec(memory_space=pltpu.SMEM)] * 4
        + [pl.BlockSpec(memory_space=pltpu.VMEM)] * len(blocks),
        out_specs=[pl.BlockSpec(memory_space=pltpu.VMEM)] * 8,
        scratch_shapes=[pltpu.VMEM((slices, rows, both), BF16)],
        out_shape=[shape] * 8,
        compiler_params=pltpu.CompilerParams(vmem_limit_bytes=8 * 1024 * 1024),
        name="select_slices",
    )(*wanted, *blocks)


def gather_rows(pair, parts, full):
    rows = full.shape[0] // 4
    place = jnp.bitwise_and(lax.axis_index("sink"), 3)
    for flip, part in enumerate(parts):
        start = pl.multiple_of(jnp.bitwise_xor(place, flip) * rows, rows)
        full[pl.ds(start, rows), :] = part[pair]


def left_kernel(own, by_core, by_pair, by_both, peram, left, sink_el, left_mat):
    width = sink_el.shape[0]
    for pair in range(peram.shape[0]):
        gather_rows(pair, (own, by_core, by_pair, by_both), sink_el)
        a_re = sink_el[:, :width]
        a_im = sink_el[:, width:]
        left_mat[:width] = jnp.concatenate([a_re, -a_im], axis=1)
        left_mat[width:] = jnp.concatenate([a_im, a_re], axis=1)
        for a in range(4):
            band = slice((a + 2) % 4 * width, ((a + 2) % 4 + 1) * width)
            stacked = jnp.concatenate([peram[pair, 0, band], peram[pair, 1, band]], axis=0)
            both = jnp.dot(left_mat[...], stacked, preferred_element_type=F32)
            both = (both if a < 2 else -both).astype(BF16)
            left[pair, 0, a * width : (a + 1) * width] = both[:width]
            left[pair, 1, a * width : (a + 1) * width] = both[width:]


def right_kernel(own, by_core, by_pair, by_both, left, out, src_el, right_mat, block, stored):
    width = src_el.shape[0]
    window = right_mat.shape[1] // 2
    edge = 2 * width - window

    def store(pair, a):
        band = pl.ds(a * width, width)
        return pltpu.make_async_copy(block.at[a], out.at[pair, :, band, :], stored.at[a])

    for pair in range(left.shape[0]):
        gather_rows(pair, (own, by_core, by_pair, by_both), src_el)
        e_re = src_el[:, :width]
        e_im = src_el[:, width:]
        pad = jnp.zeros((width, window - width), BF16)
        hole = jnp.zeros((window - width, 2 * window), BF16)
        even_re = jnp.concatenate([e_re, pad, e_im, pad], axis=1)
        even_im = jnp.concatenate([-e_im, pad, e_re, pad], axis=1)
        odd_re = jnp.concatenate([pad, e_re, pad, e_im], axis=1)
        odd_im = jnp.concatenate([pad, -e_im, pad, e_re], axis=1)
        right_mat[0] = jnp.concatenate([even_re, hole, even_im, hole], axis=0)
        right_mat[1] = jnp.concatenate([hole, odd_re, hole, odd_im], axis=0)
        for a in range(4):
            band = slice(a * width, (a + 1) * width)
            results = []
            for odd in range(2):
                starts = [b * width - odd * (window - width) for b in (2 + odd, odd)]
                y_re = jnp.concatenate([left[pair, 0, band, at : at + window] for at in starts], axis=0)
                y_im = jnp.concatenate([left[pair, 1, band, at : at + window] for at in starts], axis=0)
                results.append(dot_nt(jnp.concatenate([y_re, y_im], axis=1), right_mat[odd]))
            if pair > 0:
                store(pair - 1, a).wait()
            for half in range(2):
                for part in range(2):
                    rect = slice(half * width, (half + 1) * width), slice(part * window, (part + 1) * window)
                    even = results[0][rect]
                    odd = results[1][rect]
                    first = 2 * half * width
                    block[a, part, :, first : first + edge] = even[:, :edge].astype(BF16)
                    middle = even[:, edge:] + odd[:, : window - edge]
                    block[a, part, :, first + edge : first + window] = middle.astype(BF16)
                    block[a, part, :, first + window : first + 2 * width] = odd[:, window - edge :].astype(BF16)
            store(pair, a).start()
    for a in range(4):
        store(left.shape[0] - 1, a).wait()


def pair_blocks(peram, sink_parts, src_parts):
    pairs, _, full, _ = peram.shape
    width = full // 4
    window = -(-width // 128) * 128
    params = pltpu.CompilerParams(vmem_limit_bytes=16 * 1024 * 1024)
    cost = pl.CostEstimate(
        flops=pairs * 8 * full * full * width, bytes_accessed=pairs * 4 * full * full, transcendentals=0
    )
    left = pl.pallas_call(
        left_kernel,
        in_specs=[pl.BlockSpec(memory_space=pltpu.VMEM)] * 5,
        out_specs=pl.BlockSpec(memory_space=pltpu.VMEM),
        scratch_shapes=[
            pltpu.VMEM((width, 2 * width), BF16),
            pltpu.VMEM((2 * width, 2 * width), BF16),
        ],
        out_shape=jax.ShapeDtypeStruct(peram.shape, BF16),
        compiler_params=params,
        cost_estimate=cost,
        name="left_product",
    )(*sink_parts, peram)
    return pl.pallas_call(
        right_kernel,
        in_specs=[pl.BlockSpec(memory_space=pltpu.VMEM)] * 5,
        out_specs=pl.BlockSpec(memory_space=pl.ANY),
        scratch_shapes=[
            pltpu.VMEM((width, 2 * width), BF16),
            pltpu.VMEM((2, 2 * window, 2 * window), BF16),
            pltpu.VMEM((4, 2, width, full), BF16),
            pltpu.SemaphoreType.DMA((4,)),
        ],
        out_shape=jax.ShapeDtypeStruct(peram.shape, BF16),
        compiler_params=params,
        cost_estimate=cost,
        name="meson_blocks",
    )(*src_parts, left)


def swap(value, flip, devices):
    return lax.ppermute(value, "sink", [(i, i ^ flip) for i in range(devices)])


def sum_near(keep, send, devices):
    over_core = keep + swap(send, 1, devices).astype(F32)
    return over_core[0] + swap(over_core[1].astype(BF16), 2, devices).astype(F32)


def sum_far(near, flip, group, devices):
    count, rows, both = near.shape
    if 8 * flip == devices:
        return [(near + swap(near.astype(BF16), 4 * flip, devices).astype(F32)).astype(BF16)]
    cut = near.reshape(count, 2, rows // 2, both)
    bit = jnp.bitwise_and(lax.shift_right_logical(group, flip.bit_length() - 1), 1)
    kept = lax.dynamic_index_in_dim(cut, bit, 1, keepdims=False)
    given = lax.dynamic_index_in_dim(cut, 1 - bit, 1, keepdims=False).astype(BF16)
    kept = kept + swap(given, 4 * flip, devices).astype(F32)
    blocks = sum_far(kept, 2 * flip, group, devices)
    if len(blocks) == 1:
        return blocks + [swap(blocks[0], 4 * flip, devices)]
    other = swap(jnp.stack(blocks), 4 * flip, devices)
    return [block for at in range(len(blocks)) for block in (blocks[at], other[at])]


def shards(eigvecs, momentum, peram, times):
    devices = lax.axis_size("sink")
    group = lax.shift_right_logical(lax.axis_index("sink"), 2)
    owners = devices // 8
    slices, _, _, width, _ = eigvecs.shape
    rows = width // 4
    momentum = momentum.reshape(1, 3)
    blocks = []
    firsts = []
    nears = [sum_near(keep, send, devices) for keep, send in elementals(eigvecs, momentum, devices)]
    first = 0
    for near in nears:
        count = near.shape[0]
        shared = sum_far(near, 1, group, devices)
        if first == 0:
            late_times, shared[0] = lax.optimization_barrier((times, shared[0]))
            core_times = swap(late_times, 1, devices)
            other = swap(jnp.concatenate([late_times, core_times]), 2, devices)
            wanted = [times, core_times, other[: times.shape[0]], other[times.shape[0] :]]
        halves = owners == 2
        if halves:
            blocks += shared
        else:
            mine = 0
            for bit in range(owners.bit_length() - 1):
                mine = 2 * mine + ((group >> bit) & 1)
            shared = jnp.take(jnp.stack(shared), jnp.arange(owners) ^ mine, axis=0)
            blocks.append(jnp.swapaxes(shared, 0, 1).reshape(count, rows, 2 * width))
        firsts.append((first, halves))
        first += count
    parts = select(blocks, firsts, wanted, slices, rows)
    sink_parts = [parts[0]] + [swap(parts[flip], flip, devices) for flip in range(1, 4)]
    src_parts = [parts[4]] + [swap(parts[4 + flip], flip, devices) for flip in range(1, 4)]
    return pair_blocks(peram, sink_parts, src_parts)


def solution(mesh):
    in_specs = (
        P("groups", None, None, None, "sink"),
        P("groups"),
        P(("groups", "sink"), None, None, None),
        P(("groups", "sink"), None),
    )
    out_specs = P(("groups", "sink"), None, None, None)
    return jax.shard_map(shards, mesh=mesh, in_specs=in_specs, out_specs=out_specs, check_vma=False)
```

time: 50.1 us -> 47.3 us (0.944)
  starting transfers between devices: 18.3 us -> 21.3 us
  Pallas kernels: 14.8 us -> 12.1 us
  waiting for transfers between devices: 14.8 us -> 12.7 us
  other arithmetic: 1.21 us -> 0.27 us
    ppermute x15 -> x18, starting transfers between devices: 18.3 us -> 21.3 us  [swap(): return lax.ppermute(value, 'sink', [(i, i ^ flip) for i in range(devices)])]
    pallas_call x4, Pallas kernels: 14.8 us -> 12.1 us  [the longest x1 7.3 us: elementals(): pl.pallas_call(functools.partial(elemental_kernel, devices, chunks, arriv...]
    ppermute x15 -> x18, waiting for transfers between devices: 14.8 us -> 12.7 us  [swap(): return lax.ppermute(value, 'sink', [(i, i ^ flip) for i in range(devices)])]
    add x2, other arithmetic: 1.06 us -> 0.1 us  [sum_near(): over_core = keep + swap(send, 1, devices).astype(F32)]
  transfers between devices with their start and end apart: 15 -> 18, of which waited for: 9 -> 9; matrix products, arithmetic and copies ran while one was open for 2% -> 1% of each run, Pallas kernels for 9% -> 3%
where the time goes in v4:
time: 47.3 us; the launch traced here: 47.2 us
  starting transfers between devices  21.3 us (45%)
  waiting for transfers between devices  12.7 us (27%)
  Pallas kernels  12.1 us (26%)
  local copies, waits for them, and re-layouts  0.75 us (2%)
    ppermute x18, starting transfers between devices, swap(): return lax.ppermute(value, 'sink', [(i, i ^ flip) for i in range(devices)])  21.3 us
    ppermute x18, waiting for transfers between devices, swap(): return lax.ppermute(value, 'sink', [(i, i ^ flip) for i in range(devices)])  12.7 us
    pallas_call x1, Pallas kernels, elementals(): pl.pallas_call(functools.partial(elemental_kernel, devices, chunks, arriv...  7.3 us
    pallas_call x1, Pallas kernels, pair_blocks(): pl.pallas_call(right_kernel, in_specs=[pl.BlockSpec(memory_space=pltpu.VM...  2.75 us
    pallas_call x1, Pallas kernels, pair_blocks(): pl.pallas_call(left_kernel, in_specs=[pl.BlockSpec(memory_space=pltpu.VME...  1.39 us
  transfers between devices with their start and end apart: 18, of which 9 were waited for; matrix products, arithmetic and copies ran while one was open for 1% of the time, Pallas kernels for 3%

profile of v4, /device:TPU:0, one launch (start us, length us, event | category | flops | bytes accessed | tf_op | source)
XLA Modules:
  0.0 47.2 jit_solution(5673236807539382178)
XLA Ops:
  0.0 0.7 %copy-done.2 = s32[3]{0:T(128)S(1)} copy-done((s32[3]{0:T(128)S(1)}, s32[3]{0:T(128)}, u32[]{:S(2)}) %copy-start.2) | copy-done | bytes 36
  0.7 7.3 %partial_elementals.1 = (f32[2,4,48,384]{3,2,1,0:T(8,128)S(1)}, bf16[2,4,48,384]{3,2,1,0:T(8,128)(2,1)S(1)}, f32[2,4,48,384]{3,2,1,0:T(8,128)S(1)}, bf16[2,4,48,384]{3,2,1,0:T(8,128)(2,1)S(1)}) custom-call(s32[1,3]{1,0:T(1,128)S(1)} %bitcast.39, bf16[8,2,3,192,512]{4,3,2,1,0:T(8,128)(2,1)} %eigvecs.1), custom_call_target="tpu_custom_call" | custom-call | flops 3623878656 | bytes 9437184 | tf_op jit(solution)/shard_map/partial_elementals/pallas_call | solution.py:95
  8.0 0.5 %collective-permute-start = (bf16[2,4,48,384]{3,2,1,0:T(8,128)(2,1)S(1)}, bf16[2,4,48,384]{3,2,1,0:T(8,128)(2,1)S(1)}, u32[]{:S(2)}, u32[]{:S(2)}) collective-permute-start(bf16[2,4,48,384]{3,2,1,0:T(8,128)(2,1)S(1)} %get-tuple-element.20), channel_id=1, source_target_pairs={{0,1},{1,0},{2,3},{3,2},{4,5},{5,4},{6,7},{7,6},{8,9},{9,8},{10,11... | collective-permute-start | bytes 884744 | tf_op jit(solution)/shard_map/ppermute | solution.py:269
  8.6 1.1 %collective-permute-done = bf16[2,4,48,384]{3,2,1,0:T(8,128)(2,1)S(1)} collective-permute-done((bf16[2,4,48,384]{3,2,1,0:T(8,128)(2,1)S(1)}, bf16[2,4,48,384]{3,2,1,0:T(8,128)(2,1)S(1)}, u32[]{:S(2)}, u32[]{:S(2)}) %collective-permute-start) | collective-permute-done | bytes 294944 | tf_op jit(solution)/shard_map/ppermute | solution.py:269
  9.8 2.9 %collective-permute-start.1 = (bf16[4,48,384]{2,1,0:T(8,128)(2,1)S(1)}, bf16[4,48,384]{2,1,0:T(8,128)(2,1)S(1)}, u32[]{:S(2)}, u32[]{:S(2)}) collective-permute-start(bf16[4,48,384]{2,1,0:T(8,128)(2,1)S(1)} %fusion.2), channel_id=1, source_target_pairs={{0,2},{1,3},{2,0},{3,1},{4,6},{5,7},{6,4},{7,5},{8,10},{9,11},{10,... | collective-permute-start | bytes 442376 | tf_op jit(solution)/shard_map/ppermute | solution.py:269
  13.1 4.2 %collective-permute-done.1 = bf16[4,48,384]{2,1,0:T(8,128)(2,1)S(1)} collective-permute-done((bf16[4,48,384]{2,1,0:T(8,128)(2,1)S(1)}, bf16[4,48,384]{2,1,0:T(8,128)(2,1)S(1)}, u32[]{:S(2)}, u32[]{:S(2)}) %collective-permute-start.1) | collective-permute-done | bytes 147488 | tf_op jit(solution)/shard_map/ppermute | solution.py:269
  17.4 2.2 %collective-permute-start.2 = (bf16[4,24,384]{2,1,0:T(8,128)(2,1)S(1)}, bf16[4,24,384]{2,1,0:T(8,128)(2,1)S(1)}, u32[]{:S(2)}, u32[]{:S(2)}) collective-permute-start(bf16[4,24,384]{2,1,0:T(8,128)(2,1)S(1)} %fusion.6), channel_id=1, source_target_pairs={{0,4},{1,5},{2,6},{3,7},{4,0},{5,1},{6,2},{7,3},{8,12},{9,13},{10,... | collective-permute-start | bytes 221192 | tf_op jit(solution)/shard_map/ppermute | solution.py:269
  19.6 0.4 collective-permute-done.8
  20.1 1.9 %collective-permute-start.9 = (bf16[4,24,384]{2,1,0:T(8,128)(2,1)S(1)}, bf16[4,24,384]{2,1,0:T(8,128)(2,1)S(1)}, u32[]{:S(2)}, u32[]{:S(2)}) collective-permute-start(bf16[4,24,384]{2,1,0:T(8,128)(2,1)S(1)} %fusion.7), channel_id=1, source_target_pairs={{0,4},{1,5},{2,6},{3,7},{4,0},{5,1},{6,2},{7,3},{8,12},{9,13},{10,... | collective-permute-start | bytes 221192 | tf_op jit(solution)/shard_map/ppermute | solution.py:269
  22.0 3.2 %collective-permute-start.3 = (bf16[4,24,384]{2,1,0:T(8,128)(2,1)S(1)}, bf16[4,24,384]{2,1,0:T(8,128)(2,1)S(1)}, u32[]{:S(2)}, u32[]{:S(2)}) collective-permute-start(bf16[4,24,384]{2,1,0:T(8,128)(2,1)S(1)} %fusion.4), channel_id=1, source_target_pairs={{0,8},{1,9},{2,10},{3,11},{4,12},{5,13},{6,14},{7,15},{8,0},{9,1},... | collective-permute-start | bytes 221192 | tf_op jit(solution)/shard_map/ppermute | solution.py:269
  25.2 2.2 %collective-permute-start.10 = (bf16[4,24,384]{2,1,0:T(8,128)(2,1)S(1)}, bf16[4,24,384]{2,1,0:T(8,128)(2,1)S(1)}, u32[]{:S(2)}, u32[]{:S(2)}) collective-permute-start(bf16[4,24,384]{2,1,0:T(8,128)(2,1)S(1)} %fusion.5), channel_id=1, source_target_pairs={{0,8},{1,9},{2,10},{3,11},{4,12},{5,13},{6,14},{7,15},{8,0},{9,1},... | collective-permute-start | bytes 221192 | tf_op jit(solution)/shard_map/ppermute | solution.py:269
  27.4 2.3 %collective-permute-done.3 = bf16[4,24,384]{2,1,0:T(8,128)(2,1)S(1)} collective-permute-done((bf16[4,24,384]{2,1,0:T(8,128)(2,1)S(1)}, bf16[4,24,384]{2,1,0:T(8,128)(2,1)S(1)}, u32[]{:S(2)}, u32[]{:S(2)}) %collective-permute-start.3) | collective-permute-done | bytes 73760 | tf_op jit(solution)/shard_map/ppermute | solution.py:269
  29.8 1.5 %collective-permute-start.6 = (bf16[4,24,384]{2,1,0:T(8,128)(2,1)S(1)}, bf16[4,24,384]{2,1,0:T(8,128)(2,1)S(1)}, u32[]{:S(2)}, u32[]{:S(2)}) collective-permute-start(bf16[4,24,384]{2,1,0:T(8,128)(2,1)S(1)} %add_convert_fusion.1.refs_4_), channel_id=1, source_target_pairs={{0,4},{1,5},{2,6},{3,7},{4,0},{5,1},{6,2},{7,3},{8,12},{9,13},{10,... | collective-permute-start | bytes 221192 | tf_op jit(solution)/shard_map/ppermute | solution.py:269
  31.4 0.8 %collective-permute-start.11 = (bf16[4,24,384]{2,1,0:T(8,128)(2,1)S(1)}, bf16[4,24,384]{2,1,0:T(8,128)(2,1)S(1)}, u32[]{:S(2)}, u32[]{:S(2)}) collective-permute-start(bf16[4,24,384]{2,1,0:T(8,128)(2,1)S(1)} %add_convert_fusion.refs_6_), channel_id=1, source_target_pairs={{0,4},{1,5},{2,6},{3,7},{4,0},{5,1},{6,2},{7,3},{8,12},{9,13},{10,... | collective-permute-start | bytes 221192 | tf_op jit(solution)/shard_map/ppermute | solution.py:269
  32.5 1.6 %collective-permute-start.5 = (s32[2,2]{1,0:T(2,128)S(1)}, s32[2,2]{1,0:T(2,128)S(1)}, u32[]{:S(2)}, u32[]{:S(2)}) collective-permute-start(s32[2,2]{1,0:T(2,128)S(1)} %pad_add_fusion), channel_id=1, source_target_pairs={{0,2},{1,3},{2,0},{3,1},{4,6},{5,7},{6,4},{7,5},{8,10},{9,11},{10,... | collective-permute-start | bytes 56 | tf_op jit(solution)/shard_map/ppermute | solution.py:269
  34.1 2.0 %collective-permute-done.5 = s32[2,2]{1,0:T(2,128)S(1)} collective-permute-done((s32[2,2]{1,0:T(2,128)S(1)}, s32[2,2]{1,0:T(2,128)S(1)}, u32[]{:S(2)}, u32[]{:S(2)}) %collective-permute-start.5) | collective-permute-done | bytes 48 | tf_op jit(solution)/shard_map/ppermute | solution.py:269
  36.1 0.6 %select_slices.1 = (bf16[1,48,384]{2,1,0:T(8,128)(2,1)S(1)}, bf16[1,48,384]{2,1,0:T(8,128)(2,1)S(1)}, bf16[1,48,384]{2,1,0:T(8,128)(2,1)S(1)}, bf16[1,48,384]{2,...) custom-call(s32[1,2]{1,0:T(1,128)S(1)} %copy-done.1, ...), custom_call_target="tpu_custom_call" | custom-call | tf_op jit(solution)/shard_map/select_slices/pallas_call | solution.py:147
  36.8 1.7 %collective-permute-start.16 = (bf16[1,48,384]{2,1,0:T(8,128)(2,1)S(1)}, bf16[1,48,384]{2,1,0:T(8,128)(2,1)S(1)}, u32[]{:S(2)}, u32[]{:S(2)}) collective-permute-start(bf16[1,48,384]{2,1,0:T(8,128)(2,1)S(1)} %get-tuple-element.31), channel_id=1, source_target_pairs={{0,2},{1,3},{2,0},{3,1},{4,6},{5,7},{6,4},{7,5},{8,10},{9,11},{10,... | collective-permute-start | bytes 110600 | tf_op jit(solution)/shard_map/ppermute | solution.py:269
  38.7 0.3 collective-permute-start.12
  39.0 1.6 %collective-permute-start.13 = (bf16[1,48,384]{2,1,0:T(8,128)(2,1)S(1)}, bf16[1,48,384]{2,1,0:T(8,128)(2,1)S(1)}, u32[]{:S(2)}, u32[]{:S(2)}) collective-permute-start(bf16[1,48,384]{2,1,0:T(8,128)(2,1)S(1)} %get-tuple-element.27), channel_id=1, source_target_pairs={{0,2},{1,3},{2,0},{3,1},{4,6},{5,7},{6,4},{7,5},{8,10},{9,11},{10,... | collective-permute-start | bytes 110600 | tf_op jit(solution)/shard_map/ppermute | solution.py:269
  40.9 1.1 %collective-permute-done.17.by_both = bf16[1,48,384]{2,1,0:T(8,128)(2,1)S(1)} collective-permute-done((bf16[1,48,384]{2,1,0:T(8,128)(2,1)S(1)}, bf16[1,48,384]{2,1,0:T(8,128)(2,1)S(1)}, u32[]{:S(2)}, u32[]{:S(2)}) %collective-permute-start.17) | collective-permute-done | bytes 36896 | tf_op jit(solution)/shard_map/ppermute | solution.py:269
  42.0 1.4 %left_product.1.left = bf16[1,2,768,768]{3,2,1,0:T(8,128)(2,1)S(1)} custom-call(bf16[1,48,384]{2,1,0:T(8,128)(2,1)S(1)} %get-tuple-element.29.own, bf16[1,48,384]{2,1,0:T(8,128)(2,1)S(1)} %collective-permute-done.15.by_core, bf16[1,48,384]{2,1,0:T(8,128)(2,1)S(1)} %collective-permute-done.16.by_pair, ...), custom_call_target="tpu_custom_call" | custom-call | flops 905969664 | bytes 2359296 | tf_op jit(solution)/shard_map/left_product/pallas_call | solution.py:238
  43.4 1.0 %collective-permute-done.14.by_both = bf16[1,48,384]{2,1,0:T(8,128)(2,1)S(1)} collective-permute-done((bf16[1,48,384]{2,1,0:T(8,128)(2,1)S(1)}, bf16[1,48,384]{2,1,0:T(8,128)(2,1)S(1)}, u32[]{:S(2)}, u32[]{:S(2)}) %collective-permute-start.14) | collective-permute-done | bytes 36896 | tf_op jit(solution)/shard_map/ppermute | solution.py:269
  44.4 2.8 %meson_blocks.1 = bf16[1,2,768,768]{3,2,1,0:T(8,128)(2,1)} custom-call(bf16[1,48,384]{2,1,0:T(8,128)(2,1)S(1)} %get-tuple-element.25.own, bf16[1,48,384]{2,1,0:T(8,128)(2,1)S(1)} %collective-permute-done.12.by_core, bf16[1,48,384]{2,1,0:T(8,128)(2,1)S(1)} %collective-permute-done.13.by_pair, bf16[1,48,384]{2,1,0:T(8,128)(2,1)S(1)} %collective-permute-done.14.by_both, ...), custom_call_target="tpu_custom_call" | custom-call | flops 905969664 | bytes 2359296 | tf_op jit(solution)/shard_map/meson_blocks/pallas_call | solution.py:251
  (36 shorter events, 1.4 us)
Async XLA Ops:
  0.0 0.7 %copy-start.2 = (s32[3]{0:T(128)S(1)}, s32[3]{0:T(128)}, u32[]{:S(2)}) copy-start(s32[3]{0:T(128)} %param.5) | copy-start | bytes 40
  8.0 1.7 %collective-permute-start = (bf16[2,4,48,384]{3,2,1,0:T(8,128)(2,1)S(1)}, bf16[2,4,48,384]{3,2,1,0:T(8,128)(2,1)S(1)}, u32[]{:S(2)}, u32[]{:S(2)}) collective-permute-start(bf16[2,4,48,384]{3,2,1,0:T(8,128)(2,1)S(1)} %get-tuple-element.20), channel_id=1, source_target_pairs={{0,1},{1,0},{2,3},{3,2},{4,5},{5,4},{6,7},{7,6},{8,9},{9,8},{10,11... | collective-permute-start | bytes 884744 | tf_op jit(solution)/shard_map/ppermute | solution.py:269
  8.5 4.2 %collective-permute-start.7 = (bf16[2,4,48,384]{3,2,1,0:T(8,128)(2,1)S(1)}, bf16[2,4,48,384]{3,2,1,0:T(8,128)(2,1)S(1)}, u32[]{:S(2)}, u32[]{:S(2)}) collective-permute-start(bf16[2,4,48,384]{3,2,1,0:T(8,128)(2,1)S(1)} %get-tuple-element.24), channel_id=1, source_target_pairs={{0,1},{1,0},{2,3},{3,2},{4,5},{5,4},{6,7},{7,6},{8,9},{9,8},{10,11... | collective-permute-start | bytes 884744 | tf_op jit(solution)/shard_map/ppermute | solution.py:269
  9.8 21.6 %copy-start.1 = (s32[1,2]{1,0:T(1,128)S(1)}, s32[1,2]{1,0:T(1,128)}, u32[]{:S(2)}) copy-start(s32[1,2]{1,0:T(1,128)} %refs_0_.1) | copy-start | bytes 28
  9.8 7.5 %collective-permute-start.1 = (bf16[4,48,384]{2,1,0:T(8,128)(2,1)S(1)}, bf16[4,48,384]{2,1,0:T(8,128)(2,1)S(1)}, u32[]{:S(2)}, u32[]{:S(2)}) collective-permute-start(bf16[4,48,384]{2,1,0:T(8,128)(2,1)S(1)} %fusion.2), channel_id=1, source_target_pairs={{0,2},{1,3},{2,0},{3,1},{4,6},{5,7},{6,4},{7,5},{8,10},{9,11},{10,... | collective-permute-start | bytes 442376 | tf_op jit(solution)/shard_map/ppermute | solution.py:269
  12.7 29.3 %copy-start = (bf16[1,2,768,768]{3,2,1,0:T(8,128)(2,1)S(1)}, bf16[1,2,768,768]{3,2,1,0:T(8,128)(2,1)}, u32[]{:S(2)}) copy-start(bf16[1,2,768,768]{3,2,1,0:T(8,128)(2,1)} %peram.1) | copy-start | bytes 7077892
  12.8 7.2 %collective-permute-start.8 = (bf16[4,48,384]{2,1,0:T(8,128)(2,1)S(1)}, bf16[4,48,384]{2,1,0:T(8,128)(2,1)S(1)}, u32[]{:S(2)}, u32[]{:S(2)}) collective-permute-start(bf16[4,48,384]{2,1,0:T(8,128)(2,1)S(1)} %fusion.3), channel_id=1, source_target_pairs={{0,2},{1,3},{2,0},{3,1},{4,6},{5,7},{6,4},{7,5},{8,10},{9,11},{10,... | collective-permute-start | bytes 442376 | tf_op jit(solution)/shard_map/ppermute | solution.py:269
  17.4 4.6 %collective-permute-start.2 = (bf16[4,24,384]{2,1,0:T(8,128)(2,1)S(1)}, bf16[4,24,384]{2,1,0:T(8,128)(2,1)S(1)}, u32[]{:S(2)}, u32[]{:S(2)}) collective-permute-start(bf16[4,24,384]{2,1,0:T(8,128)(2,1)S(1)} %fusion.6), channel_id=1, source_target_pairs={{0,4},{1,5},{2,6},{3,7},{4,0},{5,1},{6,2},{7,3},{8,12},{9,13},{10,... | collective-permute-start | bytes 221192 | tf_op jit(solution)/shard_map/ppermute | solution.py:269
  20.1 5.1 %collective-permute-start.9 = (bf16[4,24,384]{2,1,0:T(8,128)(2,1)S(1)}, bf16[4,24,384]{2,1,0:T(8,128)(2,1)S(1)}, u32[]{:S(2)}, u32[]{:S(2)}) collective-permute-start(bf16[4,24,384]{2,1,0:T(8,128)(2,1)S(1)} %fusion.7), channel_id=1, source_target_pairs={{0,4},{1,5},{2,6},{3,7},{4,0},{5,1},{6,2},{7,3},{8,12},{9,13},{10,... | collective-permute-start | bytes 221192 | tf_op jit(solution)/shard_map/ppermute | solution.py:269
  22.0 7.8 %collective-permute-start.3 = (bf16[4,24,384]{2,1,0:T(8,128)(2,1)S(1)}, bf16[4,24,384]{2,1,0:T(8,128)(2,1)S(1)}, u32[]{:S(2)}, u32[]{:S(2)}) collective-permute-start(bf16[4,24,384]{2,1,0:T(8,128)(2,1)S(1)} %fusion.4), channel_id=1, source_target_pairs={{0,8},{1,9},{2,10},{3,11},{4,12},{5,13},{6,14},{7,15},{8,0},{9,1},... | collective-permute-start | bytes 221192 | tf_op jit(solution)/shard_map/ppermute | solution.py:269
  25.2 6.1 %collective-permute-start.10 = (bf16[4,24,384]{2,1,0:T(8,128)(2,1)S(1)}, bf16[4,24,384]{2,1,0:T(8,128)(2,1)S(1)}, u32[]{:S(2)}, u32[]{:S(2)}) collective-permute-start(bf16[4,24,384]{2,1,0:T(8,128)(2,1)S(1)} %fusion.5), channel_id=1, source_target_pairs={{0,8},{1,9},{2,10},{3,11},{4,12},{5,13},{6,14},{7,15},{8,0},{9,1},... | collective-permute-start | bytes 221192 | tf_op jit(solution)/shard_map/ppermute | solution.py:269
  29.8 6.3 %collective-permute-start.6 = (bf16[4,24,384]{2,1,0:T(8,128)(2,1)S(1)}, bf16[4,24,384]{2,1,0:T(8,128)(2,1)S(1)}, u32[]{:S(2)}, u32[]{:S(2)}) collective-permute-start(bf16[4,24,384]{2,1,0:T(8,128)(2,1)S(1)} %add_convert_fusion.1.refs_4_), channel_id=1, source_target_pairs={{0,4},{1,5},{2,6},{3,7},{4,0},{5,1},{6,2},{7,3},{8,12},{9,13},{10,... | collective-permute-start | bytes 221192 | tf_op jit(solution)/shard_map/ppermute | solution.py:269
  31.3 1.1 %collective-permute-start.4 = (s32[1,2]{1,0:T(1,128)S(1)}, s32[1,2]{1,0:T(1,128)S(1)}, u32[]{:S(2)}, u32[]{:S(2)}) collective-permute-start(s32[1,2]{1,0:T(1,128)S(1)} %copy-done.1), channel_id=1, source_target_pairs={{0,1},{1,0},{2,3},{3,2},{4,5},{5,4},{6,7},{7,6},{8,9},{9,8},{10,11... | collective-permute-start | bytes 32 | tf_op jit(solution)/shard_map/ppermute | solution.py:269
  31.4 4.7 %collective-permute-start.11 = (bf16[4,24,384]{2,1,0:T(8,128)(2,1)S(1)}, bf16[4,24,384]{2,1,0:T(8,128)(2,1)S(1)}, u32[]{:S(2)}, u32[]{:S(2)}) collective-permute-start(bf16[4,24,384]{2,1,0:T(8,128)(2,1)S(1)} %add_convert_fusion.refs_6_), channel_id=1, source_target_pairs={{0,4},{1,5},{2,6},{3,7},{4,0},{5,1},{6,2},{7,3},{8,12},{9,13},{10,... | collective-permute-start | bytes 221192 | tf_op jit(solution)/shard_map/ppermute | solution.py:269
  32.5 3.6 %collective-permute-start.5 = (s32[2,2]{1,0:T(2,128)S(1)}, s32[2,2]{1,0:T(2,128)S(1)}, u32[]{:S(2)}, u32[]{:S(2)}) collective-permute-start(s32[2,2]{1,0:T(2,128)S(1)} %pad_add_fusion), channel_id=1, source_target_pairs={{0,2},{1,3},{2,0},{3,1},{4,6},{5,7},{6,4},{7,5},{8,10},{9,11},{10,... | collective-permute-start | bytes 56 | tf_op jit(solution)/shard_map/ppermute | solution.py:269
  36.8 3.9 %collective-permute-start.15 = (bf16[1,48,384]{2,1,0:T(8,128)(2,1)S(1)}, bf16[1,48,384]{2,1,0:T(8,128)(2,1)S(1)}, u32[]{:S(2)}, u32[]{:S(2)}) collective-permute-start(bf16[1,48,384]{2,1,0:T(8,128)(2,1)S(1)} %get-tuple-element.30), channel_id=1, source_target_pairs={{0,1},{1,0},{2,3},{3,2},{4,5},{5,4},{6,7},{7,6},{8,9},{9,8},{10,11... | collective-permute-start | bytes 110600 | tf_op jit(solution)/shard_map/ppermute | solution.py:269
  36.8 4.0 %collective-permute-start.16 = (bf16[1,48,384]{2,1,0:T(8,128)(2,1)S(1)}, bf16[1,48,384]{2,1,0:T(8,128)(2,1)S(1)}, u32[]{:S(2)}, u32[]{:S(2)}) collective-permute-start(bf16[1,48,384]{2,1,0:T(8,128)(2,1)S(1)} %get-tuple-element.31), channel_id=1, source_target_pairs={{0,2},{1,3},{2,0},{3,1},{4,6},{5,7},{6,4},{7,5},{8,10},{9,11},{10,... | collective-permute-start | bytes 110600 | tf_op jit(solution)/shard_map/ppermute | solution.py:269
  38.6 3.4 %collective-permute-start.17 = (bf16[1,48,384]{2,1,0:T(8,128)(2,1)S(1)}, bf16[1,48,384]{2,1,0:T(8,128)(2,1)S(1)}, u32[]{:S(2)}, u32[]{:S(2)}) collective-permute-start(bf16[1,48,384]{2,1,0:T(8,128)(2,1)S(1)} %get-tuple-element.32), channel_id=1, source_target_pairs={{0,3},{1,2},{2,1},{3,0},{4,7},{5,6},{6,5},{7,4},{8,11},{9,10},{10,... | collective-permute-start | bytes 110600 | tf_op jit(solution)/shard_map/ppermute | solution.py:269
  38.7 4.7 %collective-permute-start.12 = (bf16[1,48,384]{2,1,0:T(8,128)(2,1)S(1)}, bf16[1,48,384]{2,1,0:T(8,128)(2,1)S(1)}, u32[]{:S(2)}, u32[]{:S(2)}) collective-permute-start(bf16[1,48,384]{2,1,0:T(8,128)(2,1)S(1)} %get-tuple-element.26), channel_id=1, source_target_pairs={{0,1},{1,0},{2,3},{3,2},{4,5},{5,4},{6,7},{7,6},{8,9},{9,8},{10,11... | collective-permute-start | bytes 110600 | tf_op jit(solution)/shard_map/ppermute | solution.py:269
  39.0 4.4 %collective-permute-start.13 = (bf16[1,48,384]{2,1,0:T(8,128)(2,1)S(1)}, bf16[1,48,384]{2,1,0:T(8,128)(2,1)S(1)}, u32[]{:S(2)}, u32[]{:S(2)}) collective-permute-start(bf16[1,48,384]{2,1,0:T(8,128)(2,1)S(1)} %get-tuple-element.27), channel_id=1, source_target_pairs={{0,2},{1,3},{2,0},{3,1},{4,6},{5,7},{6,4},{7,5},{8,10},{9,11},{10,... | collective-permute-start | bytes 110600 | tf_op jit(solution)/shard_map/ppermute | solution.py:269
  40.7 3.7 %collective-permute-start.14 = (bf16[1,48,384]{2,1,0:T(8,128)(2,1)S(1)}, bf16[1,48,384]{2,1,0:T(8,128)(2,1)S(1)}, u32[]{:S(2)}, u32[]{:S(2)}) collective-permute-start(bf16[1,48,384]{2,1,0:T(8,128)(2,1)S(1)} %get-tuple-element.28), channel_id=1, source_target_pairs={{0,3},{1,2},{2,1},{3,0},{4,7},{5,6},{6,5},{7,4},{8,11},{9,10},{10,... | collective-permute-start | bytes 110600 | tf_op jit(solution)/shard_map/ppermute | solution.py:269

commit v5 on v4

--- a/solution.py
+++ b/solution.py
@@ -117,7 +117,7 @@
     many = sum(2 if halves else 1 for _, halves in firsts)
     wanted = refs[:4]
     blocks = refs[4 : 4 + many]
-    outs = refs[4 + many : 12 + many]
+    outs = refs[4 + many : 8 + many]
     held = refs[-1]
     rows = held.shape[1]
     upper = jnp.bitwise_and(lax.shift_right_logical(lax.axis_index("sink"), 2), 1)
@@ -133,65 +133,68 @@
                     held[first : first + block.shape[0], start : start + block.shape[1], :] = block[...]
                     at += 1
 
-    for at, times in enumerate(wanted):
-        for side in range(2):
-            out = outs[4 * side + at]
-            for pair in range(out.shape[0]):
-                out[pair] = held[times[pair, side]]
+    for out, times in zip(outs, wanted):
+        for pair in range(out.shape[0]):
+            for side in range(2):
+                out[pair, side] = held[jnp.max(times[pair : pair + 1, side : side + 1])]
 
 
 def select(blocks, firsts, wanted, slices, rows):
     pairs = wanted[0].shape[0]
     both = blocks[0].shape[2]
-    shape = jax.ShapeDtypeStruct((pairs, rows, both), BF16)
+    shape = jax.ShapeDtypeStruct((pairs, 2, rows, both), BF16)
     return pl.pallas_call(
         functools.partial(select_kernel, firsts),
-        in_specs=[pl.BlockSpec(memory_space=pltpu.SMEM)] * 4
-        + [pl.BlockSpec(memory_space=pltpu.VMEM)] * len(blocks),
-        out_specs=[pl.BlockSpec(memory_space=pltpu.VMEM)] * 8,
+        in_specs=[pl.BlockSpec(memory_space=pltpu.VMEM)] * (4 + len(blocks)),
+        out_specs=[pl.BlockSpec(memory_space=pltpu.VMEM)] * 4,
         scratch_shapes=[pltpu.VMEM((slices, rows, both), BF16)],
-        out_shape=[shape] * 8,
+        out_shape=[shape] * 4,
         compiler_params=pltpu.CompilerParams(vmem_limit_bytes=8 * 1024 * 1024),
         name="select_slices",
     )(*wanted, *blocks)
 
 
-def gather_rows(pair, parts, full):
-    rows = full.shape[0] // 4
-    place = jnp.bitwise_and(lax.axis_index("sink"), 3)
-    for flip, part in enumerate(parts):
-        start = pl.multiple_of(jnp.bitwise_xor(place, flip) * rows, rows)
-        full[pl.ds(start, rows), :] = part[pair]
-
-
-def left_kernel(own, by_core, by_pair, by_both, peram, left, sink_el, left_mat):
-    width = sink_el.shape[0]
+def left_rows(pair, parts, peram, left, mat):
+    width = peram.shape[2] // 4
+    rows = parts[0].shape[2]
+    half = 2 * rows
+    for at, part in enumerate(parts):
+        band = slice(at * rows, (at + 1) * rows)
+        lower = slice(half + at * rows, half + (at + 1) * rows)
+        a_re = part[pair, 0, :, :width]
+        a_im = part[pair, 0, :, width:]
+        mat[band] = jnp.concatenate([a_re, -a_im], axis=1)
+        mat[lower] = jnp.concatenate([a_im, a_re], axis=1)
+    for a in range(4):
+        band = slice((a + 2) % 4 * width, ((a + 2) % 4 + 1) * width)
+        stacked = jnp.concatenate([peram[pair, 0, band], peram[pair, 1, band]], axis=0)
+        both = jnp.dot(mat[...], stacked, preferred_element_type=F32)
+        both = (both if a < 2 else -both).astype(BF16)
+        left[pair, 0, a] = both[:half]
+        left[pair, 1, a] = both[half:]
+
+
+def near_kernel(own, by_core, peram, left, mat):
     for pair in range(peram.shape[0]):
-        gather_rows(pair, (own, by_core, by_pair, by_both), sink_el)
-        a_re = sink_el[:, :width]
-        a_im = sink_el[:, width:]
-        left_mat[:width] = jnp.concatenate([a_re, -a_im], axis=1)
-        left_mat[width:] = jnp.concatenate([a_im, a_re], axis=1)
-        for a in range(4):
-            band = slice((a + 2) % 4 * width, ((a + 2) % 4 + 1) * width)
-            stacked = jnp.concatenate([peram[pair, 0, band], peram[pair, 1, band]], axis=0)
-            both = jnp.dot(left_mat[...], stacked, preferred_element_type=F32)
-            both = (both if a < 2 else -both).astype(BF16)
-            left[pair, 0, a * width : (a + 1) * width] = both[:width]
-            left[pair, 1, a * width : (a + 1) * width] = both[width:]
-
-
-def right_kernel(own, by_core, by_pair, by_both, left, out, src_el, right_mat, block, stored):
+        left_rows(pair, (own, by_core), peram, left, mat)
+
+
+def block_kernel(own, by_core, by_pair, by_both, near, peram, out, far, mat, src_el, right_mat, block, stored):
     width = src_el.shape[0]
     window = right_mat.shape[1] // 2
     edge = 2 * width - window
+    rows = width // 4
+    place = jnp.bitwise_and(lax.axis_index("sink"), 3)
+    starts = [pl.multiple_of(jnp.bitwise_xor(place, flip) * rows, rows) for flip in range(4)]
 
     def store(pair, a):
         band = pl.ds(a * width, width)
         return pltpu.make_async_copy(block.at[a], out.at[pair, :, band, :], stored.at[a])
 
-    for pair in range(left.shape[0]):
-        gather_rows(pair, (own, by_core, by_pair, by_both), src_el)
+    for pair in range(peram.shape[0]):
+        left_rows(pair, (by_pair, by_both), peram, far, mat)
+        for start, part in zip(starts, (own, by_core, by_pair, by_both)):
+            src_el[pl.ds(start, rows), :] = part[pair, 1]
         e_re = src_el[:, :width]
         e_im = src_el[:, width:]
         pad = jnp.zeros((width, window - width), BF16)
@@ -203,31 +206,30 @@
         right_mat[0] = jnp.concatenate([even_re, hole, even_im, hole], axis=0)
         right_mat[1] = jnp.concatenate([hole, odd_re, hole, odd_im], axis=0)
         for a in range(4):
-            band = slice(a * width, (a + 1) * width)
             results = []
             for odd in range(2):
-                starts = [b * width - odd * (window - width) for b in (2 + odd, odd)]
-                y_re = jnp.concatenate([left[pair, 0, band, at : at + window] for at in starts], axis=0)
-                y_im = jnp.concatenate([left[pair, 1, band, at : at + window] for at in starts], axis=0)
+                windows = [slice(b * width - odd * (window - width), b * width - odd * (window - width) + window) for b in (2 + odd, odd)]
+                y_re = jnp.concatenate([part[pair, 0, a, :, at] for at in windows for part in (near, far)], axis=0)
+                y_im = jnp.concatenate([part[pair, 1, a, :, at] for at in windows for part in (near, far)], axis=0)
                 results.append(dot_nt(jnp.concatenate([y_re, y_im], axis=1), right_mat[odd]))
             if pair > 0:
                 store(pair - 1, a).wait()
             for half in range(2):
                 for part in range(2):
-                    rect = slice(half * width, (half + 1) * width), slice(part * window, (part + 1) * window)
-                    even = results[0][rect]
-                    odd = results[1][rect]
+                    lanes = slice(part * window, (part + 1) * window)
                     first = 2 * half * width
-                    block[a, part, :, first : first + edge] = even[:, :edge].astype(BF16)
-                    middle = even[:, edge:] + odd[:, : window - edge]
-                    block[a, part, :, first + edge : first + window] = middle.astype(BF16)
-                    block[a, part, :, first + window : first + 2 * width] = odd[:, window - edge :].astype(BF16)
+                    for flip, start in enumerate(starts):
+                        band = slice(half * width + flip * rows, half * width + (flip + 1) * rows)
+                        even = results[0][band, lanes]
+                        odd = results[1][band, lanes]
+                        row = jnp.concatenate([even[:, :edge], even[:, edge:] + odd[:, : window - edge], odd[:, window - edge :]], axis=1)
+                        block[a, part, pl.ds(start, rows), first : first + 2 * width] = row.astype(BF16)
             store(pair, a).start()
     for a in range(4):
-        store(left.shape[0] - 1, a).wait()
-
-
-def pair_blocks(peram, sink_parts, src_parts):
+        store(peram.shape[0] - 1, a).wait()
+
+
+def pair_blocks(peram, parts):
     pairs, _, full, _ = peram.shape
     width = full // 4
     window = -(-width // 128) * 128
@@ -235,24 +237,25 @@
     cost = pl.CostEstimate(
         flops=pairs * 8 * full * full * width, bytes_accessed=pairs * 4 * full * full, transcendentals=0
     )
-    left = pl.pallas_call(
-        left_kernel,
-        in_specs=[pl.BlockSpec(memory_space=pltpu.VMEM)] * 5,
-        out_specs=pl.BlockSpec(memory_space=pltpu.VMEM),
-        scratch_shapes=[
-            pltpu.VMEM((width, 2 * width), BF16),
-            pltpu.VMEM((2 * width, 2 * width), BF16),
-        ],
-        out_shape=jax.ShapeDtypeStruct(peram.shape, BF16),
+    half = jax.ShapeDtypeStruct((pairs, 2, 4, width // 2, full), BF16)
+    in_vmem = pl.BlockSpec(memory_space=pltpu.VMEM)
+    near = pl.pallas_call(
+        near_kernel,
+        in_specs=[in_vmem] * 3,
+        out_specs=in_vmem,
+        scratch_shapes=[pltpu.VMEM((width, 2 * width), BF16)],
+        out_shape=half,
         compiler_params=params,
         cost_estimate=cost,
-        name="left_product",
-    )(*sink_parts, peram)
+        name="left_near",
+    )(*parts[:2], peram)
     return pl.pallas_call(
-        right_kernel,
-        in_specs=[pl.BlockSpec(memory_space=pltpu.VMEM)] * 5,
+        block_kernel,
+        in_specs=[in_vmem] * 6,
         out_specs=pl.BlockSpec(memory_space=pl.ANY),
         scratch_shapes=[
+            pltpu.VMEM(half.shape, BF16),
+            pltpu.VMEM((width, 2 * width), BF16),
             pltpu.VMEM((width, 2 * width), BF16),
             pltpu.VMEM((2, 2 * window, 2 * window), BF16),
             pltpu.VMEM((4, 2, width, full), BF16),
@@ -262,7 +265,7 @@
         compiler_params=params,
         cost_estimate=cost,
         name="meson_blocks",
-    )(*src_parts, left)
+    )(*parts, near, peram)
 
 
 def swap(value, flip, devices):
@@ -321,9 +324,8 @@
         firsts.append((first, halves))
         first += count
     parts = select(blocks, firsts, wanted, slices, rows)
-    sink_parts = [parts[0]] + [swap(parts[flip], flip, devices) for flip in range(1, 4)]
-    src_parts = [parts[4]] + [swap(parts[4 + flip], flip, devices) for flip in range(1, 4)]
-    return pair_blocks(peram, sink_parts, src_parts)
+    parts = [parts[0]] + [swap(parts[flip], flip, devices) for flip in range(1, 4)]
+    return pair_blocks(peram, parts)
 
 
 def solution(mesh):

time: 47.3 us -> 45.8 us (0.968)
  starting transfers between devices: 21.3 us -> 19.2 us
  waiting for transfers between devices: 12.7 us -> 13.7 us
  Pallas kernels: 12.1 us -> 11.6 us
    ppermute x18 -> x15, starting transfers between devices: 21.3 us -> 19.2 us  [swap(): return lax.ppermute(value, 'sink', [(i, i ^ flip) for i in range(devices)])]
    ppermute x18 -> x15, waiting for transfers between devices: 12.7 us -> 13.7 us  [swap(): return lax.ppermute(value, 'sink', [(i, i ^ flip) for i in range(devices)])]
  transfers between devices with their start and end apart: 18 -> 15, of which waited for: 9 -> 8; matrix products, arithmetic and copies ran while one was open for 1% -> 1% of each run, Pallas kernels for 3% -> 2%
where the time goes in v5:
time: 45.8 us; the launch traced here: 45.6 us
  starting transfers between devices  19.2 us (42%)
  waiting for transfers between devices  13.7 us (30%)
  Pallas kernels  11.6 us (25%)
  local copies, waits for them, and re-layouts  0.75 us (2%)
    ppermute x15, starting transfers between devices, swap(): return lax.ppermute(value, 'sink', [(i, i ^ flip) for i in range(devices)])  19.2 us
    ppermute x15, waiting for transfers between devices, swap(): return lax.ppermute(value, 'sink', [(i, i ^ flip) for i in range(devices)])  13.7 us
    pallas_call x1, Pallas kernels, elementals(): pl.pallas_call(functools.partial(elemental_kernel, devices, chunks, arriv...  7.3 us
    pallas_call x1, Pallas kernels, pair_blocks(): pl.pallas_call(block_kernel, in_specs=[in_vmem] * 6, out_specs=pl.BlockSp...  3.31 us
  transfers between devices with their start and end apart: 15, of which 8 were waited for; matrix products, arithmetic and copies ran while one was open for 1% of the time, Pallas kernels for 2%

profile of v5, /device:TPU:0, one launch (start us, length us, event | category | flops | bytes accessed | tf_op | source)
XLA Modules:
  0.0 45.6 jit_solution(9354048557865181970)
XLA Ops:
  0.0 0.7 %copy-done.2 = s32[3]{0:T(128)S(1)} copy-done((s32[3]{0:T(128)S(1)}, s32[3]{0:T(128)}, u32[]{:S(2)}) %copy-start.2) | copy-done | bytes 36
  0.7 7.3 %partial_elementals.1 = (f32[2,4,48,384]{3,2,1,0:T(8,128)S(1)}, bf16[2,4,48,384]{3,2,1,0:T(8,128)(2,1)S(1)}, f32[2,4,48,384]{3,2,1,0:T(8,128)S(1)}, bf16[2,4,48,384]{3,2,1,0:T(8,128)(2,1)S(1)}) custom-call(s32[1,3]{1,0:T(1,128)S(1)} %bitcast.39, bf16[8,2,3,192,512]{4,3,2,1,0:T(8,128)(2,1)} %eigvecs.1), custom_call_target="tpu_custom_call" | custom-call | flops 3623878656 | bytes 9437184 | tf_op jit(solution)/shard_map/partial_elementals/pallas_call | solution.py:95
  8.0 0.5 %collective-permute-start = (bf16[2,4,48,384]{3,2,1,0:T(8,128)(2,1)S(1)}, bf16[2,4,48,384]{3,2,1,0:T(8,128)(2,1)S(1)}, u32[]{:S(2)}, u32[]{:S(2)}) collective-permute-start(bf16[2,4,48,384]{3,2,1,0:T(8,128)(2,1)S(1)} %get-tuple-element.16), channel_id=1, source_target_pairs={{0,1},{1,0},{2,3},{3,2},{4,5},{5,4},{6,7},{7,6},{8,9},{9,8},{10,11... | collective-permute-start | bytes 884744 | tf_op jit(solution)/shard_map/ppermute | solution.py:272
  8.6 1.1 %collective-permute-done = bf16[2,4,48,384]{3,2,1,0:T(8,128)(2,1)S(1)} collective-permute-done((bf16[2,4,48,384]{3,2,1,0:T(8,128)(2,1)S(1)}, bf16[2,4,48,384]{3,2,1,0:T(8,128)(2,1)S(1)}, u32[]{:S(2)}, u32[]{:S(2)}) %collective-permute-start) | collective-permute-done | bytes 294944 | tf_op jit(solution)/shard_map/ppermute | solution.py:272
  9.8 2.9 %collective-permute-start.1 = (bf16[4,48,384]{2,1,0:T(8,128)(2,1)S(1)}, bf16[4,48,384]{2,1,0:T(8,128)(2,1)S(1)}, u32[]{:S(2)}, u32[]{:S(2)}) collective-permute-start(bf16[4,48,384]{2,1,0:T(8,128)(2,1)S(1)} %fusion.2), channel_id=1, source_target_pairs={{0,2},{1,3},{2,0},{3,1},{4,6},{5,7},{6,4},{7,5},{8,10},{9,11},{10,... | collective-permute-start | bytes 442376 | tf_op jit(solution)/shard_map/ppermute | solution.py:272
  12.8 0.3 collective-permute-start.8
  13.1 4.2 %collective-permute-done.1 = bf16[4,48,384]{2,1,0:T(8,128)(2,1)S(1)} collective-permute-done((bf16[4,48,384]{2,1,0:T(8,128)(2,1)S(1)}, bf16[4,48,384]{2,1,0:T(8,128)(2,1)S(1)}, u32[]{:S(2)}, u32[]{:S(2)}) %collective-permute-start.1) | collective-permute-done | bytes 147488 | tf_op jit(solution)/shard_map/ppermute | solution.py:272
  17.4 2.2 %collective-permute-start.2 = (bf16[4,24,384]{2,1,0:T(8,128)(2,1)S(1)}, bf16[4,24,384]{2,1,0:T(8,128)(2,1)S(1)}, u32[]{:S(2)}, u32[]{:S(2)}) collective-permute-start(bf16[4,24,384]{2,1,0:T(8,128)(2,1)S(1)} %fusion.6), channel_id=1, source_target_pairs={{0,4},{1,5},{2,6},{3,7},{4,0},{5,1},{6,2},{7,3},{8,12},{9,13},{10,... | collective-permute-start | bytes 221192 | tf_op jit(solution)/shard_map/ppermute | solution.py:272
  19.6 0.4 collective-permute-done.8
  20.1 1.9 %collective-permute-start.9 = (bf16[4,24,384]{2,1,0:T(8,128)(2,1)S(1)}, bf16[4,24,384]{2,1,0:T(8,128)(2,1)S(1)}, u32[]{:S(2)}, u32[]{:S(2)}) collective-permute-start(bf16[4,24,384]{2,1,0:T(8,128)(2,1)S(1)} %fusion.7), channel_id=1, source_target_pairs={{0,4},{1,5},{2,6},{3,7},{4,0},{5,1},{6,2},{7,3},{8,12},{9,13},{10,... | collective-permute-start | bytes 221192 | tf_op jit(solution)/shard_map/ppermute | solution.py:272
  22.0 3.2 %collective-permute-start.3 = (bf16[4,24,384]{2,1,0:T(8,128)(2,1)S(1)}, bf16[4,24,384]{2,1,0:T(8,128)(2,1)S(1)}, u32[]{:S(2)}, u32[]{:S(2)}) collective-permute-start(bf16[4,24,384]{2,1,0:T(8,128)(2,1)S(1)} %fusion.4), channel_id=1, source_target_pairs={{0,8},{1,9},{2,10},{3,11},{4,12},{5,13},{6,14},{7,15},{8,0},{9,1},... | collective-permute-start | bytes 221192 | tf_op jit(solution)/shard_map/ppermute | solution.py:272
  25.2 2.2 %collective-permute-start.10 = (bf16[4,24,384]{2,1,0:T(8,128)(2,1)S(1)}, bf16[4,24,384]{2,1,0:T(8,128)(2,1)S(1)}, u32[]{:S(2)}, u32[]{:S(2)}) collective-permute-start(bf16[4,24,384]{2,1,0:T(8,128)(2,1)S(1)} %fusion.5), channel_id=1, source_target_pairs={{0,8},{1,9},{2,10},{3,11},{4,12},{5,13},{6,14},{7,15},{8,0},{9,1},... | collective-permute-start | bytes 221192 | tf_op jit(solution)/shard_map/ppermute | solution.py:272
  27.4 2.3 %collective-permute-done.3 = bf16[4,24,384]{2,1,0:T(8,128)(2,1)S(1)} collective-permute-done((bf16[4,24,384]{2,1,0:T(8,128)(2,1)S(1)}, bf16[4,24,384]{2,1,0:T(8,128)(2,1)S(1)}, u32[]{:S(2)}, u32[]{:S(2)}) %collective-permute-start.3) | collective-permute-done | bytes 73760 | tf_op jit(solution)/shard_map/ppermute | solution.py:272
  29.8 1.5 %collective-permute-start.6 = (bf16[4,24,384]{2,1,0:T(8,128)(2,1)S(1)}, bf16[4,24,384]{2,1,0:T(8,128)(2,1)S(1)}, u32[]{:S(2)}, u32[]{:S(2)}) collective-permute-start(bf16[4,24,384]{2,1,0:T(8,128)(2,1)S(1)} %add_convert_fusion.1.refs_4_), channel_id=1, source_target_pairs={{0,4},{1,5},{2,6},{3,7},{4,0},{5,1},{6,2},{7,3},{8,12},{9,13},{10,... | collective-permute-start | bytes 221192 | tf_op jit(solution)/shard_map/ppermute | solution.py:272
  31.4 0.8 %collective-permute-start.11 = (bf16[4,24,384]{2,1,0:T(8,128)(2,1)S(1)}, bf16[4,24,384]{2,1,0:T(8,128)(2,1)S(1)}, u32[]{:S(2)}, u32[]{:S(2)}) collective-permute-start(bf16[4,24,384]{2,1,0:T(8,128)(2,1)S(1)} %add_convert_fusion.refs_6_), channel_id=1, source_target_pairs={{0,4},{1,5},{2,6},{3,7},{4,0},{5,1},{6,2},{7,3},{8,12},{9,13},{10,... | collective-permute-start | bytes 221192 | tf_op jit(solution)/shard_map/ppermute | solution.py:272
  32.2 0.2 collective-permute-done.4.refs_1_
  32.5 1.6 %collective-permute-start.5 = (s32[2,2]{1,0:T(2,128)S(1)}, s32[2,2]{1,0:T(2,128)S(1)}, u32[]{:S(2)}, u32[]{:S(2)}) collective-permute-start(s32[2,2]{1,0:T(2,128)S(1)} %pad_add_fusion), channel_id=1, source_target_pairs={{0,2},{1,3},{2,0},{3,1},{4,6},{5,7},{6,4},{7,5},{8,10},{9,11},{10,... | collective-permute-start | bytes 56 | tf_op jit(solution)/shard_map/ppermute | solution.py:272
  34.0 2.0 %collective-permute-done.5 = s32[2,2]{1,0:T(2,128)S(1)} collective-permute-done((s32[2,2]{1,0:T(2,128)S(1)}, s32[2,2]{1,0:T(2,128)S(1)}, u32[]{:S(2)}, u32[]{:S(2)}) %collective-permute-start.5) | collective-permute-done | bytes 48 | tf_op jit(solution)/shard_map/ppermute | solution.py:272
  36.1 0.2 select_slices.1
  36.4 1.7 %collective-permute-start.13 = (bf16[1,2,48,384]{3,2,1,0:T(8,128)(2,1)S(1)}, bf16[1,2,48,384]{3,2,1,0:T(8,128)(2,1)S(1)}, u32[]{:S(2)}, u32[]{:S(2)}) collective-permute-start(bf16[1,2,48,384]{3,2,1,0:T(8,128)(2,1)S(1)} %get-tuple-element.23), channel_id=1, source_target_pairs={{0,2},{1,3},{2,0},{3,1},{4,6},{5,7},{6,4},{7,5},{8,10},{9,11},{10,... | collective-permute-start | bytes 221192 | tf_op jit(solution)/shard_map/ppermute | solution.py:272
  38.2 0.8 %left_near.1.near = bf16[1,2,4,96,768]{4,3,2,1,0:T(8,128)(2,1)S(1)} custom-call(bf16[1,2,48,384]{3,2,1,0:T(8,128)(2,1)S(1)} %get-tuple-element.21.own, bf16[1,2,48,384]{3,2,1,0:T(8,128)(2,1)S(1)} %collective-permute-done.12.by_core, bf16[1,2,768,768]{3,2,1,0:T(8,128)(2,1)S(1)} %copy-done), custom_call_target="tpu_custom_call" | custom-call | flops 905969664 | bytes 2359296 | tf_op jit(solution)/shard_map/left_near/pallas_call | solution.py:242
  39.0 2.0 %collective-permute-done.13.by_pair = bf16[1,2,48,384]{3,2,1,0:T(8,128)(2,1)S(1)} collective-permute-done((bf16[1,2,48,384]{3,2,1,0:T(8,128)(2,1)S(1)}, bf16[1,2,48,384]{3,2,1,0:T(8,128)(2,1)S(1)}, u32[]{:S(2)}, u32[]{:S(2)}) %collective-permute-start.13) | collective-permute-done | bytes 73760 | tf_op jit(solution)/shard_map/ppermute | solution.py:272
  41.1 1.2 %collective-permute-done.14.by_both = bf16[1,2,48,384]{3,2,1,0:T(8,128)(2,1)S(1)} collective-permute-done((bf16[1,2,48,384]{3,2,1,0:T(8,128)(2,1)S(1)}, bf16[1,2,48,384]{3,2,1,0:T(8,128)(2,1)S(1)}, u32[]{:S(2)}, u32[]{:S(2)}) %collective-permute-start.14) | collective-permute-done | bytes 73760 | tf_op jit(solution)/shard_map/ppermute | solution.py:272
  42.3 3.3 %meson_blocks.1 = bf16[1,2,768,768]{3,2,1,0:T(8,128)(2,1)} custom-call(bf16[1,2,48,384]{3,2,1,0:T(8,128)(2,1)S(1)} %get-tuple-element.21.own, bf16[1,2,48,384]{3,2,1,0:T(8,128)(2,1)S(1)} %collective-permute-done.12.by_core, bf16[1,2,48,384]{3,2,1,0:T(8,128)(2,1)S(1)} %collective-permute-done.13.by_pair, ...), custom_call_target="tpu_custom_call" | custom-call | flops 905969664 | bytes 2359296 | tf_op jit(solution)/shard_map/meson_blocks/pallas_call | solution.py:252
  (30 shorter events, 0.7 us)
Async XLA Ops:
  0.0 0.7 %copy-start.2 = (s32[3]{0:T(128)S(1)}, s32[3]{0:T(128)}, u32[]{:S(2)}) copy-start(s32[3]{0:T(128)} %param.5) | copy-start | bytes 40
  8.0 1.7 %collective-permute-start = (bf16[2,4,48,384]{3,2,1,0:T(8,128)(2,1)S(1)}, bf16[2,4,48,384]{3,2,1,0:T(8,128)(2,1)S(1)}, u32[]{:S(2)}, u32[]{:S(2)}) collective-permute-start(bf16[2,4,48,384]{3,2,1,0:T(8,128)(2,1)S(1)} %get-tuple-element.16), channel_id=1, source_target_pairs={{0,1},{1,0},{2,3},{3,2},{4,5},{5,4},{6,7},{7,6},{8,9},{9,8},{10,11... | collective-permute-start | bytes 884744 | tf_op jit(solution)/shard_map/ppermute | solution.py:272
  8.5 4.2 %collective-permute-start.7 = (bf16[2,4,48,384]{3,2,1,0:T(8,128)(2,1)S(1)}, bf16[2,4,48,384]{3,2,1,0:T(8,128)(2,1)S(1)}, u32[]{:S(2)}, u32[]{:S(2)}) collective-permute-start(bf16[2,4,48,384]{3,2,1,0:T(8,128)(2,1)S(1)} %get-tuple-element.20), channel_id=1, source_target_pairs={{0,1},{1,0},{2,3},{3,2},{4,5},{5,4},{6,7},{7,6},{8,9},{9,8},{10,11... | collective-permute-start | bytes 884744 | tf_op jit(solution)/shard_map/ppermute | solution.py:272
  9.8 21.6 %copy-start.1 = (s32[1,2]{1,0:T(1,128)S(1)}, s32[1,2]{1,0:T(1,128)}, u32[]{:S(2)}) copy-start(s32[1,2]{1,0:T(1,128)} %refs_0_.1) | copy-start | bytes 28
  9.8 7.5 %collective-permute-start.1 = (bf16[4,48,384]{2,1,0:T(8,128)(2,1)S(1)}, bf16[4,48,384]{2,1,0:T(8,128)(2,1)S(1)}, u32[]{:S(2)}, u32[]{:S(2)}) collective-permute-start(bf16[4,48,384]{2,1,0:T(8,128)(2,1)S(1)} %fusion.2), channel_id=1, source_target_pairs={{0,2},{1,3},{2,0},{3,1},{4,6},{5,7},{6,4},{7,5},{8,10},{9,11},{10,... | collective-permute-start | bytes 442376 | tf_op jit(solution)/shard_map/ppermute | solution.py:272
  12.7 25.5 %copy-start = (bf16[1,2,768,768]{3,2,1,0:T(8,128)(2,1)S(1)}, bf16[1,2,768,768]{3,2,1,0:T(8,128)(2,1)}, u32[]{:S(2)}) copy-start(bf16[1,2,768,768]{3,2,1,0:T(8,128)(2,1)} %peram.3) | copy-start | bytes 7077892
  12.8 7.2 %collective-permute-start.8 = (bf16[4,48,384]{2,1,0:T(8,128)(2,1)S(1)}, bf16[4,48,384]{2,1,0:T(8,128)(2,1)S(1)}, u32[]{:S(2)}, u32[]{:S(2)}) collective-permute-start(bf16[4,48,384]{2,1,0:T(8,128)(2,1)S(1)} %fusion.3), channel_id=1, source_target_pairs={{0,2},{1,3},{2,0},{3,1},{4,6},{5,7},{6,4},{7,5},{8,10},{9,11},{10,... | collective-permute-start | bytes 442376 | tf_op jit(solution)/shard_map/ppermute | solution.py:272
  17.4 4.6 %collective-permute-start.2 = (bf16[4,24,384]{2,1,0:T(8,128)(2,1)S(1)}, bf16[4,24,384]{2,1,0:T(8,128)(2,1)S(1)}, u32[]{:S(2)}, u32[]{:S(2)}) collective-permute-start(bf16[4,24,384]{2,1,0:T(8,128)(2,1)S(1)} %fusion.6), channel_id=1, source_target_pairs={{0,4},{1,5},{2,6},{3,7},{4,0},{5,1},{6,2},{7,3},{8,12},{9,13},{10,... | collective-permute-start | bytes 221192 | tf_op jit(solution)/shard_map/ppermute | solution.py:272
  20.1 5.1 %collective-permute-start.9 = (bf16[4,24,384]{2,1,0:T(8,128)(2,1)S(1)}, bf16[4,24,384]{2,1,0:T(8,128)(2,1)S(1)}, u32[]{:S(2)}, u32[]{:S(2)}) collective-permute-start(bf16[4,24,384]{2,1,0:T(8,128)(2,1)S(1)} %fusion.7), channel_id=1, source_target_pairs={{0,4},{1,5},{2,6},{3,7},{4,0},{5,1},{6,2},{7,3},{8,12},{9,13},{10,... | collective-permute-start | bytes 221192 | tf_op jit(solution)/shard_map/ppermute | solution.py:272
  22.0 7.8 %collective-permute-start.3 = (bf16[4,24,384]{2,1,0:T(8,128)(2,1)S(1)}, bf16[4,24,384]{2,1,0:T(8,128)(2,1)S(1)}, u32[]{:S(2)}, u32[]{:S(2)}) collective-permute-start(bf16[4,24,384]{2,1,0:T(8,128)(2,1)S(1)} %fusion.4), channel_id=1, source_target_pairs={{0,8},{1,9},{2,10},{3,11},{4,12},{5,13},{6,14},{7,15},{8,0},{9,1},... | collective-permute-start | bytes 221192 | tf_op jit(solution)/shard_map/ppermute | solution.py:272
  25.2 6.1 %collective-permute-start.10 = (bf16[4,24,384]{2,1,0:T(8,128)(2,1)S(1)}, bf16[4,24,384]{2,1,0:T(8,128)(2,1)S(1)}, u32[]{:S(2)}, u32[]{:S(2)}) collective-permute-start(bf16[4,24,384]{2,1,0:T(8,128)(2,1)S(1)} %fusion.5), channel_id=1, source_target_pairs={{0,8},{1,9},{2,10},{3,11},{4,12},{5,13},{6,14},{7,15},{8,0},{9,1},... | collective-permute-start | bytes 221192 | tf_op jit(solution)/shard_map/ppermute | solution.py:272
  29.8 6.3 %collective-permute-start.6 = (bf16[4,24,384]{2,1,0:T(8,128)(2,1)S(1)}, bf16[4,24,384]{2,1,0:T(8,128)(2,1)S(1)}, u32[]{:S(2)}, u32[]{:S(2)}) collective-permute-start(bf16[4,24,384]{2,1,0:T(8,128)(2,1)S(1)} %add_convert_fusion.1.refs_4_), channel_id=1, source_target_pairs={{0,4},{1,5},{2,6},{3,7},{4,0},{5,1},{6,2},{7,3},{8,12},{9,13},{10,... | collective-permute-start | bytes 221192 | tf_op jit(solution)/shard_map/ppermute | solution.py:272
  31.3 1.1 %collective-permute-start.4 = (s32[1,2]{1,0:T(1,128)S(1)}, s32[1,2]{1,0:T(1,128)S(1)}, u32[]{:S(2)}, u32[]{:S(2)}) collective-permute-start(s32[1,2]{1,0:T(1,128)S(1)} %copy-done.1), channel_id=1, source_target_pairs={{0,1},{1,0},{2,3},{3,2},{4,5},{5,4},{6,7},{7,6},{8,9},{9,8},{10,11... | collective-permute-start | bytes 32 | tf_op jit(solution)/shard_map/ppermute | solution.py:272
  31.4 4.7 %collective-permute-start.11 = (bf16[4,24,384]{2,1,0:T(8,128)(2,1)S(1)}, bf16[4,24,384]{2,1,0:T(8,128)(2,1)S(1)}, u32[]{:S(2)}, u32[]{:S(2)}) collective-permute-start(bf16[4,24,384]{2,1,0:T(8,128)(2,1)S(1)} %add_convert_fusion.refs_6_), channel_id=1, source_target_pairs={{0,4},{1,5},{2,6},{3,7},{4,0},{5,1},{6,2},{7,3},{8,12},{9,13},{10,... | collective-permute-start | bytes 221192 | tf_op jit(solution)/shard_map/ppermute | solution.py:272
  32.5 3.6 %collective-permute-start.5 = (s32[2,2]{1,0:T(2,128)S(1)}, s32[2,2]{1,0:T(2,128)S(1)}, u32[]{:S(2)}, u32[]{:S(2)}) collective-permute-start(s32[2,2]{1,0:T(2,128)S(1)} %pad_add_fusion), channel_id=1, source_target_pairs={{0,2},{1,3},{2,0},{3,1},{4,6},{5,7},{6,4},{7,5},{8,10},{9,11},{10,... | collective-permute-start | bytes 56 | tf_op jit(solution)/shard_map/ppermute | solution.py:272
  36.3 1.9 %collective-permute-start.12 = (bf16[1,2,48,384]{3,2,1,0:T(8,128)(2,1)S(1)}, bf16[1,2,48,384]{3,2,1,0:T(8,128)(2,1)S(1)}, u32[]{:S(2)}, u32[]{:S(2)}) collective-permute-start(bf16[1,2,48,384]{3,2,1,0:T(8,128)(2,1)S(1)} %get-tuple-element.22), channel_id=1, source_target_pairs={{0,1},{1,0},{2,3},{3,2},{4,5},{5,4},{6,7},{7,6},{8,9},{9,8},{10,11... | collective-permute-start | bytes 221192 | tf_op jit(solution)/shard_map/ppermute | solution.py:272
  36.4 4.7 %collective-permute-start.13 = (bf16[1,2,48,384]{3,2,1,0:T(8,128)(2,1)S(1)}, bf16[1,2,48,384]{3,2,1,0:T(8,128)(2,1)S(1)}, u32[]{:S(2)}, u32[]{:S(2)}) collective-permute-start(bf16[1,2,48,384]{3,2,1,0:T(8,128)(2,1)S(1)} %get-tuple-element.23), channel_id=1, source_target_pairs={{0,2},{1,3},{2,0},{3,1},{4,6},{5,7},{6,4},{7,5},{8,10},{9,11},{10,... | collective-permute-start | bytes 221192 | tf_op jit(solution)/shard_map/ppermute | solution.py:272
  38.1 4.2 %collective-permute-start.14 = (bf16[1,2,48,384]{3,2,1,0:T(8,128)(2,1)S(1)}, bf16[1,2,48,384]{3,2,1,0:T(8,128)(2,1)S(1)}, u32[]{:S(2)}, u32[]{:S(2)}) collective-permute-start(bf16[1,2,48,384]{3,2,1,0:T(8,128)(2,1)S(1)} %get-tuple-element.24), channel_id=1, source_target_pairs={{0,3},{1,2},{2,1},{3,0},{4,7},{5,6},{6,5},{7,4},{8,11},{9,10},{10,... | collective-permute-start | bytes 221192 | tf_op jit(solution)/shard_map/ppermute | solution.py:272

commit v6 on v5

--- a/solution.py
+++ b/solution.py
@@ -113,56 +113,59 @@
     return [outs[at : at + 2] for at in range(0, len(outs), 2)]
 
 
-def select_kernel(firsts, *refs):
-    many = sum(2 if halves else 1 for _, halves in firsts)
-    wanted = refs[:4]
-    blocks = refs[4 : 4 + many]
-    outs = refs[4 + many : 8 + many]
+def select_kernel(*refs):
+    wanted = refs[:8]
+    chunks = refs[8:-5]
+    outs = refs[-5:-1]
     held = refs[-1]
-    rows = held.shape[1]
+    first = 0
+    for chunk in chunks:
+        held[first : first + chunk.shape[0]] = chunk[...]
+        first += chunk.shape[0]
+    for at, times in enumerate(wanted):
+        out = outs[at // 2]
+        for pair in range(out.shape[1]):
+            for side in range(2):
+                out[at % 2, pair, side] = held[jnp.max(times[pair : pair + 1, side : side + 1])]
+
+
+def select(chunks, wanted, slices):
+    pairs = wanted[0].shape[0]
+    _, rows, both = chunks[0].shape
+    in_vmem = pl.BlockSpec(memory_space=pltpu.VMEM)
+    return pl.pallas_call(
+        select_kernel,
+        in_specs=[in_vmem] * (8 + len(chunks)),
+        out_specs=[in_vmem] * 4,
+        scratch_shapes=[pltpu.VMEM((slices, rows, both), BF16)],
+        out_shape=[jax.ShapeDtypeStruct((2, pairs, 2, rows, both), BF16)] * 4,
+        compiler_params=pltpu.CompilerParams(vmem_limit_bytes=8 * 1024 * 1024),
+        name="select_slices",
+    )(*wanted, *chunks)
+
+
+def join_halves(parts, flips, quarters):
+    rows = parts[0].shape[3]
     upper = jnp.bitwise_and(lax.shift_right_logical(lax.axis_index("sink"), 2), 1)
     for side in range(2):
 
         @pl.when(upper == side)
         def _():
-            at = 0
-            for first, halves in firsts:
-                for flip in range(2 if halves else 1):
-                    block = blocks[at]
-                    start = (side ^ flip) * (rows // 2) if halves else 0
-                    held[first : first + block.shape[0], start : start + block.shape[1], :] = block[...]
-                    at += 1
-
-    for out, times in zip(outs, wanted):
-        for pair in range(out.shape[0]):
-            for side in range(2):
-                out[pair, side] = held[jnp.max(times[pair : pair + 1, side : side + 1])]
-
-
-def select(blocks, firsts, wanted, slices, rows):
-    pairs = wanted[0].shape[0]
-    both = blocks[0].shape[2]
-    shape = jax.ShapeDtypeStruct((pairs, 2, rows, both), BF16)
-    return pl.pallas_call(
-        functools.partial(select_kernel, firsts),
-        in_specs=[pl.BlockSpec(memory_space=pltpu.VMEM)] * (4 + len(blocks)),
-        out_specs=[pl.BlockSpec(memory_space=pltpu.VMEM)] * 4,
-        scratch_shapes=[pltpu.VMEM((slices, rows, both), BF16)],
-        out_shape=[shape] * 4,
-        compiler_params=pltpu.CompilerParams(vmem_limit_bytes=8 * 1024 * 1024),
-        name="select_slices",
-    )(*wanted, *blocks)
-
-
-def left_rows(pair, parts, peram, left, mat):
+            for at in range(len(flips)):
+                for half in range(2):
+                    part = parts[2 * at + (half ^ side)]
+                    quarters[flips[at], :, :, half * rows : (half + 1) * rows, :] = part[0]
+
+
+def left_rows(pair, quarters, flips, peram, left, mat):
     width = peram.shape[2] // 4
-    rows = parts[0].shape[2]
+    rows = quarters.shape[3]
     half = 2 * rows
-    for at, part in enumerate(parts):
+    for at, flip in enumerate(flips):
         band = slice(at * rows, (at + 1) * rows)
         lower = slice(half + at * rows, half + (at + 1) * rows)
-        a_re = part[pair, 0, :, :width]
-        a_im = part[pair, 0, :, width:]
+        a_re = quarters[flip, pair, 0, :, :width]
+        a_im = quarters[flip, pair, 0, :, width:]
         mat[band] = jnp.concatenate([a_re, -a_im], axis=1)
         mat[lower] = jnp.concatenate([a_im, a_re], axis=1)
     for a in range(4):
@@ -174,12 +177,15 @@
         left[pair, 1, a] = both[half:]
 
 
-def near_kernel(own, by_core, peram, left, mat):
+def near_kernel(own, by_z, by_core, by_z_core, peram, left, quarters, mat):
+    join_halves((own, by_z, by_core, by_z_core), (0, 1), quarters)
     for pair in range(peram.shape[0]):
-        left_rows(pair, (own, by_core), peram, left, mat)
-
-
-def block_kernel(own, by_core, by_pair, by_both, near, peram, out, far, mat, src_el, right_mat, block, stored):
+        left_rows(pair, quarters, (0, 1), peram, left, mat)
+
+
+def block_kernel(*refs):
+    parts = refs[:8]
+    near, peram, out, far, quarters, mat, src_el, right_mat, block, stored = refs[8:]
     width = src_el.shape[0]
     window = right_mat.shape[1] // 2
     edge = 2 * width - window
@@ -191,10 +197,11 @@
         band = pl.ds(a * width, width)
         return pltpu.make_async_copy(block.at[a], out.at[pair, :, band, :], stored.at[a])
 
+    join_halves(parts, (0, 1, 2, 3), quarters)
     for pair in range(peram.shape[0]):
-        left_rows(pair, (by_pair, by_both), peram, far, mat)
-        for start, part in zip(starts, (own, by_core, by_pair, by_both)):
-            src_el[pl.ds(start, rows), :] = part[pair, 1]
+        left_rows(pair, quarters, (2, 3), peram, far, mat)
+        for flip, start in enumerate(starts):
+            src_el[pl.ds(start, rows), :] = quarters[flip, pair, 1]
         e_re = src_el[:, :width]
         e_im = src_el[:, width:]
         pad = jnp.zeros((width, window - width), BF16)
@@ -237,24 +244,26 @@
     cost = pl.CostEstimate(
         flops=pairs * 8 * full * full * width, bytes_accessed=pairs * 4 * full * full, transcendentals=0
     )
+    quarters = (4, pairs, 2, width // 4, 2 * width)
     half = jax.ShapeDtypeStruct((pairs, 2, 4, width // 2, full), BF16)
     in_vmem = pl.BlockSpec(memory_space=pltpu.VMEM)
     near = pl.pallas_call(
         near_kernel,
-        in_specs=[in_vmem] * 3,
+        in_specs=[in_vmem] * 5,
         out_specs=in_vmem,
-        scratch_shapes=[pltpu.VMEM((width, 2 * width), BF16)],
+        scratch_shapes=[pltpu.VMEM(quarters, BF16), pltpu.VMEM((width, 2 * width), BF16)],
         out_shape=half,
         compiler_params=params,
         cost_estimate=cost,
         name="left_near",
-    )(*parts[:2], peram)
+    )(*parts[:4], peram)
     return pl.pallas_call(
         block_kernel,
-        in_specs=[in_vmem] * 6,
+        in_specs=[in_vmem] * 10,
         out_specs=pl.BlockSpec(memory_space=pl.ANY),
         scratch_shapes=[
             pltpu.VMEM(half.shape, BF16),
+            pltpu.VMEM(quarters, BF16),
             pltpu.VMEM((width, 2 * width), BF16),
             pltpu.VMEM((width, 2 * width), BF16),
             pltpu.VMEM((2, 2 * window, 2 * window), BF16),
@@ -272,60 +281,72 @@
     return lax.ppermute(value, "sink", [(i, i ^ flip) for i in range(devices)])
 
 
-def sum_near(keep, send, devices):
-    over_core = keep + swap(send, 1, devices).astype(F32)
-    return over_core[0] + swap(over_core[1].astype(BF16), 2, devices).astype(F32)
-
-
-def sum_far(near, flip, group, devices):
+def with_times(rows, times):
+    both = rows.shape[-1]
+    known = jnp.concatenate([time.reshape(-1) for time in times]).astype(BF16)
+    known = jnp.broadcast_to(jnp.pad(known, (0, both - known.shape[0])), (8, both))
+    return jnp.concatenate([rows.reshape(-1, both), known])
+
+
+def without_times(got, shape, many, times_shape):
+    rows = math.prod(shape[:-1])
+    times = got[rows, : many * math.prod(times_shape)].astype(jnp.int32).reshape(many, *times_shape)
+    return got[:rows].reshape(shape), [times[at] for at in range(many)]
+
+
+def sum_near(keep, send, devices, times=None):
+    if times is None:
+        over_core = keep + swap(send, 1, devices).astype(F32)
+        given = over_core[1].astype(BF16)
+        return over_core[0] + swap(given, 2, devices).astype(F32), None
+    got, other = without_times(swap(with_times(send, [times]), 1, devices), send.shape, 1, times.shape)
+    over_core = keep + got.astype(F32)
+    given = over_core[1].astype(BF16)
+    times = [times] + other
+    got = swap(with_times(given, times), 2, devices)
+    got, other = without_times(got, given.shape, 2, times[0].shape)
+    return over_core[0] + got.astype(F32), times + other
+
+
+def cut_rows(near, flip, group, devices, times=None):
     count, rows, both = near.shape
-    if 8 * flip == devices:
-        return [(near + swap(near.astype(BF16), 4 * flip, devices).astype(F32)).astype(BF16)]
     cut = near.reshape(count, 2, rows // 2, both)
     bit = jnp.bitwise_and(lax.shift_right_logical(group, flip.bit_length() - 1), 1)
     kept = lax.dynamic_index_in_dim(cut, bit, 1, keepdims=False)
     given = lax.dynamic_index_in_dim(cut, 1 - bit, 1, keepdims=False).astype(BF16)
-    kept = kept + swap(given, 4 * flip, devices).astype(F32)
-    blocks = sum_far(kept, 2 * flip, group, devices)
-    if len(blocks) == 1:
-        return blocks + [swap(blocks[0], 4 * flip, devices)]
-    other = swap(jnp.stack(blocks), 4 * flip, devices)
-    return [block for at in range(len(blocks)) for block in (blocks[at], other[at])]
+    if times is None:
+        return kept + swap(given, 4 * flip, devices).astype(F32), None
+    got = swap(with_times(given, times), 4 * flip, devices)
+    got, other = without_times(got, given.shape, len(times), times[0].shape)
+    return kept + got.astype(F32), times + other
+
+
+def sum_rest(near, flip, group, devices):
+    if 8 * flip == devices:
+        return (near + swap(near.astype(BF16), 4 * flip, devices).astype(F32)).astype(BF16)
+    kept, _ = cut_rows(near, flip, group, devices)
+    mine = sum_rest(kept, 2 * flip, group, devices)
+    other = swap(mine, 4 * flip, devices)
+    bit = jnp.bitwise_and(lax.shift_right_logical(group, flip.bit_length() - 1), 1)
+    return jnp.where(bit == 0, jnp.concatenate([mine, other], axis=1), jnp.concatenate([other, mine], axis=1))
 
 
 def shards(eigvecs, momentum, peram, times):
     devices = lax.axis_size("sink")
     group = lax.shift_right_logical(lax.axis_index("sink"), 2)
-    owners = devices // 8
-    slices, _, _, width, _ = eigvecs.shape
-    rows = width // 4
-    momentum = momentum.reshape(1, 3)
-    blocks = []
-    firsts = []
-    nears = [sum_near(keep, send, devices) for keep, send in elementals(eigvecs, momentum, devices)]
-    first = 0
-    for near in nears:
-        count = near.shape[0]
-        shared = sum_far(near, 1, group, devices)
-        if first == 0:
-            late_times, shared[0] = lax.optimization_barrier((times, shared[0]))
-            core_times = swap(late_times, 1, devices)
-            other = swap(jnp.concatenate([late_times, core_times]), 2, devices)
-            wanted = [times, core_times, other[: times.shape[0]], other[times.shape[0] :]]
-        halves = owners == 2
-        if halves:
-            blocks += shared
-        else:
-            mine = 0
-            for bit in range(owners.bit_length() - 1):
-                mine = 2 * mine + ((group >> bit) & 1)
-            shared = jnp.take(jnp.stack(shared), jnp.arange(owners) ^ mine, axis=0)
-            blocks.append(jnp.swapaxes(shared, 0, 1).reshape(count, rows, 2 * width))
-        firsts.append((first, halves))
-        first += count
-    parts = select(blocks, firsts, wanted, slices, rows)
-    parts = [parts[0]] + [swap(parts[flip], flip, devices) for flip in range(1, 4)]
-    return pair_blocks(peram, parts)
+    early, late = elementals(eigvecs, momentum.reshape(1, 3), devices)
+    early, _ = sum_near(*early, devices)
+    late, wanted = sum_near(*late, devices, times)
+    early, _ = cut_rows(early, 1, group, devices)
+    late, wanted = cut_rows(late, 1, group, devices, wanted)
+    early = sum_rest(early, 2, group, devices)
+    late = sum_rest(late, 2, group, devices)
+    chips = select([early, late], wanted, eigvecs.shape[0])
+    got = {0: chips[0]}
+    for flip in (4, 6, 2):
+        got[flip] = swap(chips[flip // 2], flip, devices)
+    over = {flip: swap(value[1:], 1, devices) for flip, value in got.items()}
+    return pair_blocks(peram, [got[0], got[4], over[0], over[4], got[2], got[6], over[2], over[6]])
 
 
 def solution(mesh):

time: 45.8 us -> 44.1 us (0.963)
  starting transfers between devices: 19.2 us -> 18 us
  waiting for transfers between devices: 13.7 us -> 12.5 us
    ppermute x15, starting transfers between devices: 19.2 us -> 18 us  [swap(): return lax.ppermute(value, 'sink', [(i, i ^ flip) for i in range(devices)])]
    ppermute x15, waiting for transfers between devices: 13.7 us -> 12.5 us  [swap(): return lax.ppermute(value, 'sink', [(i, i ^ flip) for i in range(devices)])]
  transfers between devices with their start and end apart: 15 -> 15, of which waited for: 8 -> 9; matrix products, arithmetic and copies ran while one was open for 1% -> 2% of each run, Pallas kernels for 2% -> 2%
where the time goes in v6:
time: 44.1 us; the launch traced here: 43.9 us
  starting transfers between devices  18 us (41%)
  waiting for transfers between devices  12.5 us (28%)
  Pallas kernels  11.6 us (26%)
  local copies, waits for them, and re-layouts  1.01 us (2%)
  other arithmetic  0.53 us (1%)
    ppermute x15, starting transfers between devices, swap(): return lax.ppermute(value, 'sink', [(i, i ^ flip) for i in range(devices)])  18 us
    ppermute x15, waiting for transfers between devices, swap(): return lax.ppermute(value, 'sink', [(i, i ^ flip) for i in range(devices)])  12.5 us
    pallas_call x1, Pallas kernels, elementals(): pl.pallas_call(functools.partial(elemental_kernel, devices, chunks, arriv...  7.31 us
    pallas_call x1, Pallas kernels, pair_blocks(): pl.pallas_call(block_kernel, in_specs=[in_vmem] * 10, out_specs=pl.BlockS...  3.35 us
  transfers between devices with their start and end apart: 15, of which 9 were waited for; matrix products, arithmetic and copies ran while one was open for 2% of the time, Pallas kernels for 2%

profile of v6, /device:TPU:0, one launch (start us, length us, event | category | flops | bytes accessed | tf_op | source)
XLA Modules:
  0.0 43.9 jit_solution(7582096085412384184)
XLA Ops:
  0.0 0.7 %copy-done.2 = s32[3]{0:T(128)S(1)} copy-done((s32[3]{0:T(128)S(1)}, s32[3]{0:T(128)}, u32[]{:S(2)}) %copy-start.2) | copy-done | bytes 36
  0.7 7.3 %partial_elementals.1 = (f32[2,4,48,384]{3,2,1,0:T(8,128)S(1)}, bf16[2,4,48,384]{3,2,1,0:T(8,128)(2,1)S(1)}, f32[2,4,48,384]{3,2,1,0:T(8,128)S(1)}, bf16[2,4,48,384]{3,2,1,0:T(8,128)(2,1)S(1)}) custom-call(s32[1,3]{1,0:T(1,128)S(1)} %bitcast.43, bf16[8,2,3,192,512]{4,3,2,1,0:T(8,128)(2,1)} %eigvecs.1), custom_call_target="tpu_custom_call" | custom-call | flops 3623878656 | bytes 9437184 | tf_op jit(solution)/shard_map/partial_elementals/pallas_call | solution.py:95
  8.0 0.5 %collective-permute-start.3 = (bf16[2,4,48,384]{3,2,1,0:T(8,128)(2,1)S(1)}, bf16[2,4,48,384]{3,2,1,0:T(8,128)(2,1)S(1)}, u32[]{:S(2)}, u32[]{:S(2)}) collective-permute-start(bf16[2,4,48,384]{3,2,1,0:T(8,128)(2,1)S(1)} %get-tuple-element.16), channel_id=1, source_target_pairs={{0,1},{1,0},{2,3},{3,2},{4,5},{5,4},{6,7},{7,6},{8,9},{9,8},{10,11... | collective-permute-start | bytes 884744 | tf_op jit(solution)/shard_map/ppermute | solution.py:281
  8.7 1.0 %collective-permute-done.3 = bf16[2,4,48,384]{3,2,1,0:T(8,128)(2,1)S(1)} collective-permute-done((bf16[2,4,48,384]{3,2,1,0:T(8,128)(2,1)S(1)}, bf16[2,4,48,384]{3,2,1,0:T(8,128)(2,1)S(1)}, u32[]{:S(2)}, u32[]{:S(2)}) %collective-permute-start.3) | collective-permute-done | bytes 294944 | tf_op jit(solution)/shard_map/ppermute | solution.py:281
  9.8 2.9 %collective-permute-start.4 = (bf16[4,48,384]{2,1,0:T(8,128)(2,1)S(1)}, bf16[4,48,384]{2,1,0:T(8,128)(2,1)S(1)}, u32[]{:S(2)}, u32[]{:S(2)}) collective-permute-start(bf16[4,48,384]{2,1,0:T(8,128)(2,1)S(1)} %fusion.1), channel_id=1, source_target_pairs={{0,2},{1,3},{2,0},{3,1},{4,6},{5,7},{6,4},{7,5},{8,10},{9,11},{10,... | collective-permute-start | bytes 442376 | tf_op jit(solution)/shard_map/ppermute | solution.py:281
  13.0 0.3 collective-permute-start.1
  13.4 4.0 %collective-permute-done.4 = bf16[4,48,384]{2,1,0:T(8,128)(2,1)S(1)} collective-permute-done((bf16[4,48,384]{2,1,0:T(8,128)(2,1)S(1)}, bf16[4,48,384]{2,1,0:T(8,128)(2,1)S(1)}, u32[]{:S(2)}, u32[]{:S(2)}) %collective-permute-start.4) | collective-permute-done | bytes 147488 | tf_op jit(solution)/shard_map/ppermute | solution.py:281
  17.4 2.2 %collective-permute-start.5 = (bf16[4,24,384]{2,1,0:T(8,128)(2,1)S(1)}, bf16[4,24,384]{2,1,0:T(8,128)(2,1)S(1)}, u32[]{:S(2)}, u32[]{:S(2)}) collective-permute-start(bf16[4,24,384]{2,1,0:T(8,128)(2,1)S(1)} %fusion.4), channel_id=1, source_target_pairs={{0,4},{1,5},{2,6},{3,7},{4,0},{5,1},{6,2},{7,3},{8,12},{9,13},{10,... | collective-permute-start | bytes 221192 | tf_op jit(solution)/shard_map/ppermute | solution.py:281
  19.6 0.5 %collective-permute-done.1 = bf16[200,384]{1,0:T(8,128)(2,1)S(1)} collective-permute-done((bf16[200,384]{1,0:T(8,128)(2,1)S(1)}, bf16[200,384]{1,0:T(8,128)(2,1)S(1)}, u32[]{:S(2)}, u32[]{:S(2)}) %collective-permute-start.1) | collective-permute-done | bytes 153632 | tf_op jit(solution)/shard_map/ppermute | solution.py:281
  20.4 1.9 %collective-permute-start.2 = (bf16[104,384]{1,0:T(8,128)(2,1)S(1)}, bf16[104,384]{1,0:T(8,128)(2,1)S(1)}, u32[]{:S(2)}, u32[]{:S(2)}) collective-permute-start(bf16[104,384]{1,0:T(8,128)(2,1)S(1)} %pad_maximum_fusion.2), channel_id=1, source_target_pairs={{0,4},{1,5},{2,6},{3,7},{4,0},{5,1},{6,2},{7,3},{8,12},{9,13},{10,... | collective-permute-start | bytes 239624 | tf_op jit(solution)/shard_map/ppermute | solution.py:281
  22.4 2.7 %collective-permute-start.6 = (bf16[4,24,384]{2,1,0:T(8,128)(2,1)S(1)}, bf16[4,24,384]{2,1,0:T(8,128)(2,1)S(1)}, u32[]{:S(2)}, u32[]{:S(2)}) collective-permute-start(bf16[4,24,384]{2,1,0:T(8,128)(2,1)S(1)} %fusion.2), channel_id=1, source_target_pairs={{0,8},{1,9},{2,10},{3,11},{4,12},{5,13},{6,14},{7,15},{8,0},{9,1},... | collective-permute-start | bytes 221192 | tf_op jit(solution)/shard_map/ppermute | solution.py:281
  25.2 2.7 %collective-permute-start.7 = (bf16[4,24,384]{2,1,0:T(8,128)(2,1)S(1)}, bf16[4,24,384]{2,1,0:T(8,128)(2,1)S(1)}, u32[]{:S(2)}, u32[]{:S(2)}) collective-permute-start(bf16[4,24,384]{2,1,0:T(8,128)(2,1)S(1)} %fusion.3), channel_id=1, source_target_pairs={{0,8},{1,9},{2,10},{3,11},{4,12},{5,13},{6,14},{7,15},{8,0},{9,1},... | collective-permute-start | bytes 221192 | tf_op jit(solution)/shard_map/ppermute | solution.py:281
  27.9 0.1 collective-permute-done.6
  28.1 2.8 %collective-permute-done.7 = bf16[4,24,384]{2,1,0:T(8,128)(2,1)S(1)} collective-permute-done((bf16[4,24,384]{2,1,0:T(8,128)(2,1)S(1)}, bf16[4,24,384]{2,1,0:T(8,128)(2,1)S(1)}, u32[]{:S(2)}, u32[]{:S(2)}) %collective-permute-start.7) | collective-permute-done | bytes 73760 | tf_op jit(solution)/shard_map/ppermute | solution.py:281
  31.0 1.6 %collective-permute-start.8 = (bf16[2,1,2,24,384]{4,3,2,1,0:T(8,128)(2,1)S(1)}, bf16[2,1,2,24,384]{4,3,2,1,0:T(8,128)(2,1)S(1)}, u32[]{:S(2)}, u32[]{:S(2)}) collective-permute-start(bf16[2,1,2,24,384]{4,3,2,1,0:T(8,128)(2,1)S(1)} %get-tuple-element.18), channel_id=1, source_target_pairs={{0,4},{1,5},{2,6},{3,7},{4,0},{5,1},{6,2},{7,3},{8,12},{9,13},{10,... | collective-permute-start | bytes 221192 | tf_op jit(solution)/shard_map/ppermute | solution.py:281
  32.6 1.5 %collective-permute-start.11 = (bf16[2,1,2,24,384]{4,3,2,1,0:T(8,128)(2,1)S(1)}, bf16[2,1,2,24,384]{4,3,2,1,0:T(8,128)(2,1)S(1)}, u32[]{:S(2)}, u32[]{:S(2)}) collective-permute-start(bf16[2,1,2,24,384]{4,3,2,1,0:T(8,128)(2,1)S(1)} %get-tuple-element.19), channel_id=1, source_target_pairs={{0,2},{1,3},{2,0},{3,1},{4,6},{5,7},{6,4},{7,5},{8,10},{9,11},{10,... | collective-permute-start | bytes 221192 | tf_op jit(solution)/shard_map/ppermute | solution.py:281
  34.1 1.1 %collective-permute-start.12 = (bf16[2,1,2,24,384]{4,3,2,1,0:T(8,128)(2,1)S(1)}, bf16[2,1,2,24,384]{4,3,2,1,0:T(8,128)(2,1)S(1)}, u32[]{:S(2)}, u32[]{:S(2)}) collective-permute-start(bf16[2,1,2,24,384]{4,3,2,1,0:T(8,128)(2,1)S(1)} %get-tuple-element.20), channel_id=1, source_target_pairs={{0,6},{1,7},{2,4},{3,5},{4,2},{5,3},{6,0},{7,1},{8,14},{9,15},{10,... | collective-permute-start | bytes 221192 | tf_op jit(solution)/shard_map/ppermute | solution.py:281
  35.3 0.2 collective-permute-done.8.by_z.refs_1_
  35.4 0.4 collective-permute-start.10
  35.8 1.9 %collective-permute-done.11.refs_4_ = bf16[2,1,2,24,384]{4,3,2,1,0:T(8,128)(2,1)S(1)} collective-permute-done((bf16[2,1,2,24,384]{4,3,2,1,0:T(8,128)(2,1)S(1)}, bf16[2,1,2,24,384]{4,3,2,1,0:T(8,128)(2,1)S(1)}, u32[]{:S(2)}, u32[]{:S(2)}) %collective-permute-start.11) | collective-permute-done | bytes 73760 | tf_op jit(solution)/shard_map/ppermute | solution.py:281
  37.8 1.6 %collective-permute-done.12.refs_5_ = bf16[2,1,2,24,384]{4,3,2,1,0:T(8,128)(2,1)S(1)} collective-permute-done((bf16[2,1,2,24,384]{4,3,2,1,0:T(8,128)(2,1)S(1)}, bf16[2,1,2,24,384]{4,3,2,1,0:T(8,128)(2,1)S(1)}, u32[]{:S(2)}, u32[]{:S(2)}) %collective-permute-start.12) | collective-permute-done | bytes 73760 | tf_op jit(solution)/shard_map/ppermute | solution.py:281
  39.4 0.8 %left_near.1.refs_8_ = bf16[1,2,4,96,768]{4,3,2,1,0:T(8,128)(2,1)S(1)} custom-call(bf16[2,1,2,24,384]{4,3,2,1,0:T(8,128)(2,1)S(1)} %get-tuple-element.17.own.refs_0_, bf16[2,1,2,24,384]{4,3,2,1,0:T(8,128)(2,1)S(1)} %collective-permute-done.8.by_z.refs_1_, bf16[1,1,2,24,384]{4,3,2,1,0:T(8,128)(2,1)S(1)} %collective-permute-done.9.by_core.refs_2_, ...), custom_call_target="tpu_custom_call" | custom-call | flops 905969664 | bytes 2359296 | tf_op jit(solution)/shard_map/left_near/pallas_call | solution.py:250
  40.2 0.3 collective-permute-done.14.refs_7_
  40.6 3.3 %meson_blocks.1 = bf16[1,2,768,768]{3,2,1,0:T(8,128)(2,1)} custom-call(bf16[2,1,2,24,384]{4,3,2,1,0:T(8,128)(2,1)S(1)} %get-tuple-element.17.own.refs_0_, bf16[2,1,2,24,384]{4,3,2,1,0:T(8,128)(2,1)S(1)} %collective-permute-done.8.by_z.refs_1_, bf16[1,1,2,24,384]{4,3,2,1,0:T(8,128)(2,1)S(1)} %collective-permute-done.9.by_core.refs_2_, ...), custom_call_target="tpu_custom_call" | custom-call | flops 905969664 | bytes 2359296 | tf_op jit(solution)/shard_map/meson_blocks/pallas_call | solution.py:260
  (51 shorter events, 1.2 us)
Async XLA Ops:
  0.0 0.7 %copy-start.2 = (s32[3]{0:T(128)S(1)}, s32[3]{0:T(128)}, u32[]{:S(2)}) copy-start(s32[3]{0:T(128)} %param.5) | copy-start | bytes 40
  0.7 7.9 %copy-start.1 = (s32[1,2]{1,0:T(1,128)S(1)}, s32[1,2]{1,0:T(1,128)}, u32[]{:S(2)}) copy-start(s32[1,2]{1,0:T(1,128)} %refs_0_.1) | copy-start | bytes 28
  8.0 1.7 %collective-permute-start.3 = (bf16[2,4,48,384]{3,2,1,0:T(8,128)(2,1)S(1)}, bf16[2,4,48,384]{3,2,1,0:T(8,128)(2,1)S(1)}, u32[]{:S(2)}, u32[]{:S(2)}) collective-permute-start(bf16[2,4,48,384]{3,2,1,0:T(8,128)(2,1)S(1)} %get-tuple-element.16), channel_id=1, source_target_pairs={{0,1},{1,0},{2,3},{3,2},{4,5},{5,4},{6,7},{7,6},{8,9},{9,8},{10,11... | collective-permute-start | bytes 884744 | tf_op jit(solution)/shard_map/ppermute | solution.py:281
  8.6 4.2 %collective-permute-start = (bf16[392,384]{1,0:T(8,128)(2,1)S(1)}, bf16[392,384]{1,0:T(8,128)(2,1)S(1)}, u32[]{:S(2)}, u32[]{:S(2)}) collective-permute-start(bf16[392,384]{1,0:T(8,128)(2,1)S(1)} %pad_maximum_fusion), channel_id=1, source_target_pairs={{0,1},{1,0},{2,3},{3,2},{4,5},{5,4},{6,7},{7,6},{8,9},{9,8},{10,11... | collective-permute-start | bytes 903176 | tf_op jit(solution)/shard_map/ppermute | solution.py:281
  9.8 7.5 %collective-permute-start.4 = (bf16[4,48,384]{2,1,0:T(8,128)(2,1)S(1)}, bf16[4,48,384]{2,1,0:T(8,128)(2,1)S(1)}, u32[]{:S(2)}, u32[]{:S(2)}) collective-permute-start(bf16[4,48,384]{2,1,0:T(8,128)(2,1)S(1)} %fusion.1), channel_id=1, source_target_pairs={{0,2},{1,3},{2,0},{3,1},{4,6},{5,7},{6,4},{7,5},{8,10},{9,11},{10,... | collective-permute-start | bytes 442376 | tf_op jit(solution)/shard_map/ppermute | solution.py:281
  13.0 26.4 %copy-start = (bf16[1,2,768,768]{3,2,1,0:T(8,128)(2,1)S(1)}, bf16[1,2,768,768]{3,2,1,0:T(8,128)(2,1)}, u32[]{:S(2)}) copy-start(bf16[1,2,768,768]{3,2,1,0:T(8,128)(2,1)} %refs_9_.1) | copy-start | bytes 7077892
  13.0 7.1 %collective-permute-start.1 = (bf16[200,384]{1,0:T(8,128)(2,1)S(1)}, bf16[200,384]{1,0:T(8,128)(2,1)S(1)}, u32[]{:S(2)}, u32[]{:S(2)}) collective-permute-start(bf16[200,384]{1,0:T(8,128)(2,1)S(1)} %pad_maximum_fusion.1), channel_id=1, source_target_pairs={{0,2},{1,3},{2,0},{3,1},{4,6},{5,7},{6,4},{7,5},{8,10},{9,11},{10,... | collective-permute-start | bytes 460808 | tf_op jit(solution)/shard_map/ppermute | solution.py:281
  17.4 4.9 %collective-permute-start.5 = (bf16[4,24,384]{2,1,0:T(8,128)(2,1)S(1)}, bf16[4,24,384]{2,1,0:T(8,128)(2,1)S(1)}, u32[]{:S(2)}, u32[]{:S(2)}) collective-permute-start(bf16[4,24,384]{2,1,0:T(8,128)(2,1)S(1)} %fusion.4), channel_id=1, source_target_pairs={{0,4},{1,5},{2,6},{3,7},{4,0},{5,1},{6,2},{7,3},{8,12},{9,13},{10,... | collective-permute-start | bytes 221192 | tf_op jit(solution)/shard_map/ppermute | solution.py:281
  20.4 4.6 %collective-permute-start.2 = (bf16[104,384]{1,0:T(8,128)(2,1)S(1)}, bf16[104,384]{1,0:T(8,128)(2,1)S(1)}, u32[]{:S(2)}, u32[]{:S(2)}) collective-permute-start(bf16[104,384]{1,0:T(8,128)(2,1)S(1)} %pad_maximum_fusion.2), channel_id=1, source_target_pairs={{0,4},{1,5},{2,6},{3,7},{4,0},{5,1},{6,2},{7,3},{8,12},{9,13},{10,... | collective-permute-start | bytes 239624 | tf_op jit(solution)/shard_map/ppermute | solution.py:281
  22.4 5.7 %collective-permute-start.6 = (bf16[4,24,384]{2,1,0:T(8,128)(2,1)S(1)}, bf16[4,24,384]{2,1,0:T(8,128)(2,1)S(1)}, u32[]{:S(2)}, u32[]{:S(2)}) collective-permute-start(bf16[4,24,384]{2,1,0:T(8,128)(2,1)S(1)} %fusion.2), channel_id=1, source_target_pairs={{0,8},{1,9},{2,10},{3,11},{4,12},{5,13},{6,14},{7,15},{8,0},{9,1},... | collective-permute-start | bytes 221192 | tf_op jit(solution)/shard_map/ppermute | solution.py:281
  25.2 5.6 %collective-permute-start.7 = (bf16[4,24,384]{2,1,0:T(8,128)(2,1)S(1)}, bf16[4,24,384]{2,1,0:T(8,128)(2,1)S(1)}, u32[]{:S(2)}, u32[]{:S(2)}) collective-permute-start(bf16[4,24,384]{2,1,0:T(8,128)(2,1)S(1)} %fusion.3), channel_id=1, source_target_pairs={{0,8},{1,9},{2,10},{3,11},{4,12},{5,13},{6,14},{7,15},{8,0},{9,1},... | collective-permute-start | bytes 221192 | tf_op jit(solution)/shard_map/ppermute | solution.py:281
  31.0 4.4 %collective-permute-start.8 = (bf16[2,1,2,24,384]{4,3,2,1,0:T(8,128)(2,1)S(1)}, bf16[2,1,2,24,384]{4,3,2,1,0:T(8,128)(2,1)S(1)}, u32[]{:S(2)}, u32[]{:S(2)}) collective-permute-start(bf16[2,1,2,24,384]{4,3,2,1,0:T(8,128)(2,1)S(1)} %get-tuple-element.18), channel_id=1, source_target_pairs={{0,4},{1,5},{2,6},{3,7},{4,0},{5,1},{6,2},{7,3},{8,12},{9,13},{10,... | collective-permute-start | bytes 221192 | tf_op jit(solution)/shard_map/ppermute | solution.py:281
  32.6 5.1 %collective-permute-start.11 = (bf16[2,1,2,24,384]{4,3,2,1,0:T(8,128)(2,1)S(1)}, bf16[2,1,2,24,384]{4,3,2,1,0:T(8,128)(2,1)S(1)}, u32[]{:S(2)}, u32[]{:S(2)}) collective-permute-start(bf16[2,1,2,24,384]{4,3,2,1,0:T(8,128)(2,1)S(1)} %get-tuple-element.19), channel_id=1, source_target_pairs={{0,2},{1,3},{2,0},{3,1},{4,6},{5,7},{6,4},{7,5},{8,10},{9,11},{10,... | collective-permute-start | bytes 221192 | tf_op jit(solution)/shard_map/ppermute | solution.py:281
  34.1 5.3 %collective-permute-start.12 = (bf16[2,1,2,24,384]{4,3,2,1,0:T(8,128)(2,1)S(1)}, bf16[2,1,2,24,384]{4,3,2,1,0:T(8,128)(2,1)S(1)}, u32[]{:S(2)}, u32[]{:S(2)}) collective-permute-start(bf16[2,1,2,24,384]{4,3,2,1,0:T(8,128)(2,1)S(1)} %get-tuple-element.20), channel_id=1, source_target_pairs={{0,6},{1,7},{2,4},{3,5},{4,2},{5,3},{6,0},{7,1},{8,14},{9,15},{10,... | collective-permute-start | bytes 221192 | tf_op jit(solution)/shard_map/ppermute | solution.py:281
  35.3 4.1 %collective-permute-start.9 = (bf16[1,1,2,24,384]{4,3,2,1,0:T(8,128)(2,1)S(1)}, bf16[1,1,2,24,384]{4,3,2,1,0:T(8,128)(2,1)S(1)}, u32[]{:S(2)}, u32[]{:S(2)}) collective-permute-start(bf16[1,1,2,24,384]{4,3,2,1,0:T(8,128)(2,1)S(1)} %slice.91), channel_id=1, source_target_pairs={{0,1},{1,0},{2,3},{3,2},{4,5},{5,4},{6,7},{7,6},{8,9},{9,8},{10,11... | collective-permute-start | bytes 110600 | tf_op jit(solution)/shard_map/ppermute | solution.py:281
  35.4 4.0 %collective-permute-start.10 = (bf16[1,1,2,24,384]{4,3,2,1,0:T(8,128)(2,1)S(1)}, bf16[1,1,2,24,384]{4,3,2,1,0:T(8,128)(2,1)S(1)}, u32[]{:S(2)}, u32[]{:S(2)}) collective-permute-start(bf16[1,1,2,24,384]{4,3,2,1,0:T(8,128)(2,1)S(1)} %slice.105), channel_id=1, source_target_pairs={{0,1},{1,0},{2,3},{3,2},{4,5},{5,4},{6,7},{7,6},{8,9},{9,8},{10,11... | collective-permute-start | bytes 110600 | tf_op jit(solution)/shard_map/ppermute | solution.py:281
  37.8 2.5 %collective-permute-start.13 = (bf16[1,1,2,24,384]{4,3,2,1,0:T(8,128)(2,1)S(1)}, bf16[1,1,2,24,384]{4,3,2,1,0:T(8,128)(2,1)S(1)}, u32[]{:S(2)}, u32[]{:S(2)}) collective-permute-start(bf16[1,1,2,24,384]{4,3,2,1,0:T(8,128)(2,1)S(1)} %slice.106), channel_id=1, source_target_pairs={{0,1},{1,0},{2,3},{3,2},{4,5},{5,4},{6,7},{7,6},{8,9},{9,8},{10,11... | collective-permute-start | bytes 110600 | tf_op jit(solution)/shard_map/ppermute | solution.py:281
  39.4 1.2 %collective-permute-start.14 = (bf16[1,1,2,24,384]{4,3,2,1,0:T(8,128)(2,1)S(1)}, bf16[1,1,2,24,384]{4,3,2,1,0:T(8,128)(2,1)S(1)}, u32[]{:S(2)}, u32[]{:S(2)}) collective-permute-start(bf16[1,1,2,24,384]{4,3,2,1,0:T(8,128)(2,1)S(1)} %slice.107), channel_id=1, source_target_pairs={{0,1},{1,0},{2,3},{3,2},{4,5},{5,4},{6,7},{7,6},{8,9},{9,8},{10,11... | collective-permute-start | bytes 110600 | tf_op jit(solution)/shard_map/ppermute | solution.py:281

commit v7 on v6

--- a/solution.py
+++ b/solution.py
@@ -177,15 +177,15 @@
         left[pair, 1, a] = both[half:]
 
 
-def near_kernel(own, by_z, by_core, by_z_core, peram, left, quarters, mat):
-    join_halves((own, by_z, by_core, by_z_core), (0, 1), quarters)
+def across_kernel(by_both, by_x, by_both_core, by_x_core, peram, left, quarters, mat):
+    join_halves((by_x, by_both, by_x_core, by_both_core), (2, 3), quarters)
     for pair in range(peram.shape[0]):
-        left_rows(pair, quarters, (0, 1), peram, left, mat)
+        left_rows(pair, quarters, (2, 3), peram, left, mat)
 
 
 def block_kernel(*refs):
-    parts = refs[:8]
-    near, peram, out, far, quarters, mat, src_el, right_mat, block, stored = refs[8:]
+    parts = [refs[at] for at in (6, 2, 7, 5, 1, 0, 4, 3)]
+    far, peram, out, near, quarters, mat, src_el, right_mat, block, stored = refs[8:]
     width = src_el.shape[0]
     window = right_mat.shape[1] // 2
     edge = 2 * width - window
@@ -199,7 +199,7 @@
 
     join_halves(parts, (0, 1, 2, 3), quarters)
     for pair in range(peram.shape[0]):
-        left_rows(pair, quarters, (2, 3), peram, far, mat)
+        left_rows(pair, quarters, (0, 1), peram, near, mat)
         for flip, start in enumerate(starts):
             src_el[pl.ds(start, rows), :] = quarters[flip, pair, 1]
         e_re = src_el[:, :width]
@@ -247,16 +247,16 @@
     quarters = (4, pairs, 2, width // 4, 2 * width)
     half = jax.ShapeDtypeStruct((pairs, 2, 4, width // 2, full), BF16)
     in_vmem = pl.BlockSpec(memory_space=pltpu.VMEM)
-    near = pl.pallas_call(
-        near_kernel,
+    far = pl.pallas_call(
+        across_kernel,
         in_specs=[in_vmem] * 5,
         out_specs=in_vmem,
         scratch_shapes=[pltpu.VMEM(quarters, BF16), pltpu.VMEM((width, 2 * width), BF16)],
         out_shape=half,
         compiler_params=params,
         cost_estimate=cost,
-        name="left_near",
-    )(*parts[:4], peram)
+        name="left_across",
+    )(*[parts[at] for at in (5, 4, 7, 6)], peram)
     return pl.pallas_call(
         block_kernel,
         in_specs=[in_vmem] * 10,
@@ -274,7 +274,7 @@
         compiler_params=params,
         cost_estimate=cost,
         name="meson_blocks",
-    )(*parts, near, peram)
+    )(*[parts[at] for at in (5, 4, 1, 7, 6, 3, 0, 2)], far, peram)
 
 
 def swap(value, flip, devices):

time: 44.1 us -> 43.5 us (0.986)
  waiting for transfers between devices: 12.5 us -> 11.7 us
    ppermute x15, waiting for transfers between devices: 12.5 us -> 11.7 us  [swap(): return lax.ppermute(value, 'sink', [(i, i ^ flip) for i in range(devices)])]
  transfers between devices with their start and end apart: 15 -> 15, of which waited for: 9 -> 8; matrix products, arithmetic and copies ran while one was open for 2% -> 2% of each run, Pallas kernels for 2% -> 2%
where the time goes in v7:
time: 43.5 us; the launch traced here: 43.3 us
  starting transfers between devices  18.3 us (42%)
  waiting for transfers between devices  11.7 us (27%)
  Pallas kernels  11.6 us (27%)
  local copies, waits for them, and re-layouts  1.01 us (2%)
  other arithmetic  0.53 us (1%)
    ppermute x15, starting transfers between devices, swap(): return lax.ppermute(value, 'sink', [(i, i ^ flip) for i in range(devices)])  18.3 us
    ppermute x15, waiting for transfers between devices, swap(): return lax.ppermute(value, 'sink', [(i, i ^ flip) for i in range(devices)])  11.7 us
    pallas_call x1, Pallas kernels, elementals(): pl.pallas_call(functools.partial(elemental_kernel, devices, chunks, arriv...  7.31 us
    pallas_call x1, Pallas kernels, pair_blocks(): pl.pallas_call(block_kernel, in_specs=[in_vmem] * 10, out_specs=pl.BlockS...  3.36 us
  transfers between devices with their start and end apart: 15, of which 8 were waited for; matrix products, arithmetic and copies ran while one was open for 2% of the time, Pallas kernels for 2%

profile of v7, /device:TPU:0, one launch (start us, length us, event | category | flops | bytes accessed | tf_op | source)
XLA Modules:
  0.0 43.3 jit_solution(8467114811141942085)
XLA Ops:
  0.0 0.7 %copy-done.2 = s32[3]{0:T(128)S(1)} copy-done((s32[3]{0:T(128)S(1)}, s32[3]{0:T(128)}, u32[]{:S(2)}) %copy-start.2) | copy-done | bytes 36
  0.7 7.3 %partial_elementals.1 = (f32[2,4,48,384]{3,2,1,0:T(8,128)S(1)}, bf16[2,4,48,384]{3,2,1,0:T(8,128)(2,1)S(1)}, f32[2,4,48,384]{3,2,1,0:T(8,128)S(1)}, bf16[2,4,48,384]{3,2,1,0:T(8,128)(2,1)S(1)}) custom-call(s32[1,3]{1,0:T(1,128)S(1)} %bitcast.43, bf16[8,2,3,192,512]{4,3,2,1,0:T(8,128)(2,1)} %eigvecs.1), custom_call_target="tpu_custom_call" | custom-call | flops 3623878656 | bytes 9437184 | tf_op jit(solution)/shard_map/partial_elementals/pallas_call | solution.py:95
  8.0 0.5 %collective-permute-start.3 = (bf16[2,4,48,384]{3,2,1,0:T(8,128)(2,1)S(1)}, bf16[2,4,48,384]{3,2,1,0:T(8,128)(2,1)S(1)}, u32[]{:S(2)}, u32[]{:S(2)}) collective-permute-start(bf16[2,4,48,384]{3,2,1,0:T(8,128)(2,1)S(1)} %get-tuple-element.16), channel_id=1, source_target_pairs={{0,1},{1,0},{2,3},{3,2},{4,5},{5,4},{6,7},{7,6},{8,9},{9,8},{10,11... | collective-permute-start | bytes 884744 | tf_op jit(solution)/shard_map/ppermute | solution.py:281
  8.7 1.0 %collective-permute-done.3 = bf16[2,4,48,384]{3,2,1,0:T(8,128)(2,1)S(1)} collective-permute-done((bf16[2,4,48,384]{3,2,1,0:T(8,128)(2,1)S(1)}, bf16[2,4,48,384]{3,2,1,0:T(8,128)(2,1)S(1)}, u32[]{:S(2)}, u32[]{:S(2)}) %collective-permute-start.3) | collective-permute-done | bytes 294944 | tf_op jit(solution)/shard_map/ppermute | solution.py:281
  9.8 2.9 %collective-permute-start.4 = (bf16[4,48,384]{2,1,0:T(8,128)(2,1)S(1)}, bf16[4,48,384]{2,1,0:T(8,128)(2,1)S(1)}, u32[]{:S(2)}, u32[]{:S(2)}) collective-permute-start(bf16[4,48,384]{2,1,0:T(8,128)(2,1)S(1)} %fusion.1), channel_id=1, source_target_pairs={{0,2},{1,3},{2,0},{3,1},{4,6},{5,7},{6,4},{7,5},{8,10},{9,11},{10,... | collective-permute-start | bytes 442376 | tf_op jit(solution)/shard_map/ppermute | solution.py:281
  13.0 0.3 collective-permute-start.1
  13.4 4.0 %collective-permute-done.4 = bf16[4,48,384]{2,1,0:T(8,128)(2,1)S(1)} collective-permute-done((bf16[4,48,384]{2,1,0:T(8,128)(2,1)S(1)}, bf16[4,48,384]{2,1,0:T(8,128)(2,1)S(1)}, u32[]{:S(2)}, u32[]{:S(2)}) %collective-permute-start.4) | collective-permute-done | bytes 147488 | tf_op jit(solution)/shard_map/ppermute | solution.py:281
  17.4 2.2 %collective-permute-start.5 = (bf16[4,24,384]{2,1,0:T(8,128)(2,1)S(1)}, bf16[4,24,384]{2,1,0:T(8,128)(2,1)S(1)}, u32[]{:S(2)}, u32[]{:S(2)}) collective-permute-start(bf16[4,24,384]{2,1,0:T(8,128)(2,1)S(1)} %fusion.4), channel_id=1, source_target_pairs={{0,4},{1,5},{2,6},{3,7},{4,0},{5,1},{6,2},{7,3},{8,12},{9,13},{10,... | collective-permute-start | bytes 221192 | tf_op jit(solution)/shard_map/ppermute | solution.py:281
  19.6 0.5 %collective-permute-done.1 = bf16[200,384]{1,0:T(8,128)(2,1)S(1)} collective-permute-done((bf16[200,384]{1,0:T(8,128)(2,1)S(1)}, bf16[200,384]{1,0:T(8,128)(2,1)S(1)}, u32[]{:S(2)}, u32[]{:S(2)}) %collective-permute-start.1) | collective-permute-done | bytes 153632 | tf_op jit(solution)/shard_map/ppermute | solution.py:281
  20.4 1.9 %collective-permute-start.2 = (bf16[104,384]{1,0:T(8,128)(2,1)S(1)}, bf16[104,384]{1,0:T(8,128)(2,1)S(1)}, u32[]{:S(2)}, u32[]{:S(2)}) collective-permute-start(bf16[104,384]{1,0:T(8,128)(2,1)S(1)} %pad_maximum_fusion.2), channel_id=1, source_target_pairs={{0,4},{1,5},{2,6},{3,7},{4,0},{5,1},{6,2},{7,3},{8,12},{9,13},{10,... | collective-permute-start | bytes 239624 | tf_op jit(solution)/shard_map/ppermute | solution.py:281
  22.4 2.7 %collective-permute-start.6 = (bf16[4,24,384]{2,1,0:T(8,128)(2,1)S(1)}, bf16[4,24,384]{2,1,0:T(8,128)(2,1)S(1)}, u32[]{:S(2)}, u32[]{:S(2)}) collective-permute-start(bf16[4,24,384]{2,1,0:T(8,128)(2,1)S(1)} %fusion.2), channel_id=1, source_target_pairs={{0,8},{1,9},{2,10},{3,11},{4,12},{5,13},{6,14},{7,15},{8,0},{9,1},... | collective-permute-start | bytes 221192 | tf_op jit(solution)/shard_map/ppermute | solution.py:281
  25.2 2.7 %collective-permute-start.7 = (bf16[4,24,384]{2,1,0:T(8,128)(2,1)S(1)}, bf16[4,24,384]{2,1,0:T(8,128)(2,1)S(1)}, u32[]{:S(2)}, u32[]{:S(2)}) collective-permute-start(bf16[4,24,384]{2,1,0:T(8,128)(2,1)S(1)} %fusion.3), channel_id=1, source_target_pairs={{0,8},{1,9},{2,10},{3,11},{4,12},{5,13},{6,14},{7,15},{8,0},{9,1},... | collective-permute-start | bytes 221192 | tf_op jit(solution)/shard_map/ppermute | solution.py:281
  27.9 0.1 collective-permute-done.6
  28.1 2.8 %collective-permute-done.7 = bf16[4,24,384]{2,1,0:T(8,128)(2,1)S(1)} collective-permute-done((bf16[4,24,384]{2,1,0:T(8,128)(2,1)S(1)}, bf16[4,24,384]{2,1,0:T(8,128)(2,1)S(1)}, u32[]{:S(2)}, u32[]{:S(2)}) %collective-permute-start.7) | collective-permute-done | bytes 73760 | tf_op jit(solution)/shard_map/ppermute | solution.py:281
  31.0 2.5 %collective-permute-start.8 = (bf16[2,1,2,24,384]{4,3,2,1,0:T(8,128)(2,1)S(1)}, bf16[2,1,2,24,384]{4,3,2,1,0:T(8,128)(2,1)S(1)}, u32[]{:S(2)}, u32[]{:S(2)}) collective-permute-start(bf16[2,1,2,24,384]{4,3,2,1,0:T(8,128)(2,1)S(1)} %get-tuple-element.17), channel_id=1, source_target_pairs={{0,6},{1,7},{2,4},{3,5},{4,2},{5,3},{6,0},{7,1},{8,14},{9,15},{10,... | collective-permute-start | bytes 221192 | tf_op jit(solution)/shard_map/ppermute | solution.py:281
  33.6 0.5 %collective-permute-start.9 = (bf16[2,1,2,24,384]{4,3,2,1,0:T(8,128)(2,1)S(1)}, bf16[2,1,2,24,384]{4,3,2,1,0:T(8,128)(2,1)S(1)}, u32[]{:S(2)}, u32[]{:S(2)}) collective-permute-start(bf16[2,1,2,24,384]{4,3,2,1,0:T(8,128)(2,1)S(1)} %get-tuple-element.18), channel_id=1, source_target_pairs={{0,2},{1,3},{2,0},{3,1},{4,6},{5,7},{6,4},{7,5},{8,10},{9,11},{10,... | collective-permute-start | bytes 221192 | tf_op jit(solution)/shard_map/ppermute | solution.py:281
  34.1 1.2 %collective-permute-start.10 = (bf16[2,1,2,24,384]{4,3,2,1,0:T(8,128)(2,1)S(1)}, bf16[2,1,2,24,384]{4,3,2,1,0:T(8,128)(2,1)S(1)}, u32[]{:S(2)}, u32[]{:S(2)}) collective-permute-start(bf16[2,1,2,24,384]{4,3,2,1,0:T(8,128)(2,1)S(1)} %get-tuple-element.19), channel_id=1, source_target_pairs={{0,4},{1,5},{2,6},{3,7},{4,0},{5,1},{6,2},{7,3},{8,12},{9,13},{10,... | collective-permute-start | bytes 221192 | tf_op jit(solution)/shard_map/ppermute | solution.py:281
  35.2 1.2 %collective-permute-done.8.by_both.refs_0_ = bf16[2,1,2,24,384]{4,3,2,1,0:T(8,128)(2,1)S(1)} collective-permute-done((bf16[2,1,2,24,384]{4,3,2,1,0:T(8,128)(2,1)S(1)}, bf16[2,1,2,24,384]{4,3,2,1,0:T(8,128)(2,1)S(1)}, u32[]{:S(2)}, u32[]{:S(2)}) %collective-permute-start.8) | collective-permute-done | bytes 73760 | tf_op jit(solution)/shard_map/ppermute | solution.py:281
  36.4 1.5 %collective-permute-done.9.by_x.refs_1_ = bf16[2,1,2,24,384]{4,3,2,1,0:T(8,128)(2,1)S(1)} collective-permute-done((bf16[2,1,2,24,384]{4,3,2,1,0:T(8,128)(2,1)S(1)}, bf16[2,1,2,24,384]{4,3,2,1,0:T(8,128)(2,1)S(1)}, u32[]{:S(2)}, u32[]{:S(2)}) %collective-permute-start.9) | collective-permute-done | bytes 73760 | tf_op jit(solution)/shard_map/ppermute | solution.py:281
  37.9 0.5 %collective-permute-start.14 = (bf16[1,1,2,24,384]{4,3,2,1,0:T(8,128)(2,1)S(1)}, bf16[1,1,2,24,384]{4,3,2,1,0:T(8,128)(2,1)S(1)}, u32[]{:S(2)}, u32[]{:S(2)}) collective-permute-start(bf16[1,1,2,24,384]{4,3,2,1,0:T(8,128)(2,1)S(1)} %slice.94), channel_id=1, source_target_pairs={{0,1},{1,0},{2,3},{3,2},{4,5},{5,4},{6,7},{7,6},{8,9},{9,8},{10,11... | collective-permute-start | bytes 110600 | tf_op jit(solution)/shard_map/ppermute | solution.py:281
  38.4 0.1 collective-permute-start.13
  38.6 0.5 %collective-permute-done.12.by_x_core.refs_4_ = bf16[1,1,2,24,384]{4,3,2,1,0:T(8,128)(2,1)S(1)} collective-permute-done((bf16[1,1,2,24,384]{4,3,2,1,0:T(8,128)(2,1)S(1)}, bf16[1,1,2,24,384]{4,3,2,1,0:T(8,128)(2,1)S(1)}, u32[]{:S(2)}, u32[]{:S(2)}) %collective-permute-start.12) | collective-permute-done | bytes 36896 | tf_op jit(solution)/shard_map/ppermute | solution.py:281
  39.1 0.8 %left_across.1.refs_8_ = bf16[1,2,4,96,768]{4,3,2,1,0:T(8,128)(2,1)S(1)} custom-call(bf16[2,1,2,24,384]{4,3,2,1,0:T(8,128)(2,1)S(1)} %collective-permute-done.8.by_both.refs_0_, bf16[2,1,2,24,384]{4,3,2,1,0:T(8,128)(2,1)S(1)} %collective-permute-done.9.by_x.refs_1_, bf16[1,1,2,24,384]{4,3,2,1,0:T(8,128)(2,1)S(1)} %collective-permute-done.11.by_both_core.refs_3_, ...), custom_call_target="tpu_custom_call" | custom-call | flops 905969664 | bytes 2359296 | tf_op jit(solution)/shard_map/left_across/pallas_call | solution.py:250
  40.0 3.4 %meson_blocks.1 = bf16[1,2,768,768]{3,2,1,0:T(8,128)(2,1)} custom-call(bf16[2,1,2,24,384]{4,3,2,1,0:T(8,128)(2,1)S(1)} %collective-permute-done.8.by_both.refs_0_, bf16[2,1,2,24,384]{4,3,2,1,0:T(8,128)(2,1)S(1)} %collective-permute-done.9.by_x.refs_1_, bf16[2,1,2,24,384]{4,3,2,1,0:T(8,128)(2,1)S(1)} %collective-permute-done.10.refs_2_, ...), custom_call_target="tpu_custom_call" | custom-call | flops 905969664 | bytes 2359296 | tf_op jit(solution)/shard_map/meson_blocks/pallas_call | solution.py:260
  (51 shorter events, 1.2 us)
Async XLA Ops:
  0.0 0.7 %copy-start.2 = (s32[3]{0:T(128)S(1)}, s32[3]{0:T(128)}, u32[]{:S(2)}) copy-start(s32[3]{0:T(128)} %param.5) | copy-start | bytes 40
  0.7 7.9 %copy-start.1 = (s32[1,2]{1,0:T(1,128)S(1)}, s32[1,2]{1,0:T(1,128)}, u32[]{:S(2)}) copy-start(s32[1,2]{1,0:T(1,128)} %refs_0_.1) | copy-start | bytes 28
  8.0 1.7 %collective-permute-start.3 = (bf16[2,4,48,384]{3,2,1,0:T(8,128)(2,1)S(1)}, bf16[2,4,48,384]{3,2,1,0:T(8,128)(2,1)S(1)}, u32[]{:S(2)}, u32[]{:S(2)}) collective-permute-start(bf16[2,4,48,384]{3,2,1,0:T(8,128)(2,1)S(1)} %get-tuple-element.16), channel_id=1, source_target_pairs={{0,1},{1,0},{2,3},{3,2},{4,5},{5,4},{6,7},{7,6},{8,9},{9,8},{10,11... | collective-permute-start | bytes 884744 | tf_op jit(solution)/shard_map/ppermute | solution.py:281
  8.6 4.2 %collective-permute-start = (bf16[392,384]{1,0:T(8,128)(2,1)S(1)}, bf16[392,384]{1,0:T(8,128)(2,1)S(1)}, u32[]{:S(2)}, u32[]{:S(2)}) collective-permute-start(bf16[392,384]{1,0:T(8,128)(2,1)S(1)} %pad_maximum_fusion), channel_id=1, source_target_pairs={{0,1},{1,0},{2,3},{3,2},{4,5},{5,4},{6,7},{7,6},{8,9},{9,8},{10,11... | collective-permute-start | bytes 903176 | tf_op jit(solution)/shard_map/ppermute | solution.py:281
  9.8 7.5 %collective-permute-start.4 = (bf16[4,48,384]{2,1,0:T(8,128)(2,1)S(1)}, bf16[4,48,384]{2,1,0:T(8,128)(2,1)S(1)}, u32[]{:S(2)}, u32[]{:S(2)}) collective-permute-start(bf16[4,48,384]{2,1,0:T(8,128)(2,1)S(1)} %fusion.1), channel_id=1, source_target_pairs={{0,2},{1,3},{2,0},{3,1},{4,6},{5,7},{6,4},{7,5},{8,10},{9,11},{10,... | collective-permute-start | bytes 442376 | tf_op jit(solution)/shard_map/ppermute | solution.py:281
  13.0 26.2 %copy-start = (bf16[1,2,768,768]{3,2,1,0:T(8,128)(2,1)S(1)}, bf16[1,2,768,768]{3,2,1,0:T(8,128)(2,1)}, u32[]{:S(2)}) copy-start(bf16[1,2,768,768]{3,2,1,0:T(8,128)(2,1)} %refs_9_.1) | copy-start | bytes 7077892
  13.0 7.1 %collective-permute-start.1 = (bf16[200,384]{1,0:T(8,128)(2,1)S(1)}, bf16[200,384]{1,0:T(8,128)(2,1)S(1)}, u32[]{:S(2)}, u32[]{:S(2)}) collective-permute-start(bf16[200,384]{1,0:T(8,128)(2,1)S(1)} %pad_maximum_fusion.1), channel_id=1, source_target_pairs={{0,2},{1,3},{2,0},{3,1},{4,6},{5,7},{6,4},{7,5},{8,10},{9,11},{10,... | collective-permute-start | bytes 460808 | tf_op jit(solution)/shard_map/ppermute | solution.py:281
  17.4 4.9 %collective-permute-start.5 = (bf16[4,24,384]{2,1,0:T(8,128)(2,1)S(1)}, bf16[4,24,384]{2,1,0:T(8,128)(2,1)S(1)}, u32[]{:S(2)}, u32[]{:S(2)}) collective-permute-start(bf16[4,24,384]{2,1,0:T(8,128)(2,1)S(1)} %fusion.4), channel_id=1, source_target_pairs={{0,4},{1,5},{2,6},{3,7},{4,0},{5,1},{6,2},{7,3},{8,12},{9,13},{10,... | collective-permute-start | bytes 221192 | tf_op jit(solution)/shard_map/ppermute | solution.py:281
  20.4 4.6 %collective-permute-start.2 = (bf16[104,384]{1,0:T(8,128)(2,1)S(1)}, bf16[104,384]{1,0:T(8,128)(2,1)S(1)}, u32[]{:S(2)}, u32[]{:S(2)}) collective-permute-start(bf16[104,384]{1,0:T(8,128)(2,1)S(1)} %pad_maximum_fusion.2), channel_id=1, source_target_pairs={{0,4},{1,5},{2,6},{3,7},{4,0},{5,1},{6,2},{7,3},{8,12},{9,13},{10,... | collective-permute-start | bytes 239624 | tf_op jit(solution)/shard_map/ppermute | solution.py:281
  22.4 5.7 %collective-permute-start.6 = (bf16[4,24,384]{2,1,0:T(8,128)(2,1)S(1)}, bf16[4,24,384]{2,1,0:T(8,128)(2,1)S(1)}, u32[]{:S(2)}, u32[]{:S(2)}) collective-permute-start(bf16[4,24,384]{2,1,0:T(8,128)(2,1)S(1)} %fusion.2), channel_id=1, source_target_pairs={{0,8},{1,9},{2,10},{3,11},{4,12},{5,13},{6,14},{7,15},{8,0},{9,1},... | collective-permute-start | bytes 221192 | tf_op jit(solution)/shard_map/ppermute | solution.py:281
  25.2 5.6 %collective-permute-start.7 = (bf16[4,24,384]{2,1,0:T(8,128)(2,1)S(1)}, bf16[4,24,384]{2,1,0:T(8,128)(2,1)S(1)}, u32[]{:S(2)}, u32[]{:S(2)}) collective-permute-start(bf16[4,24,384]{2,1,0:T(8,128)(2,1)S(1)} %fusion.3), channel_id=1, source_target_pairs={{0,8},{1,9},{2,10},{3,11},{4,12},{5,13},{6,14},{7,15},{8,0},{9,1},... | collective-permute-start | bytes 221192 | tf_op jit(solution)/shard_map/ppermute | solution.py:281
  31.0 5.4 %collective-permute-start.8 = (bf16[2,1,2,24,384]{4,3,2,1,0:T(8,128)(2,1)S(1)}, bf16[2,1,2,24,384]{4,3,2,1,0:T(8,128)(2,1)S(1)}, u32[]{:S(2)}, u32[]{:S(2)}) collective-permute-start(bf16[2,1,2,24,384]{4,3,2,1,0:T(8,128)(2,1)S(1)} %get-tuple-element.17), channel_id=1, source_target_pairs={{0,6},{1,7},{2,4},{3,5},{4,2},{5,3},{6,0},{7,1},{8,14},{9,15},{10,... | collective-permute-start | bytes 221192 | tf_op jit(solution)/shard_map/ppermute | solution.py:281
  33.6 4.4 %collective-permute-start.9 = (bf16[2,1,2,24,384]{4,3,2,1,0:T(8,128)(2,1)S(1)}, bf16[2,1,2,24,384]{4,3,2,1,0:T(8,128)(2,1)S(1)}, u32[]{:S(2)}, u32[]{:S(2)}) collective-permute-start(bf16[2,1,2,24,384]{4,3,2,1,0:T(8,128)(2,1)S(1)} %get-tuple-element.18), channel_id=1, source_target_pairs={{0,2},{1,3},{2,0},{3,1},{4,6},{5,7},{6,4},{7,5},{8,10},{9,11},{10,... | collective-permute-start | bytes 221192 | tf_op jit(solution)/shard_map/ppermute | solution.py:281
  34.1 4.4 %collective-permute-start.10 = (bf16[2,1,2,24,384]{4,3,2,1,0:T(8,128)(2,1)S(1)}, bf16[2,1,2,24,384]{4,3,2,1,0:T(8,128)(2,1)S(1)}, u32[]{:S(2)}, u32[]{:S(2)}) collective-permute-start(bf16[2,1,2,24,384]{4,3,2,1,0:T(8,128)(2,1)S(1)} %get-tuple-element.19), channel_id=1, source_target_pairs={{0,4},{1,5},{2,6},{3,7},{4,0},{5,1},{6,2},{7,3},{8,12},{9,13},{10,... | collective-permute-start | bytes 221192 | tf_op jit(solution)/shard_map/ppermute | solution.py:281
  36.4 2.1 %collective-permute-start.11 = (bf16[1,1,2,24,384]{4,3,2,1,0:T(8,128)(2,1)S(1)}, bf16[1,1,2,24,384]{4,3,2,1,0:T(8,128)(2,1)S(1)}, u32[]{:S(2)}, u32[]{:S(2)}) collective-permute-start(bf16[1,1,2,24,384]{4,3,2,1,0:T(8,128)(2,1)S(1)} %slice.105), channel_id=1, source_target_pairs={{0,1},{1,0},{2,3},{3,2},{4,5},{5,4},{6,7},{7,6},{8,9},{9,8},{10,11... | collective-permute-start | bytes 110600 | tf_op jit(solution)/shard_map/ppermute | solution.py:281
  37.9 1.2 %collective-permute-start.12 = (bf16[1,1,2,24,384]{4,3,2,1,0:T(8,128)(2,1)S(1)}, bf16[1,1,2,24,384]{4,3,2,1,0:T(8,128)(2,1)S(1)}, u32[]{:S(2)}, u32[]{:S(2)}) collective-permute-start(bf16[1,1,2,24,384]{4,3,2,1,0:T(8,128)(2,1)S(1)} %slice.106), channel_id=1, source_target_pairs={{0,1},{1,0},{2,3},{3,2},{4,5},{5,4},{6,7},{7,6},{8,9},{9,8},{10,11... | collective-permute-start | bytes 110600 | tf_op jit(solution)/shard_map/ppermute | solution.py:281
  37.9 2.0 %collective-permute-start.14 = (bf16[1,1,2,24,384]{4,3,2,1,0:T(8,128)(2,1)S(1)}, bf16[1,1,2,24,384]{4,3,2,1,0:T(8,128)(2,1)S(1)}, u32[]{:S(2)}, u32[]{:S(2)}) collective-permute-start(bf16[1,1,2,24,384]{4,3,2,1,0:T(8,128)(2,1)S(1)} %slice.94), channel_id=1, source_target_pairs={{0,1},{1,0},{2,3},{3,2},{4,5},{5,4},{6,7},{7,6},{8,9},{9,8},{10,11... | collective-permute-start | bytes 110600 | tf_op jit(solution)/shard_map/ppermute | solution.py:281
  38.4 1.5 %collective-permute-start.13 = (bf16[1,1,2,24,384]{4,3,2,1,0:T(8,128)(2,1)S(1)}, bf16[1,1,2,24,384]{4,3,2,1,0:T(8,128)(2,1)S(1)}, u32[]{:S(2)}, u32[]{:S(2)}) collective-permute-start(bf16[1,1,2,24,384]{4,3,2,1,0:T(8,128)(2,1)S(1)} %slice.107), channel_id=1, source_target_pairs={{0,1},{1,0},{2,3},{3,2},{4,5},{5,4},{6,7},{7,6},{8,9},{9,8},{10,11... | collective-permute-start | bytes 110600 | tf_op jit(solution)/shard_map/ppermute | solution.py:281

commit v8 on v7

--- a/solution.py
+++ b/solution.py
@@ -160,7 +160,7 @@
 def left_rows(pair, quarters, flips, peram, left, mat):
     width = peram.shape[2] // 4
     rows = quarters.shape[3]
-    half = 2 * rows
+    half = len(flips) * rows
     for at, flip in enumerate(flips):
         band = slice(at * rows, (at + 1) * rows)
         lower = slice(half + at * rows, half + (at + 1) * rows)
@@ -177,10 +177,10 @@
         left[pair, 1, a] = both[half:]
 
 
-def across_kernel(by_both, by_x, by_both_core, by_x_core, peram, left, quarters, mat):
-    join_halves((by_x, by_both, by_x_core, by_both_core), (2, 3), quarters)
+def across_kernel(by_both, by_x, peram, left, quarters, mat):
+    join_halves((by_x, by_both), (2,), quarters)
     for pair in range(peram.shape[0]):
-        left_rows(pair, quarters, (2, 3), peram, left, mat)
+        left_rows(pair, quarters, (2,), peram, left, mat)
 
 
 def block_kernel(*refs):
@@ -199,7 +199,7 @@
 
     join_halves(parts, (0, 1, 2, 3), quarters)
     for pair in range(peram.shape[0]):
-        left_rows(pair, quarters, (0, 1), peram, near, mat)
+        left_rows(pair, quarters, (0, 1, 3), peram, near, mat)
         for flip, start in enumerate(starts):
             src_el[pl.ds(start, rows), :] = quarters[flip, pair, 1]
         e_re = src_el[:, :width]
@@ -225,8 +225,9 @@
                 for part in range(2):
                     lanes = slice(part * window, (part + 1) * window)
                     first = 2 * half * width
-                    for flip, start in enumerate(starts):
-                        band = slice(half * width + flip * rows, half * width + (flip + 1) * rows)
+                    for at, flip in enumerate((0, 1, 3, 2)):
+                        start = starts[flip]
+                        band = slice(half * width + at * rows, half * width + (at + 1) * rows)
                         even = results[0][band, lanes]
                         odd = results[1][band, lanes]
                         row = jnp.concatenate([even[:, :edge], even[:, edge:] + odd[:, : window - edge], odd[:, window - edge :]], axis=1)
@@ -245,26 +246,27 @@
         flops=pairs * 8 * full * full * width, bytes_accessed=pairs * 4 * full * full, transcendentals=0
     )
     quarters = (4, pairs, 2, width // 4, 2 * width)
-    half = jax.ShapeDtypeStruct((pairs, 2, 4, width // 2, full), BF16)
+    rows = width // 4
+    one = jax.ShapeDtypeStruct((pairs, 2, 4, rows, full), BF16)
     in_vmem = pl.BlockSpec(memory_space=pltpu.VMEM)
     far = pl.pallas_call(
         across_kernel,
-        in_specs=[in_vmem] * 5,
+        in_specs=[in_vmem] * 3,
         out_specs=in_vmem,
-        scratch_shapes=[pltpu.VMEM(quarters, BF16), pltpu.VMEM((width, 2 * width), BF16)],
-        out_shape=half,
+        scratch_shapes=[pltpu.VMEM(quarters, BF16), pltpu.VMEM((2 * rows, 2 * width), BF16)],
+        out_shape=one,
         compiler_params=params,
         cost_estimate=cost,
         name="left_across",
-    )(*[parts[at] for at in (5, 4, 7, 6)], peram)
+    )(*[parts[at] for at in (5, 4)], peram)
     return pl.pallas_call(
         block_kernel,
         in_specs=[in_vmem] * 10,
         out_specs=pl.BlockSpec(memory_space=pl.ANY),
         scratch_shapes=[
-            pltpu.VMEM(half.shape, BF16),
+            pltpu.VMEM((pairs, 2, 4, 3 * rows, full), BF16),
             pltpu.VMEM(quarters, BF16),
-            pltpu.VMEM((width, 2 * width), BF16),
+            pltpu.VMEM((6 * rows, 2 * width), BF16),
             pltpu.VMEM((width, 2 * width), BF16),
             pltpu.VMEM((2, 2 * window, 2 * window), BF16),
             pltpu.VMEM((4, 2, width, full), BF16),

time: 43.5 us -> 43.5 us (level)
  starting transfers between devices: 18.3 us -> 17.7 us
    ppermute x15, starting transfers between devices: 18.3 us -> 17.7 us  [swap(): return lax.ppermute(value, 'sink', [(i, i ^ flip) for i in range(devices)])]
    ppermute x15, waiting for transfers between devices: 11.7 us -> 12.1 us  [swap(): return lax.ppermute(value, 'sink', [(i, i ^ flip) for i in range(devices)])]
  transfers between devices with their start and end apart: 15 -> 15, of which waited for: 8 -> 9; matrix products, arithmetic and copies ran while one was open for 2% -> 2% of each run, Pallas kernels for 2% -> 1%
where the time goes in v8:
time: 43.5 us; the launch traced here: 43.3 us
  starting transfers between devices  17.7 us (41%)
  waiting for transfers between devices  12.1 us (28%)
  Pallas kernels  11.7 us (27%)
  local copies, waits for them, and re-layouts  1.01 us (2%)
  other arithmetic  0.53 us (1%)
    ppermute x15, starting transfers between devices, swap(): return lax.ppermute(value, 'sink', [(i, i ^ flip) for i in range(devices)])  17.7 us
    ppermute x15, waiting for transfers between devices, swap(): return lax.ppermute(value, 'sink', [(i, i ^ flip) for i in range(devices)])  12.1 us
    pallas_call x1, Pallas kernels, elementals(): pl.pallas_call(functools.partial(elemental_kernel, devices, chunks, arriv...  7.31 us
    pallas_call x1, Pallas kernels, pair_blocks(): pl.pallas_call(block_kernel, in_specs=[in_vmem] * 10, out_specs=pl.BlockS...  3.69 us
  transfers between devices with their start and end apart: 15, of which 9 were waited for; matrix products, arithmetic and copies ran while one was open for 2% of the time, Pallas kernels for 1%

profile of v8, /device:TPU:0, one launch (start us, length us, event | category | flops | bytes accessed | tf_op | source)
XLA Modules:
  0.0 43.3 jit_solution(5864812173778533126)
XLA Ops:
  0.0 0.7 %copy-done.2 = s32[3]{0:T(128)S(1)} copy-done((s32[3]{0:T(128)S(1)}, s32[3]{0:T(128)}, u32[]{:S(2)}) %copy-start.2) | copy-done | bytes 36
  0.7 7.3 %partial_elementals.1 = (f32[2,4,48,384]{3,2,1,0:T(8,128)S(1)}, bf16[2,4,48,384]{3,2,1,0:T(8,128)(2,1)S(1)}, f32[2,4,48,384]{3,2,1,0:T(8,128)S(1)}, bf16[2,4,48,384]{3,2,1,0:T(8,128)(2,1)S(1)}) custom-call(s32[1,3]{1,0:T(1,128)S(1)} %bitcast.43, bf16[8,2,3,192,512]{4,3,2,1,0:T(8,128)(2,1)} %eigvecs.1), custom_call_target="tpu_custom_call" | custom-call | flops 3623878656 | bytes 9437184 | tf_op jit(solution)/shard_map/partial_elementals/pallas_call | solution.py:95
  8.0 0.5 %collective-permute-start.3 = (bf16[2,4,48,384]{3,2,1,0:T(8,128)(2,1)S(1)}, bf16[2,4,48,384]{3,2,1,0:T(8,128)(2,1)S(1)}, u32[]{:S(2)}, u32[]{:S(2)}) collective-permute-start(bf16[2,4,48,384]{3,2,1,0:T(8,128)(2,1)S(1)} %get-tuple-element.16), channel_id=1, source_target_pairs={{0,1},{1,0},{2,3},{3,2},{4,5},{5,4},{6,7},{7,6},{8,9},{9,8},{10,11... | collective-permute-start | bytes 884744 | tf_op jit(solution)/shard_map/ppermute | solution.py:283
  8.7 1.0 %collective-permute-done.3 = bf16[2,4,48,384]{3,2,1,0:T(8,128)(2,1)S(1)} collective-permute-done((bf16[2,4,48,384]{3,2,1,0:T(8,128)(2,1)S(1)}, bf16[2,4,48,384]{3,2,1,0:T(8,128)(2,1)S(1)}, u32[]{:S(2)}, u32[]{:S(2)}) %collective-permute-start.3) | collective-permute-done | bytes 294944 | tf_op jit(solution)/shard_map/ppermute | solution.py:283
  9.8 2.9 %collective-permute-start.4 = (bf16[4,48,384]{2,1,0:T(8,128)(2,1)S(1)}, bf16[4,48,384]{2,1,0:T(8,128)(2,1)S(1)}, u32[]{:S(2)}, u32[]{:S(2)}) collective-permute-start(bf16[4,48,384]{2,1,0:T(8,128)(2,1)S(1)} %fusion.1), channel_id=1, source_target_pairs={{0,2},{1,3},{2,0},{3,1},{4,6},{5,7},{6,4},{7,5},{8,10},{9,11},{10,... | collective-permute-start | bytes 442376 | tf_op jit(solution)/shard_map/ppermute | solution.py:283
  13.0 0.3 collective-permute-start.1
  13.4 4.0 %collective-permute-done.4 = bf16[4,48,384]{2,1,0:T(8,128)(2,1)S(1)} collective-permute-done((bf16[4,48,384]{2,1,0:T(8,128)(2,1)S(1)}, bf16[4,48,384]{2,1,0:T(8,128)(2,1)S(1)}, u32[]{:S(2)}, u32[]{:S(2)}) %collective-permute-start.4) | collective-permute-done | bytes 147488 | tf_op jit(solution)/shard_map/ppermute | solution.py:283
  17.4 2.2 %collective-permute-start.5 = (bf16[4,24,384]{2,1,0:T(8,128)(2,1)S(1)}, bf16[4,24,384]{2,1,0:T(8,128)(2,1)S(1)}, u32[]{:S(2)}, u32[]{:S(2)}) collective-permute-start(bf16[4,24,384]{2,1,0:T(8,128)(2,1)S(1)} %fusion.4), channel_id=1, source_target_pairs={{0,4},{1,5},{2,6},{3,7},{4,0},{5,1},{6,2},{7,3},{8,12},{9,13},{10,... | collective-permute-start | bytes 221192 | tf_op jit(solution)/shard_map/ppermute | solution.py:283
  19.6 0.5 %collective-permute-done.1 = bf16[200,384]{1,0:T(8,128)(2,1)S(1)} collective-permute-done((bf16[200,384]{1,0:T(8,128)(2,1)S(1)}, bf16[200,384]{1,0:T(8,128)(2,1)S(1)}, u32[]{:S(2)}, u32[]{:S(2)}) %collective-permute-start.1) | collective-permute-done | bytes 153632 | tf_op jit(solution)/shard_map/ppermute | solution.py:283
  20.4 1.9 %collective-permute-start.2 = (bf16[104,384]{1,0:T(8,128)(2,1)S(1)}, bf16[104,384]{1,0:T(8,128)(2,1)S(1)}, u32[]{:S(2)}, u32[]{:S(2)}) collective-permute-start(bf16[104,384]{1,0:T(8,128)(2,1)S(1)} %pad_maximum_fusion.2), channel_id=1, source_target_pairs={{0,4},{1,5},{2,6},{3,7},{4,0},{5,1},{6,2},{7,3},{8,12},{9,13},{10,... | collective-permute-start | bytes 239624 | tf_op jit(solution)/shard_map/ppermute | solution.py:283
  22.4 2.7 %collective-permute-start.6 = (bf16[4,24,384]{2,1,0:T(8,128)(2,1)S(1)}, bf16[4,24,384]{2,1,0:T(8,128)(2,1)S(1)}, u32[]{:S(2)}, u32[]{:S(2)}) collective-permute-start(bf16[4,24,384]{2,1,0:T(8,128)(2,1)S(1)} %fusion.2), channel_id=1, source_target_pairs={{0,8},{1,9},{2,10},{3,11},{4,12},{5,13},{6,14},{7,15},{8,0},{9,1},... | collective-permute-start | bytes 221192 | tf_op jit(solution)/shard_map/ppermute | solution.py:283
  25.2 2.7 %collective-permute-start.7 = (bf16[4,24,384]{2,1,0:T(8,128)(2,1)S(1)}, bf16[4,24,384]{2,1,0:T(8,128)(2,1)S(1)}, u32[]{:S(2)}, u32[]{:S(2)}) collective-permute-start(bf16[4,24,384]{2,1,0:T(8,128)(2,1)S(1)} %fusion.3), channel_id=1, source_target_pairs={{0,8},{1,9},{2,10},{3,11},{4,12},{5,13},{6,14},{7,15},{8,0},{9,1},... | collective-permute-start | bytes 221192 | tf_op jit(solution)/shard_map/ppermute | solution.py:283
  27.9 0.1 collective-permute-done.6
  28.1 2.8 %collective-permute-done.7 = bf16[4,24,384]{2,1,0:T(8,128)(2,1)S(1)} collective-permute-done((bf16[4,24,384]{2,1,0:T(8,128)(2,1)S(1)}, bf16[4,24,384]{2,1,0:T(8,128)(2,1)S(1)}, u32[]{:S(2)}, u32[]{:S(2)}) %collective-permute-start.7) | collective-permute-done | bytes 73760 | tf_op jit(solution)/shard_map/ppermute | solution.py:283
  30.9 0.1 select_slices.1
  31.0 2.5 %collective-permute-start.8 = (bf16[2,1,2,24,384]{4,3,2,1,0:T(8,128)(2,1)S(1)}, bf16[2,1,2,24,384]{4,3,2,1,0:T(8,128)(2,1)S(1)}, u32[]{:S(2)}, u32[]{:S(2)}) collective-permute-start(bf16[2,1,2,24,384]{4,3,2,1,0:T(8,128)(2,1)S(1)} %get-tuple-element.17), channel_id=1, source_target_pairs={{0,6},{1,7},{2,4},{3,5},{4,2},{5,3},{6,0},{7,1},{8,14},{9,15},{10,... | collective-permute-start | bytes 221192 | tf_op jit(solution)/shard_map/ppermute | solution.py:283
  33.6 0.5 %collective-permute-start.9 = (bf16[2,1,2,24,384]{4,3,2,1,0:T(8,128)(2,1)S(1)}, bf16[2,1,2,24,384]{4,3,2,1,0:T(8,128)(2,1)S(1)}, u32[]{:S(2)}, u32[]{:S(2)}) collective-permute-start(bf16[2,1,2,24,384]{4,3,2,1,0:T(8,128)(2,1)S(1)} %get-tuple-element.18), channel_id=1, source_target_pairs={{0,2},{1,3},{2,0},{3,1},{4,6},{5,7},{6,4},{7,5},{8,10},{9,11},{10,... | collective-permute-start | bytes 221192 | tf_op jit(solution)/shard_map/ppermute | solution.py:283
  34.1 1.2 %collective-permute-start.10 = (bf16[2,1,2,24,384]{4,3,2,1,0:T(8,128)(2,1)S(1)}, bf16[2,1,2,24,384]{4,3,2,1,0:T(8,128)(2,1)S(1)}, u32[]{:S(2)}, u32[]{:S(2)}) collective-permute-start(bf16[2,1,2,24,384]{4,3,2,1,0:T(8,128)(2,1)S(1)} %get-tuple-element.19), channel_id=1, source_target_pairs={{0,4},{1,5},{2,6},{3,7},{4,0},{5,1},{6,2},{7,3},{8,12},{9,13},{10,... | collective-permute-start | bytes 221192 | tf_op jit(solution)/shard_map/ppermute | solution.py:283
  35.3 1.2 %collective-permute-done.8.by_both.refs_0_ = bf16[2,1,2,24,384]{4,3,2,1,0:T(8,128)(2,1)S(1)} collective-permute-done((bf16[2,1,2,24,384]{4,3,2,1,0:T(8,128)(2,1)S(1)}, bf16[2,1,2,24,384]{4,3,2,1,0:T(8,128)(2,1)S(1)}, u32[]{:S(2)}, u32[]{:S(2)}) %collective-permute-start.8) | collective-permute-done | bytes 73760 | tf_op jit(solution)/shard_map/ppermute | solution.py:283
  36.4 1.5 %collective-permute-done.9.by_x.refs_1_ = bf16[2,1,2,24,384]{4,3,2,1,0:T(8,128)(2,1)S(1)} collective-permute-done((bf16[2,1,2,24,384]{4,3,2,1,0:T(8,128)(2,1)S(1)}, bf16[2,1,2,24,384]{4,3,2,1,0:T(8,128)(2,1)S(1)}, u32[]{:S(2)}, u32[]{:S(2)}) %collective-permute-start.9) | collective-permute-done | bytes 73760 | tf_op jit(solution)/shard_map/ppermute | solution.py:283
  37.9 0.5 %collective-permute-done.10.refs_2_ = bf16[2,1,2,24,384]{4,3,2,1,0:T(8,128)(2,1)S(1)} collective-permute-done((bf16[2,1,2,24,384]{4,3,2,1,0:T(8,128)(2,1)S(1)}, bf16[2,1,2,24,384]{4,3,2,1,0:T(8,128)(2,1)S(1)}, u32[]{:S(2)}, u32[]{:S(2)}) %collective-permute-start.10) | collective-permute-done | bytes 73760 | tf_op jit(solution)/shard_map/ppermute | solution.py:283
  38.5 0.6 %left_across.1.refs_8_ = bf16[1,2,4,48,768]{4,3,2,1,0:T(8,128)(2,1)S(1)} custom-call(bf16[2,1,2,24,384]{4,3,2,1,0:T(8,128)(2,1)S(1)} %collective-permute-done.8.by_both.refs_0_, bf16[2,1,2,24,384]{4,3,2,1,0:T(8,128)(2,1)S(1)} %collective-permute-done.9.by_x.refs_1_, bf16[1,2,768,768]{3,2,1,0:T(8,128)(2,1)S(1)} %copy-done), custom_call_target="tpu_custom_call" | custom-call | flops 905969664 | bytes 2359296 | tf_op jit(solution)/shard_map/left_across/pallas_call | solution.py:252
  39.1 0.5 %collective-permute-done.13.refs_5_ = bf16[1,1,2,24,384]{4,3,2,1,0:T(8,128)(2,1)S(1)} collective-permute-done((bf16[1,1,2,24,384]{4,3,2,1,0:T(8,128)(2,1)S(1)}, bf16[1,1,2,24,384]{4,3,2,1,0:T(8,128)(2,1)S(1)}, u32[]{:S(2)}, u32[]{:S(2)}) %collective-permute-start.13) | collective-permute-done | bytes 36896 | tf_op jit(solution)/shard_map/ppermute | solution.py:283
  39.6 3.7 %meson_blocks.1 = bf16[1,2,768,768]{3,2,1,0:T(8,128)(2,1)} custom-call(bf16[2,1,2,24,384]{4,3,2,1,0:T(8,128)(2,1)S(1)} %collective-permute-done.8.by_both.refs_0_, bf16[2,1,2,24,384]{4,3,2,1,0:T(8,128)(2,1)S(1)} %collective-permute-done.9.by_x.refs_1_, bf16[2,1,2,24,384]{4,3,2,1,0:T(8,128)(2,1)S(1)} %collective-permute-done.10.refs_2_, ...), custom_call_target="tpu_custom_call" | custom-call | flops 905969664 | bytes 2359296 | tf_op jit(solution)/shard_map/meson_blocks/pallas_call | solution.py:262
  (51 shorter events, 1.1 us)
Async XLA Ops:
  0.0 0.7 %copy-start.2 = (s32[3]{0:T(128)S(1)}, s32[3]{0:T(128)}, u32[]{:S(2)}) copy-start(s32[3]{0:T(128)} %param.5) | copy-start | bytes 40
  0.7 7.9 %copy-start.1 = (s32[1,2]{1,0:T(1,128)S(1)}, s32[1,2]{1,0:T(1,128)}, u32[]{:S(2)}) copy-start(s32[1,2]{1,0:T(1,128)} %refs_0_.1) | copy-start | bytes 28
  8.0 1.7 %collective-permute-start.3 = (bf16[2,4,48,384]{3,2,1,0:T(8,128)(2,1)S(1)}, bf16[2,4,48,384]{3,2,1,0:T(8,128)(2,1)S(1)}, u32[]{:S(2)}, u32[]{:S(2)}) collective-permute-start(bf16[2,4,48,384]{3,2,1,0:T(8,128)(2,1)S(1)} %get-tuple-element.16), channel_id=1, source_target_pairs={{0,1},{1,0},{2,3},{3,2},{4,5},{5,4},{6,7},{7,6},{8,9},{9,8},{10,11... | collective-permute-start | bytes 884744 | tf_op jit(solution)/shard_map/ppermute | solution.py:283
  8.6 4.2 %collective-permute-start = (bf16[392,384]{1,0:T(8,128)(2,1)S(1)}, bf16[392,384]{1,0:T(8,128)(2,1)S(1)}, u32[]{:S(2)}, u32[]{:S(2)}) collective-permute-start(bf16[392,384]{1,0:T(8,128)(2,1)S(1)} %pad_maximum_fusion), channel_id=1, source_target_pairs={{0,1},{1,0},{2,3},{3,2},{4,5},{5,4},{6,7},{7,6},{8,9},{9,8},{10,11... | collective-permute-start | bytes 903176 | tf_op jit(solution)/shard_map/ppermute | solution.py:283
  9.8 7.5 %collective-permute-start.4 = (bf16[4,48,384]{2,1,0:T(8,128)(2,1)S(1)}, bf16[4,48,384]{2,1,0:T(8,128)(2,1)S(1)}, u32[]{:S(2)}, u32[]{:S(2)}) collective-permute-start(bf16[4,48,384]{2,1,0:T(8,128)(2,1)S(1)} %fusion.1), channel_id=1, source_target_pairs={{0,2},{1,3},{2,0},{3,1},{4,6},{5,7},{6,4},{7,5},{8,10},{9,11},{10,... | collective-permute-start | bytes 442376 | tf_op jit(solution)/shard_map/ppermute | solution.py:283
  13.0 25.5 %copy-start = (bf16[1,2,768,768]{3,2,1,0:T(8,128)(2,1)S(1)}, bf16[1,2,768,768]{3,2,1,0:T(8,128)(2,1)}, u32[]{:S(2)}) copy-start(bf16[1,2,768,768]{3,2,1,0:T(8,128)(2,1)} %refs_9_.1) | copy-start | bytes 7077892
  13.0 7.1 %collective-permute-start.1 = (bf16[200,384]{1,0:T(8,128)(2,1)S(1)}, bf16[200,384]{1,0:T(8,128)(2,1)S(1)}, u32[]{:S(2)}, u32[]{:S(2)}) collective-permute-start(bf16[200,384]{1,0:T(8,128)(2,1)S(1)} %pad_maximum_fusion.1), channel_id=1, source_target_pairs={{0,2},{1,3},{2,0},{3,1},{4,6},{5,7},{6,4},{7,5},{8,10},{9,11},{10,... | collective-permute-start | bytes 460808 | tf_op jit(solution)/shard_map/ppermute | solution.py:283
  17.4 4.9 %collective-permute-start.5 = (bf16[4,24,384]{2,1,0:T(8,128)(2,1)S(1)}, bf16[4,24,384]{2,1,0:T(8,128)(2,1)S(1)}, u32[]{:S(2)}, u32[]{:S(2)}) collective-permute-start(bf16[4,24,384]{2,1,0:T(8,128)(2,1)S(1)} %fusion.4), channel_id=1, source_target_pairs={{0,4},{1,5},{2,6},{3,7},{4,0},{5,1},{6,2},{7,3},{8,12},{9,13},{10,... | collective-permute-start | bytes 221192 | tf_op jit(solution)/shard_map/ppermute | solution.py:283
  20.4 4.6 %collective-permute-start.2 = (bf16[104,384]{1,0:T(8,128)(2,1)S(1)}, bf16[104,384]{1,0:T(8,128)(2,1)S(1)}, u32[]{:S(2)}, u32[]{:S(2)}) collective-permute-start(bf16[104,384]{1,0:T(8,128)(2,1)S(1)} %pad_maximum_fusion.2), channel_id=1, source_target_pairs={{0,4},{1,5},{2,6},{3,7},{4,0},{5,1},{6,2},{7,3},{8,12},{9,13},{10,... | collective-permute-start | bytes 239624 | tf_op jit(solution)/shard_map/ppermute | solution.py:283
  22.4 5.7 %collective-permute-start.6 = (bf16[4,24,384]{2,1,0:T(8,128)(2,1)S(1)}, bf16[4,24,384]{2,1,0:T(8,128)(2,1)S(1)}, u32[]{:S(2)}, u32[]{:S(2)}) collective-permute-start(bf16[4,24,384]{2,1,0:T(8,128)(2,1)S(1)} %fusion.2), channel_id=1, source_target_pairs={{0,8},{1,9},{2,10},{3,11},{4,12},{5,13},{6,14},{7,15},{8,0},{9,1},... | collective-permute-start | bytes 221192 | tf_op jit(solution)/shard_map/ppermute | solution.py:283
  25.2 5.6 %collective-permute-start.7 = (bf16[4,24,384]{2,1,0:T(8,128)(2,1)S(1)}, bf16[4,24,384]{2,1,0:T(8,128)(2,1)S(1)}, u32[]{:S(2)}, u32[]{:S(2)}) collective-permute-start(bf16[4,24,384]{2,1,0:T(8,128)(2,1)S(1)} %fusion.3), channel_id=1, source_target_pairs={{0,8},{1,9},{2,10},{3,11},{4,12},{5,13},{6,14},{7,15},{8,0},{9,1},... | collective-permute-start | bytes 221192 | tf_op jit(solution)/shard_map/ppermute | solution.py:283
  31.0 5.4 %collective-permute-start.8 = (bf16[2,1,2,24,384]{4,3,2,1,0:T(8,128)(2,1)S(1)}, bf16[2,1,2,24,384]{4,3,2,1,0:T(8,128)(2,1)S(1)}, u32[]{:S(2)}, u32[]{:S(2)}) collective-permute-start(bf16[2,1,2,24,384]{4,3,2,1,0:T(8,128)(2,1)S(1)} %get-tuple-element.17), channel_id=1, source_target_pairs={{0,6},{1,7},{2,4},{3,5},{4,2},{5,3},{6,0},{7,1},{8,14},{9,15},{10,... | collective-permute-start | bytes 221192 | tf_op jit(solution)/shard_map/ppermute | solution.py:283
  33.6 4.4 %collective-permute-start.9 = (bf16[2,1,2,24,384]{4,3,2,1,0:T(8,128)(2,1)S(1)}, bf16[2,1,2,24,384]{4,3,2,1,0:T(8,128)(2,1)S(1)}, u32[]{:S(2)}, u32[]{:S(2)}) collective-permute-start(bf16[2,1,2,24,384]{4,3,2,1,0:T(8,128)(2,1)S(1)} %get-tuple-element.18), channel_id=1, source_target_pairs={{0,2},{1,3},{2,0},{3,1},{4,6},{5,7},{6,4},{7,5},{8,10},{9,11},{10,... | collective-permute-start | bytes 221192 | tf_op jit(solution)/shard_map/ppermute | solution.py:283
  34.1 4.4 %collective-permute-start.10 = (bf16[2,1,2,24,384]{4,3,2,1,0:T(8,128)(2,1)S(1)}, bf16[2,1,2,24,384]{4,3,2,1,0:T(8,128)(2,1)S(1)}, u32[]{:S(2)}, u32[]{:S(2)}) collective-permute-start(bf16[2,1,2,24,384]{4,3,2,1,0:T(8,128)(2,1)S(1)} %get-tuple-element.19), channel_id=1, source_target_pairs={{0,4},{1,5},{2,6},{3,7},{4,0},{5,1},{6,2},{7,3},{8,12},{9,13},{10,... | collective-permute-start | bytes 221192 | tf_op jit(solution)/shard_map/ppermute | solution.py:283
  35.3 3.9 %collective-permute-start.14 = (bf16[1,1,2,24,384]{4,3,2,1,0:T(8,128)(2,1)S(1)}, bf16[1,1,2,24,384]{4,3,2,1,0:T(8,128)(2,1)S(1)}, u32[]{:S(2)}, u32[]{:S(2)}) collective-permute-start(bf16[1,1,2,24,384]{4,3,2,1,0:T(8,128)(2,1)S(1)} %slice.94), channel_id=1, source_target_pairs={{0,1},{1,0},{2,3},{3,2},{4,5},{5,4},{6,7},{7,6},{8,9},{9,8},{10,11... | collective-permute-start | bytes 110600 | tf_op jit(solution)/shard_map/ppermute | solution.py:283
  36.4 2.7 %collective-permute-start.11 = (bf16[1,1,2,24,384]{4,3,2,1,0:T(8,128)(2,1)S(1)}, bf16[1,1,2,24,384]{4,3,2,1,0:T(8,128)(2,1)S(1)}, u32[]{:S(2)}, u32[]{:S(2)}) collective-permute-start(bf16[1,1,2,24,384]{4,3,2,1,0:T(8,128)(2,1)S(1)} %slice.105), channel_id=1, source_target_pairs={{0,1},{1,0},{2,3},{3,2},{4,5},{5,4},{6,7},{7,6},{8,9},{9,8},{10,11... | collective-permute-start | bytes 110600 | tf_op jit(solution)/shard_map/ppermute | solution.py:283
  37.9 1.2 %collective-permute-start.12 = (bf16[1,1,2,24,384]{4,3,2,1,0:T(8,128)(2,1)S(1)}, bf16[1,1,2,24,384]{4,3,2,1,0:T(8,128)(2,1)S(1)}, u32[]{:S(2)}, u32[]{:S(2)}) collective-permute-start(bf16[1,1,2,24,384]{4,3,2,1,0:T(8,128)(2,1)S(1)} %slice.106), channel_id=1, source_target_pairs={{0,1},{1,0},{2,3},{3,2},{4,5},{5,4},{6,7},{7,6},{8,9},{9,8},{10,11... | collective-permute-start | bytes 110600 | tf_op jit(solution)/shard_map/ppermute | solution.py:283
  38.4 1.2 %collective-permute-start.13 = (bf16[1,1,2,24,384]{4,3,2,1,0:T(8,128)(2,1)S(1)}, bf16[1,1,2,24,384]{4,3,2,1,0:T(8,128)(2,1)S(1)}, u32[]{:S(2)}, u32[]{:S(2)}) collective-permute-start(bf16[1,1,2,24,384]{4,3,2,1,0:T(8,128)(2,1)S(1)} %slice.107), channel_id=1, source_target_pairs={{0,1},{1,0},{2,3},{3,2},{4,5},{5,4},{6,7},{7,6},{8,9},{9,8},{10,11... | collective-permute-start | bytes 110600 | tf_op jit(solution)/shard_map/ppermute | solution.py:283

commit v9 on v7

--- a/solution.py
+++ b/solution.py
@@ -29,7 +29,7 @@
         return pltpu.make_async_copy(eigvecs.at[at], vec.at[at], arrived.at[at])
 
     for at in range(count):
-        load(at).start()
+        load(at).start(priority=0 if at == 0 else 1)
     device = lax.axis_index("sink")
     core = jnp.bitwise_and(device, 1)
     chip = jnp.bitwise_and(lax.shift_right_logical(device, 1), 1)

time: 43.5 us -> 43.5 us (level)
  no operation moved by 1% of the time
where the time goes in v9:
time: 43.5 us; the launch traced here: 43.3 us
  starting transfers between devices  18.3 us (42%)
  waiting for transfers between devices  11.7 us (27%)
  Pallas kernels  11.6 us (27%)
  local copies, waits for them, and re-layouts  1.01 us (2%)
  other arithmetic  0.53 us (1%)
    ppermute x15, starting transfers between devices, swap(): return lax.ppermute(value, 'sink', [(i, i ^ flip) for i in range(devices)])  18.3 us
    ppermute x15, waiting for transfers between devices, swap(): return lax.ppermute(value, 'sink', [(i, i ^ flip) for i in range(devices)])  11.7 us
    pallas_call x1, Pallas kernels, elementals(): pl.pallas_call(functools.partial(elemental_kernel, devices, chunks, arriv...  7.32 us
    pallas_call x1, Pallas kernels, pair_blocks(): pl.pallas_call(block_kernel, in_specs=[in_vmem] * 10, out_specs=pl.BlockS...  3.36 us
  transfers between devices with their start and end apart: 15, of which 8 were waited for; matrix products, arithmetic and copies ran while one was open for 2% of the time, Pallas kernels for 2%

profile of v9, /device:TPU:0, one launch (start us, length us, event | category | flops | bytes accessed | tf_op | source)
XLA Modules:
  0.0 43.3 jit_solution(9926001569992408386)
XLA Ops:
  0.0 0.7 %copy-done.2 = s32[3]{0:T(128)S(1)} copy-done((s32[3]{0:T(128)S(1)}, s32[3]{0:T(128)}, u32[]{:S(2)}) %copy-start.2) | copy-done | bytes 36
  0.7 7.3 %partial_elementals.1 = (f32[2,4,48,384]{3,2,1,0:T(8,128)S(1)}, bf16[2,4,48,384]{3,2,1,0:T(8,128)(2,1)S(1)}, f32[2,4,48,384]{3,2,1,0:T(8,128)S(1)}, bf16[2,4,48,384]{3,2,1,0:T(8,128)(2,1)S(1)}) custom-call(s32[1,3]{1,0:T(1,128)S(1)} %bitcast.43, bf16[8,2,3,192,512]{4,3,2,1,0:T(8,128)(2,1)} %eigvecs.1), custom_call_target="tpu_custom_call" | custom-call | flops 3623878656 | bytes 9437184 | tf_op jit(solution)/shard_map/partial_elementals/pallas_call | solution.py:95
  8.0 0.5 %collective-permute-start.3 = (bf16[2,4,48,384]{3,2,1,0:T(8,128)(2,1)S(1)}, bf16[2,4,48,384]{3,2,1,0:T(8,128)(2,1)S(1)}, u32[]{:S(2)}, u32[]{:S(2)}) collective-permute-start(bf16[2,4,48,384]{3,2,1,0:T(8,128)(2,1)S(1)} %get-tuple-element.16), channel_id=1, source_target_pairs={{0,1},{1,0},{2,3},{3,2},{4,5},{5,4},{6,7},{7,6},{8,9},{9,8},{10,11... | collective-permute-start | bytes 884744 | tf_op jit(solution)/shard_map/ppermute | solution.py:281
  8.7 1.0 %collective-permute-done.3 = bf16[2,4,48,384]{3,2,1,0:T(8,128)(2,1)S(1)} collective-permute-done((bf16[2,4,48,384]{3,2,1,0:T(8,128)(2,1)S(1)}, bf16[2,4,48,384]{3,2,1,0:T(8,128)(2,1)S(1)}, u32[]{:S(2)}, u32[]{:S(2)}) %collective-permute-start.3) | collective-permute-done | bytes 294944 | tf_op jit(solution)/shard_map/ppermute | solution.py:281
  9.8 2.9 %collective-permute-start.4 = (bf16[4,48,384]{2,1,0:T(8,128)(2,1)S(1)}, bf16[4,48,384]{2,1,0:T(8,128)(2,1)S(1)}, u32[]{:S(2)}, u32[]{:S(2)}) collective-permute-start(bf16[4,48,384]{2,1,0:T(8,128)(2,1)S(1)} %fusion.1), channel_id=1, source_target_pairs={{0,2},{1,3},{2,0},{3,1},{4,6},{5,7},{6,4},{7,5},{8,10},{9,11},{10,... | collective-permute-start | bytes 442376 | tf_op jit(solution)/shard_map/ppermute | solution.py:281
  13.0 0.3 collective-permute-start.1
  13.4 4.0 %collective-permute-done.4 = bf16[4,48,384]{2,1,0:T(8,128)(2,1)S(1)} collective-permute-done((bf16[4,48,384]{2,1,0:T(8,128)(2,1)S(1)}, bf16[4,48,384]{2,1,0:T(8,128)(2,1)S(1)}, u32[]{:S(2)}, u32[]{:S(2)}) %collective-permute-start.4) | collective-permute-done | bytes 147488 | tf_op jit(solution)/shard_map/ppermute | solution.py:281
  17.4 2.2 %collective-permute-start.5 = (bf16[4,24,384]{2,1,0:T(8,128)(2,1)S(1)}, bf16[4,24,384]{2,1,0:T(8,128)(2,1)S(1)}, u32[]{:S(2)}, u32[]{:S(2)}) collective-permute-start(bf16[4,24,384]{2,1,0:T(8,128)(2,1)S(1)} %fusion.4), channel_id=1, source_target_pairs={{0,4},{1,5},{2,6},{3,7},{4,0},{5,1},{6,2},{7,3},{8,12},{9,13},{10,... | collective-permute-start | bytes 221192 | tf_op jit(solution)/shard_map/ppermute | solution.py:281
  19.6 0.5 %collective-permute-done.1 = bf16[200,384]{1,0:T(8,128)(2,1)S(1)} collective-permute-done((bf16[200,384]{1,0:T(8,128)(2,1)S(1)}, bf16[200,384]{1,0:T(8,128)(2,1)S(1)}, u32[]{:S(2)}, u32[]{:S(2)}) %collective-permute-start.1) | collective-permute-done | bytes 153632 | tf_op jit(solution)/shard_map/ppermute | solution.py:281
  20.4 1.9 %collective-permute-start.2 = (bf16[104,384]{1,0:T(8,128)(2,1)S(1)}, bf16[104,384]{1,0:T(8,128)(2,1)S(1)}, u32[]{:S(2)}, u32[]{:S(2)}) collective-permute-start(bf16[104,384]{1,0:T(8,128)(2,1)S(1)} %pad_maximum_fusion.2), channel_id=1, source_target_pairs={{0,4},{1,5},{2,6},{3,7},{4,0},{5,1},{6,2},{7,3},{8,12},{9,13},{10,... | collective-permute-start | bytes 239624 | tf_op jit(solution)/shard_map/ppermute | solution.py:281
  22.4 2.7 %collective-permute-start.6 = (bf16[4,24,384]{2,1,0:T(8,128)(2,1)S(1)}, bf16[4,24,384]{2,1,0:T(8,128)(2,1)S(1)}, u32[]{:S(2)}, u32[]{:S(2)}) collective-permute-start(bf16[4,24,384]{2,1,0:T(8,128)(2,1)S(1)} %fusion.2), channel_id=1, source_target_pairs={{0,8},{1,9},{2,10},{3,11},{4,12},{5,13},{6,14},{7,15},{8,0},{9,1},... | collective-permute-start | bytes 221192 | tf_op jit(solution)/shard_map/ppermute | solution.py:281
  25.2 2.7 %collective-permute-start.7 = (bf16[4,24,384]{2,1,0:T(8,128)(2,1)S(1)}, bf16[4,24,384]{2,1,0:T(8,128)(2,1)S(1)}, u32[]{:S(2)}, u32[]{:S(2)}) collective-permute-start(bf16[4,24,384]{2,1,0:T(8,128)(2,1)S(1)} %fusion.3), channel_id=1, source_target_pairs={{0,8},{1,9},{2,10},{3,11},{4,12},{5,13},{6,14},{7,15},{8,0},{9,1},... | collective-permute-start | bytes 221192 | tf_op jit(solution)/shard_map/ppermute | solution.py:281
  27.9 0.1 collective-permute-done.6
  28.1 2.8 %collective-permute-done.7 = bf16[4,24,384]{2,1,0:T(8,128)(2,1)S(1)} collective-permute-done((bf16[4,24,384]{2,1,0:T(8,128)(2,1)S(1)}, bf16[4,24,384]{2,1,0:T(8,128)(2,1)S(1)}, u32[]{:S(2)}, u32[]{:S(2)}) %collective-permute-start.7) | collective-permute-done | bytes 73760 | tf_op jit(solution)/shard_map/ppermute | solution.py:281
  31.0 2.5 %collective-permute-start.8 = (bf16[2,1,2,24,384]{4,3,2,1,0:T(8,128)(2,1)S(1)}, bf16[2,1,2,24,384]{4,3,2,1,0:T(8,128)(2,1)S(1)}, u32[]{:S(2)}, u32[]{:S(2)}) collective-permute-start(bf16[2,1,2,24,384]{4,3,2,1,0:T(8,128)(2,1)S(1)} %get-tuple-element.17), channel_id=1, source_target_pairs={{0,6},{1,7},{2,4},{3,5},{4,2},{5,3},{6,0},{7,1},{8,14},{9,15},{10,... | collective-permute-start | bytes 221192 | tf_op jit(solution)/shard_map/ppermute | solution.py:281
  33.6 0.5 %collective-permute-start.9 = (bf16[2,1,2,24,384]{4,3,2,1,0:T(8,128)(2,1)S(1)}, bf16[2,1,2,24,384]{4,3,2,1,0:T(8,128)(2,1)S(1)}, u32[]{:S(2)}, u32[]{:S(2)}) collective-permute-start(bf16[2,1,2,24,384]{4,3,2,1,0:T(8,128)(2,1)S(1)} %get-tuple-element.18), channel_id=1, source_target_pairs={{0,2},{1,3},{2,0},{3,1},{4,6},{5,7},{6,4},{7,5},{8,10},{9,11},{10,... | collective-permute-start | bytes 221192 | tf_op jit(solution)/shard_map/ppermute | solution.py:281
  34.1 1.2 %collective-permute-start.10 = (bf16[2,1,2,24,384]{4,3,2,1,0:T(8,128)(2,1)S(1)}, bf16[2,1,2,24,384]{4,3,2,1,0:T(8,128)(2,1)S(1)}, u32[]{:S(2)}, u32[]{:S(2)}) collective-permute-start(bf16[2,1,2,24,384]{4,3,2,1,0:T(8,128)(2,1)S(1)} %get-tuple-element.19), channel_id=1, source_target_pairs={{0,4},{1,5},{2,6},{3,7},{4,0},{5,1},{6,2},{7,3},{8,12},{9,13},{10,... | collective-permute-start | bytes 221192 | tf_op jit(solution)/shard_map/ppermute | solution.py:281
  35.3 1.2 %collective-permute-done.8.by_both.refs_0_ = bf16[2,1,2,24,384]{4,3,2,1,0:T(8,128)(2,1)S(1)} collective-permute-done((bf16[2,1,2,24,384]{4,3,2,1,0:T(8,128)(2,1)S(1)}, bf16[2,1,2,24,384]{4,3,2,1,0:T(8,128)(2,1)S(1)}, u32[]{:S(2)}, u32[]{:S(2)}) %collective-permute-start.8) | collective-permute-done | bytes 73760 | tf_op jit(solution)/shard_map/ppermute | solution.py:281
  36.5 1.5 %collective-permute-done.9.by_x.refs_1_ = bf16[2,1,2,24,384]{4,3,2,1,0:T(8,128)(2,1)S(1)} collective-permute-done((bf16[2,1,2,24,384]{4,3,2,1,0:T(8,128)(2,1)S(1)}, bf16[2,1,2,24,384]{4,3,2,1,0:T(8,128)(2,1)S(1)}, u32[]{:S(2)}, u32[]{:S(2)}) %collective-permute-start.9) | collective-permute-done | bytes 73760 | tf_op jit(solution)/shard_map/ppermute | solution.py:281
  37.9 0.5 %collective-permute-start.14 = (bf16[1,1,2,24,384]{4,3,2,1,0:T(8,128)(2,1)S(1)}, bf16[1,1,2,24,384]{4,3,2,1,0:T(8,128)(2,1)S(1)}, u32[]{:S(2)}, u32[]{:S(2)}) collective-permute-start(bf16[1,1,2,24,384]{4,3,2,1,0:T(8,128)(2,1)S(1)} %slice.94), channel_id=1, source_target_pairs={{0,1},{1,0},{2,3},{3,2},{4,5},{5,4},{6,7},{7,6},{8,9},{9,8},{10,11... | collective-permute-start | bytes 110600 | tf_op jit(solution)/shard_map/ppermute | solution.py:281
  38.5 0.1 collective-permute-start.13
  38.6 0.5 %collective-permute-done.12.by_x_core.refs_4_ = bf16[1,1,2,24,384]{4,3,2,1,0:T(8,128)(2,1)S(1)} collective-permute-done((bf16[1,1,2,24,384]{4,3,2,1,0:T(8,128)(2,1)S(1)}, bf16[1,1,2,24,384]{4,3,2,1,0:T(8,128)(2,1)S(1)}, u32[]{:S(2)}, u32[]{:S(2)}) %collective-permute-start.12) | collective-permute-done | bytes 36896 | tf_op jit(solution)/shard_map/ppermute | solution.py:281
  39.1 0.8 %left_across.1.refs_8_ = bf16[1,2,4,96,768]{4,3,2,1,0:T(8,128)(2,1)S(1)} custom-call(bf16[2,1,2,24,384]{4,3,2,1,0:T(8,128)(2,1)S(1)} %collective-permute-done.8.by_both.refs_0_, bf16[2,1,2,24,384]{4,3,2,1,0:T(8,128)(2,1)S(1)} %collective-permute-done.9.by_x.refs_1_, bf16[1,1,2,24,384]{4,3,2,1,0:T(8,128)(2,1)S(1)} %collective-permute-done.11.by_both_core.refs_3_, ...), custom_call_target="tpu_custom_call" | custom-call | flops 905969664 | bytes 2359296 | tf_op jit(solution)/shard_map/left_across/pallas_call | solution.py:250
  40.0 3.4 %meson_blocks.1 = bf16[1,2,768,768]{3,2,1,0:T(8,128)(2,1)} custom-call(bf16[2,1,2,24,384]{4,3,2,1,0:T(8,128)(2,1)S(1)} %collective-permute-done.8.by_both.refs_0_, bf16[2,1,2,24,384]{4,3,2,1,0:T(8,128)(2,1)S(1)} %collective-permute-done.9.by_x.refs_1_, bf16[2,1,2,24,384]{4,3,2,1,0:T(8,128)(2,1)S(1)} %collective-permute-done.10.refs_2_, ...), custom_call_target="tpu_custom_call" | custom-call | flops 905969664 | bytes 2359296 | tf_op jit(solution)/shard_map/meson_blocks/pallas_call | solution.py:260
  (51 shorter events, 1.2 us)
Async XLA Ops:
  0.0 0.7 %copy-start.2 = (s32[3]{0:T(128)S(1)}, s32[3]{0:T(128)}, u32[]{:S(2)}) copy-start(s32[3]{0:T(128)} %param.5) | copy-start | bytes 40
  0.7 7.9 %copy-start.1 = (s32[1,2]{1,0:T(1,128)S(1)}, s32[1,2]{1,0:T(1,128)}, u32[]{:S(2)}) copy-start(s32[1,2]{1,0:T(1,128)} %refs_0_.1) | copy-start | bytes 28
  8.0 1.7 %collective-permute-start.3 = (bf16[2,4,48,384]{3,2,1,0:T(8,128)(2,1)S(1)}, bf16[2,4,48,384]{3,2,1,0:T(8,128)(2,1)S(1)}, u32[]{:S(2)}, u32[]{:S(2)}) collective-permute-start(bf16[2,4,48,384]{3,2,1,0:T(8,128)(2,1)S(1)} %get-tuple-element.16), channel_id=1, source_target_pairs={{0,1},{1,0},{2,3},{3,2},{4,5},{5,4},{6,7},{7,6},{8,9},{9,8},{10,11... | collective-permute-start | bytes 884744 | tf_op jit(solution)/shard_map/ppermute | solution.py:281
  8.6 4.2 %collective-permute-start = (bf16[392,384]{1,0:T(8,128)(2,1)S(1)}, bf16[392,384]{1,0:T(8,128)(2,1)S(1)}, u32[]{:S(2)}, u32[]{:S(2)}) collective-permute-start(bf16[392,384]{1,0:T(8,128)(2,1)S(1)} %pad_maximum_fusion), channel_id=1, source_target_pairs={{0,1},{1,0},{2,3},{3,2},{4,5},{5,4},{6,7},{7,6},{8,9},{9,8},{10,11... | collective-permute-start | bytes 903176 | tf_op jit(solution)/shard_map/ppermute | solution.py:281
  9.8 7.5 %collective-permute-start.4 = (bf16[4,48,384]{2,1,0:T(8,128)(2,1)S(1)}, bf16[4,48,384]{2,1,0:T(8,128)(2,1)S(1)}, u32[]{:S(2)}, u32[]{:S(2)}) collective-permute-start(bf16[4,48,384]{2,1,0:T(8,128)(2,1)S(1)} %fusion.1), channel_id=1, source_target_pairs={{0,2},{1,3},{2,0},{3,1},{4,6},{5,7},{6,4},{7,5},{8,10},{9,11},{10,... | collective-permute-start | bytes 442376 | tf_op jit(solution)/shard_map/ppermute | solution.py:281
  13.0 26.2 %copy-start = (bf16[1,2,768,768]{3,2,1,0:T(8,128)(2,1)S(1)}, bf16[1,2,768,768]{3,2,1,0:T(8,128)(2,1)}, u32[]{:S(2)}) copy-start(bf16[1,2,768,768]{3,2,1,0:T(8,128)(2,1)} %refs_9_.1) | copy-start | bytes 7077892
  13.0 7.1 %collective-permute-start.1 = (bf16[200,384]{1,0:T(8,128)(2,1)S(1)}, bf16[200,384]{1,0:T(8,128)(2,1)S(1)}, u32[]{:S(2)}, u32[]{:S(2)}) collective-permute-start(bf16[200,384]{1,0:T(8,128)(2,1)S(1)} %pad_maximum_fusion.1), channel_id=1, source_target_pairs={{0,2},{1,3},{2,0},{3,1},{4,6},{5,7},{6,4},{7,5},{8,10},{9,11},{10,... | collective-permute-start | bytes 460808 | tf_op jit(solution)/shard_map/ppermute | solution.py:281
  17.4 4.9 %collective-permute-start.5 = (bf16[4,24,384]{2,1,0:T(8,128)(2,1)S(1)}, bf16[4,24,384]{2,1,0:T(8,128)(2,1)S(1)}, u32[]{:S(2)}, u32[]{:S(2)}) collective-permute-start(bf16[4,24,384]{2,1,0:T(8,128)(2,1)S(1)} %fusion.4), channel_id=1, source_target_pairs={{0,4},{1,5},{2,6},{3,7},{4,0},{5,1},{6,2},{7,3},{8,12},{9,13},{10,... | collective-permute-start | bytes 221192 | tf_op jit(solution)/shard_map/ppermute | solution.py:281
  20.4 4.6 %collective-permute-start.2 = (bf16[104,384]{1,0:T(8,128)(2,1)S(1)}, bf16[104,384]{1,0:T(8,128)(2,1)S(1)}, u32[]{:S(2)}, u32[]{:S(2)}) collective-permute-start(bf16[104,384]{1,0:T(8,128)(2,1)S(1)} %pad_maximum_fusion.2), channel_id=1, source_target_pairs={{0,4},{1,5},{2,6},{3,7},{4,0},{5,1},{6,2},{7,3},{8,12},{9,13},{10,... | collective-permute-start | bytes 239624 | tf_op jit(solution)/shard_map/ppermute | solution.py:281
  22.4 5.7 %collective-permute-start.6 = (bf16[4,24,384]{2,1,0:T(8,128)(2,1)S(1)}, bf16[4,24,384]{2,1,0:T(8,128)(2,1)S(1)}, u32[]{:S(2)}, u32[]{:S(2)}) collective-permute-start(bf16[4,24,384]{2,1,0:T(8,128)(2,1)S(1)} %fusion.2), channel_id=1, source_target_pairs={{0,8},{1,9},{2,10},{3,11},{4,12},{5,13},{6,14},{7,15},{8,0},{9,1},... | collective-permute-start | bytes 221192 | tf_op jit(solution)/shard_map/ppermute | solution.py:281
  25.2 5.6 %collective-permute-start.7 = (bf16[4,24,384]{2,1,0:T(8,128)(2,1)S(1)}, bf16[4,24,384]{2,1,0:T(8,128)(2,1)S(1)}, u32[]{:S(2)}, u32[]{:S(2)}) collective-permute-start(bf16[4,24,384]{2,1,0:T(8,128)(2,1)S(1)} %fusion.3), channel_id=1, source_target_pairs={{0,8},{1,9},{2,10},{3,11},{4,12},{5,13},{6,14},{7,15},{8,0},{9,1},... | collective-permute-start | bytes 221192 | tf_op jit(solution)/shard_map/ppermute | solution.py:281
  31.0 5.4 %collective-permute-start.8 = (bf16[2,1,2,24,384]{4,3,2,1,0:T(8,128)(2,1)S(1)}, bf16[2,1,2,24,384]{4,3,2,1,0:T(8,128)(2,1)S(1)}, u32[]{:S(2)}, u32[]{:S(2)}) collective-permute-start(bf16[2,1,2,24,384]{4,3,2,1,0:T(8,128)(2,1)S(1)} %get-tuple-element.17), channel_id=1, source_target_pairs={{0,6},{1,7},{2,4},{3,5},{4,2},{5,3},{6,0},{7,1},{8,14},{9,15},{10,... | collective-permute-start | bytes 221192 | tf_op jit(solution)/shard_map/ppermute | solution.py:281
  33.6 4.4 %collective-permute-start.9 = (bf16[2,1,2,24,384]{4,3,2,1,0:T(8,128)(2,1)S(1)}, bf16[2,1,2,24,384]{4,3,2,1,0:T(8,128)(2,1)S(1)}, u32[]{:S(2)}, u32[]{:S(2)}) collective-permute-start(bf16[2,1,2,24,384]{4,3,2,1,0:T(8,128)(2,1)S(1)} %get-tuple-element.18), channel_id=1, source_target_pairs={{0,2},{1,3},{2,0},{3,1},{4,6},{5,7},{6,4},{7,5},{8,10},{9,11},{10,... | collective-permute-start | bytes 221192 | tf_op jit(solution)/shard_map/ppermute | solution.py:281
  34.1 4.4 %collective-permute-start.10 = (bf16[2,1,2,24,384]{4,3,2,1,0:T(8,128)(2,1)S(1)}, bf16[2,1,2,24,384]{4,3,2,1,0:T(8,128)(2,1)S(1)}, u32[]{:S(2)}, u32[]{:S(2)}) collective-permute-start(bf16[2,1,2,24,384]{4,3,2,1,0:T(8,128)(2,1)S(1)} %get-tuple-element.19), channel_id=1, source_target_pairs={{0,4},{1,5},{2,6},{3,7},{4,0},{5,1},{6,2},{7,3},{8,12},{9,13},{10,... | collective-permute-start | bytes 221192 | tf_op jit(solution)/shard_map/ppermute | solution.py:281
  36.4 2.2 %collective-permute-start.11 = (bf16[1,1,2,24,384]{4,3,2,1,0:T(8,128)(2,1)S(1)}, bf16[1,1,2,24,384]{4,3,2,1,0:T(8,128)(2,1)S(1)}, u32[]{:S(2)}, u32[]{:S(2)}) collective-permute-start(bf16[1,1,2,24,384]{4,3,2,1,0:T(8,128)(2,1)S(1)} %slice.105), channel_id=1, source_target_pairs={{0,1},{1,0},{2,3},{3,2},{4,5},{5,4},{6,7},{7,6},{8,9},{9,8},{10,11... | collective-permute-start | bytes 110600 | tf_op jit(solution)/shard_map/ppermute | solution.py:281
  37.9 1.2 %collective-permute-start.12 = (bf16[1,1,2,24,384]{4,3,2,1,0:T(8,128)(2,1)S(1)}, bf16[1,1,2,24,384]{4,3,2,1,0:T(8,128)(2,1)S(1)}, u32[]{:S(2)}, u32[]{:S(2)}) collective-permute-start(bf16[1,1,2,24,384]{4,3,2,1,0:T(8,128)(2,1)S(1)} %slice.106), channel_id=1, source_target_pairs={{0,1},{1,0},{2,3},{3,2},{4,5},{5,4},{6,7},{7,6},{8,9},{9,8},{10,11... | collective-permute-start | bytes 110600 | tf_op jit(solution)/shard_map/ppermute | solution.py:281
  37.9 2.0 %collective-permute-start.14 = (bf16[1,1,2,24,384]{4,3,2,1,0:T(8,128)(2,1)S(1)}, bf16[1,1,2,24,384]{4,3,2,1,0:T(8,128)(2,1)S(1)}, u32[]{:S(2)}, u32[]{:S(2)}) collective-permute-start(bf16[1,1,2,24,384]{4,3,2,1,0:T(8,128)(2,1)S(1)} %slice.94), channel_id=1, source_target_pairs={{0,1},{1,0},{2,3},{3,2},{4,5},{5,4},{6,7},{7,6},{8,9},{9,8},{10,11... | collective-permute-start | bytes 110600 | tf_op jit(solution)/shard_map/ppermute | solution.py:281
  38.5 1.5 %collective-permute-start.13 = (bf16[1,1,2,24,384]{4,3,2,1,0:T(8,128)(2,1)S(1)}, bf16[1,1,2,24,384]{4,3,2,1,0:T(8,128)(2,1)S(1)}, u32[]{:S(2)}, u32[]{:S(2)}) collective-permute-start(bf16[1,1,2,24,384]{4,3,2,1,0:T(8,128)(2,1)S(1)} %slice.107), channel_id=1, source_target_pairs={{0,1},{1,0},{2,3},{3,2},{4,5},{5,4},{6,7},{7,6},{8,9},{9,8},{10,11... | collective-permute-start | bytes 110600 | tf_op jit(solution)/shard_map/ppermute | solution.py:281
